TPU v7x, 128 devices: a whole 4x4x4 slice. The times are simulated.
128 devices in a mesh: gx: 16 (over y, x), gy: 8 (over z, core).
Axes of the slice: x: 4, y: 4, z: 4, core: 2. Of those that a mesh axis runs over, the one named last changes fastest.
Arguments:
- right_side: float32 [256, 128, 512], P('gx', 'gy'), may hold values from -12 to 12
- coefficient: float32 [256, 128, 512], P('gx', 'gy'), may hold values from 0.25 to 4
Outputs:
- solution: float32 [256, 128, 512], P('gx', 'gy')
- residual: float32 [256, 128, 512], P('gx', 'gy')
All inputs are finite; a program needn't handle non-finite values.
Results may differ from a plain program's by a relative error of at most 0.0003.
Values sent between devices are 32-bit elements; how exact they have to be, the bound alone decides.
No kernel may reach another device: no remote copies, remote signals or barrier semaphores. Data moves between devices by JAX's collectives and lax.ppermute only.
A program may use at most 128 MiB of HBM per device.

v0:
```python
import jax
import jax.numpy as jnp
from jax import lax
from jax.sharding import PartitionSpec as P

LEVELS = 5
AGG = 3
NU = 2
BOTTOM = 16


OMEGA = 0.8


def padded_2(cells, sides, width):
    for axis, dim in sides:
        count = lax.axis_size(axis)
        ends = count - 1
        head = lax.slice_in_dim(cells, 0, width, axis=dim)
        tail = lax.slice_in_dim(cells, cells.shape[dim] - width, cells.shape[dim], axis=dim)
        cells = jnp.concatenate(
            [
                lax.ppermute(tail, axis, [(i, (i + 1) % count) for i in range(ends)]),
                cells,
                lax.ppermute(head, axis, [((i + 1) % count, i) for i in range(ends)]),
            ],
            axis=dim,
        )
    return cells


def face_weights(padded):
    centre = padded[1:-1, 1:-1, 1:-1]
    return (
        0.5 * (centre + padded[:-2, 1:-1, 1:-1]),
        0.5 * (centre + padded[2:, 1:-1, 1:-1]),
        0.5 * (centre + padded[1:-1, :-2, 1:-1]),
        0.5 * (centre + padded[1:-1, 2:, 1:-1]),
        0.5 * (centre + padded[1:-1, 1:-1, :-2]),
        0.5 * (centre + padded[1:-1, 1:-1, 2:]),
    )


def stencil(padded, weights, inv_h2):
    centre = padded[1:-1, 1:-1, 1:-1]
    summed = weights[0] * (centre - padded[:-2, 1:-1, 1:-1]) + weights[1] * (
        centre - padded[2:, 1:-1, 1:-1]
    )
    summed = (
        summed
        + weights[2] * (centre - padded[1:-1, :-2, 1:-1])
        + weights[3] * (centre - padded[1:-1, 2:, 1:-1])
    )
    summed = (
        summed
        + weights[4] * (centre - padded[1:-1, 1:-1, :-2])
        + weights[5] * (centre - padded[1:-1, 1:-1, 2:])
    )
    return summed * inv_h2


def diagonal_of(weights, inv_h2):
    return (weights[0] + weights[1] + weights[2] + weights[3] + weights[4] + weights[5]) * inv_h2


def coarsen(array_in):
    extent_x, extent_y, extent_z = array_in.shape
    return array_in.reshape(extent_x // 2, 2, extent_y // 2, 2, extent_z // 2, 2).mean(
        axis=(1, 3, 5)
    )


def refine(array_in):
    extent_x, extent_y, extent_z = array_in.shape
    spread = jnp.broadcast_to(
        array_in[:, None, :, None, :, None], (extent_x, 2, extent_y, 2, extent_z, 2)
    )
    return spread.reshape(2 * extent_x, 2 * extent_y, 2 * extent_z)


def pad_depth(array_in):
    return jnp.pad(array_in, ((0, 0), (0, 0), (1, 1)))


def make_set(padded_coef, level_index):
    inv_h2 = 1.0 / 4.0**level_index
    weights = face_weights(padded_coef)
    return (weights, inv_h2, diagonal_of(weights, inv_h2))


def box_apply(iterate, stencil_set):
    padded = padded_2(iterate, (("gx", 0), ("gy", 1)), 1)
    return stencil(pad_depth(padded), stencil_set[0], stencil_set[1])


def box_setup(coef_level, level_index):
    padded = padded_2(coef_level, (("gx", 0), ("gy", 1)), 1)
    return make_set(pad_depth(padded), level_index)


def slab_setup(coef_level, level_index):
    padded = padded_2(coef_level, (("gx", 0),), 1)
    return make_set(jnp.pad(padded, ((0, 0), (1, 1), (1, 1))), level_index)


def bottom_apply(iterate, stencil_set):
    padded = padded_2(iterate, (("gx", 0),), 1)
    return stencil(jnp.pad(padded, ((0, 0), (1, 1), (1, 1))), stencil_set[0], stencil_set[1])


def smooth(iterate, source, stencil_set, apply_fn, count):
    for repeat in range(count):
        iterate = iterate + OMEGA * (source - apply_fn(iterate, stencil_set)) / stencil_set[2]
    return iterate


def presmooth(source, stencil_set, apply_fn):
    iterate = OMEGA * source / stencil_set[2]
    return smooth(iterate, source, stencil_set, apply_fn, NU - 1)


def shards(right_side, coefficient):
    place_y = lax.axis_index("gy")
    coef_levels = [coefficient]
    for level_index in range(1, LEVELS):
        coef_levels.append(coarsen(coef_levels[-1]))
    saved_levels = []
    source = right_side
    for level_index in range(AGG):
        plain_set = box_setup(coef_levels[level_index], level_index)
        iterate = presmooth(source, plain_set, box_apply)
        leftover = source - box_apply(iterate, plain_set)
        saved_levels.append((plain_set, source, iterate, plain_set))
        source = coarsen(leftover)
    mid_set = box_setup(coef_levels[AGG], AGG)
    iterate = presmooth(source, mid_set, box_apply)
    leftover = source - box_apply(iterate, mid_set)
    coarse_source = coarsen(leftover)
    source_all, coef_all = (
        lax.all_gather(coarse_source, "gy", axis=1, tiled=True),
        lax.all_gather(coef_levels[AGG + 1], "gy", axis=1, tiled=True),
    )
    slab_set = slab_setup(coef_all, LEVELS - 1)

    def slab_turn(repeat, iterate):
        return iterate + OMEGA * (source_all - bottom_apply(iterate, slab_set)) / slab_set[2]

    correction_all = lax.fori_loop(0, BOTTOM, slab_turn, jnp.zeros_like(source_all))
    extent_y = coarse_source.shape[1]
    correction = lax.dynamic_slice_in_dim(correction_all, place_y * extent_y, extent_y, 1)
    correction = smooth(iterate + refine(correction), source, mid_set, box_apply, NU)
    for level_index in reversed(range(AGG)):
        level_set, level_source, iterate, plain_set = saved_levels[level_index]
        iterate = iterate + refine(correction)
        iterate = smooth(iterate, level_source, level_set, box_apply, NU)
        correction = iterate
    residual = right_side - box_apply(correction, saved_levels[0][3])
    return (correction, residual)


def solution(mesh):
    in_specs = (P("gx", "gy", None), P("gx", "gy", None))
    out_specs = (P("gx", "gy", None), P("gx", "gy", None))
    return jax.shard_map(shards, mesh=mesh, in_specs=in_specs, out_specs=out_specs, check_vma=False)
```

profile of v0, /device:TPU:1, one launch (start us, length us, event | category | flops | bytes accessed | tf_op | source)
XLA Modules:
  0.0 789.0 jit_solution(6342941447859596731)
XLA Ops:
  1.4 3.9 collective-permute-start.2
  6.7 35.6 %reshape.69 = f32[8,2,8,2,256,2]{5,4,3,2,1,0:T(8,128)} reshape(f32[16,16,512]{2,1,0:T(8,128)} %param.5) | data formatting | bytes 1048576 | tf_op jit(solution)/shard_map/reshape | solution.py:68
  42.3 12.3 %reduce_sum.87 = f32[8,8,256]{2,1,0:T(8,128)S(1)} reduce(f32[8,2,8,2,256,2]{5,4,3,2,1,0:T(8,128)} %reshape.69, f32[]{:T(128)} %constant.63.clone.1), dimensions={1,3,5}, to_apply=%region_1.0 | reduce | flops 114688 | bytes 589828 | tf_op jit(solution)/shard_map/reduce_sum | solution.py:68
  54.7 4.5 collective-permute-start.4
  66.6 4.3 collective-permute-start.6
  72.1 4.0 collective-permute-start.14
  77.4 5.6 div.92
  97.2 4.3 collective-permute-start.10
  118.2 35.6 %reshape.68 = f32[8,2,8,2,256,2]{5,4,3,2,1,0:T(8,128)} reshape(f32[16,16,512]{2,1,0:T(8,128)} %fusion.73) | data formatting | bytes 1048576 | tf_op jit(solution)/shard_map/reshape | solution.py:68
  153.8 12.2 %reduce_sum.86 = f32[8,8,256]{2,1,0:T(8,128)S(1)} reduce(f32[8,2,8,2,256,2]{5,4,3,2,1,0:T(8,128)} %reshape.68, f32[]{:T(128)} %constant.63.clone.1), dimensions={1,3,5}, to_apply=%region_0.0 | reduce | flops 114688 | bytes 589828 | tf_op jit(solution)/shard_map/reduce_sum | solution.py:68
  167.8 5.4 collective-permute-start.18
  175.1 6.4 collective-permute-start.26
  196.2 5.8 collective-permute-start.22
  218.0 6.3 reshape.70
  227.8 6.1 collective-permute-start.30
  235.8 6.4 collective-permute-start.38
  252.0 6.4 collective-permute-start.34
  279.8 5.7 collective-permute-start.42
  286.9 5.4 collective-permute-done.43
  302.6 6.3 collective-permute-start.48
  331.0 12.2 %all-reduce.25 = (f32[256]{0:T(256)}, f32[256]{0:T(256)}) all-reduce(f32[256]{0:T(256)} %copy-done.38, f32[256]{0:T(256)} %multiply_dynamic-update-slice_fusion), channel_id=2, replica_groups=mesh['gx'=16,'gy'=8] {'gy'}, use_global_device_ids=true, to_apply=%add.23 | all-reduce | flops 512 | bytes 4096
  344.5 6.3 collective-permute-start.46
  358.1 187.5 %while.13 = (s32[]{:T(128)}, f32[1,8,32]{2,1,0:T(8,128)}, f32[1,8,32]{2,1,0:T(8,128)}, f32[1,8,32]{2,1,0:T(8,128)}, f32[1,8,32]{2,1,0:T(8,128)}, /*index=5*/f32[...) while((s32[]{:T(128)}, f32[1,8,32]{2,1,0:T(8,128)}, ...), condition=%wide.region_11.12_spmd.clone, body=%wide.region_10.11_spmd.clone.sunk | while | flops 21447 | bytes 33984 | solution.py:148
  360.0 4.3 collective-permute-start.1
  370.0 4.4 collective-permute-start.1
  380.0 6.1 collective-permute-start.1
  391.8 6.1 collective-permute-start.1
  403.6 6.3 collective-permute-start.1
  415.6 6.3 collective-permute-start.1
  427.6 6.3 collective-permute-start.1
  439.7 6.3 collective-permute-start.1
  451.7 6.3 collective-permute-start.1
  463.7 6.3 collective-permute-start.1
  475.8 6.3 collective-permute-start.1
  487.8 6.3 collective-permute-start.1
  499.8 6.6 collective-permute-start.1
  512.1 6.3 collective-permute-start.1
  524.2 6.3 collective-permute-start.1
  536.2 6.3 collective-permute-start.1
  549.1 5.7 collective-permute-start.52
  556.2 5.4 collective-permute-done.53
  561.5 23.0 %collective-permute-start.54 = (f32[4,1,64]{2,1,0:T(1,128)S(1)}, f32[4,1,64]{2,1,0:T(1,128)S(1)}, u32[]{:S(2)}, u32[]{:S(2)}) collective-permute-start(f32[4,1,64]{2,1,0:T(1,128)S(1)} %get-tuple-element.274), channel_id=1, source_target_pairs={{0,1},{1,2},{2,3},{3,4},{4,5},{5,6},{6,7},{8,9},{9,10},{10,11},{11... | collective-permute-start | bytes 3080 | tf_op jit(solution)/shard_map/ppermute | solution.py:23
  590.4 6.0 collective-permute-start.56
  597.8 5.7 collective-permute-done.57
  615.9 5.7 collective-permute-start.60
  655.3 4.6 reshape.73
  695.3 11.3 %broadcast_in_dim.40 = f32[8,2,8,2,256,2]{5,4,3,2,1,0:T(8,128)} broadcast(f32[8,8,256]{2,1,0:T(8,128)S(1)} %fusion.124), dimensions={0,2,4} | broadcast | bytes 589824 | tf_op jit(solution)/shard_map/broadcast_in_dim | solution.py:75
  706.7 24.5 %reshape.74 = f32[16,16,512]{2,1,0:T(8,128)} reshape(f32[8,2,8,2,256,2]{5,4,3,2,1,0:T(8,128)} %broadcast_in_dim.40) | data formatting | bytes 1048576 | tf_op jit(solution)/shard_map/reshape | solution.py:78
  (450 shorter events, 395.4 us)
Async XLA Ops:
  1.4 53.1 %collective-permute-start.2 = (f32[1,16,512]{2,1,0:T(8,128)S(1)}, f32[1,16,512]{2,1,0:T(8,128)S(1)}, u32[]{:S(2)}, u32[]{:S(2)}) collective-permute-start(f32[1,16,512]{2,1,0:T(8,128)S(1)} %get-tuple-element.231), channel_id=1, source_target_pairs={{0,8},{8,16},{16,24},{24,32},{32,40},{40,48},{48,56},{56,64},{64,7... | collective-permute-start | bytes 98312 | tf_op jit(solution)/shard_map/ppermute | solution.py:23
  5.4 49.3 %collective-permute-start.3 = (f32[1,16,512]{2,1,0:T(8,128)S(1)}, f32[1,16,512]{2,1,0:T(8,128)S(1)}, u32[]{:S(2)}, u32[]{:S(2)}) collective-permute-start(f32[1,16,512]{2,1,0:T(8,128)S(1)} %get-tuple-element.230), channel_id=1, source_target_pairs={{8,0},{16,8},{24,16},{32,24},{40,32},{48,40},{56,48},{64,56},{72,6... | collective-permute-start | bytes 98312 | tf_op jit(solution)/shard_map/ppermute | solution.py:25
  66.6 19.0 %collective-permute-start.6 = (f32[1,16,512]{2,1,0:T(8,128)S(1)}, f32[1,16,512]{2,1,0:T(8,128)S(1)}, u32[]{:S(2)}, u32[]{:S(2)}) collective-permute-start(f32[1,16,512]{2,1,0:T(8,128)S(1)} %get-tuple-element.228), channel_id=1, source_target_pairs={{0,8},{8,16},{16,24},{24,32},{32,40},{40,48},{48,56},{56,64},{64,7... | collective-permute-start | bytes 98312 | tf_op jit(solution)/shard_map/ppermute | solution.py:23
  70.8 14.7 %collective-permute-start.7 = (f32[1,16,512]{2,1,0:T(8,128)S(1)}, f32[1,16,512]{2,1,0:T(8,128)S(1)}, u32[]{:S(2)}, u32[]{:S(2)}) collective-permute-start(f32[1,16,512]{2,1,0:T(8,128)S(1)} %get-tuple-element.229), channel_id=1, source_target_pairs={{8,0},{16,8},{24,16},{32,24},{40,32},{48,40},{56,48},{64,56},{72,6... | collective-permute-start | bytes 98312 | tf_op jit(solution)/shard_map/ppermute | solution.py:25
  72.1 30.7 %collective-permute-start.14 = (f32[1,8,256]{2,1,0:T(8,128)S(1)}, f32[1,8,256]{2,1,0:T(8,128)S(1)}, u32[]{:S(2)}, u32[]{:S(2)}) collective-permute-start(f32[1,8,256]{2,1,0:T(8,128)S(1)} %get-tuple-element.251), channel_id=1, source_target_pairs={{0,8},{8,16},{16,24},{24,32},{32,40},{40,48},{48,56},{56,64},{64,7... | collective-permute-start | bytes 24584 | tf_op jit(solution)/shard_map/ppermute | solution.py:23
  76.1 26.7 %collective-permute-start.15 = (f32[1,8,256]{2,1,0:T(8,128)S(1)}, f32[1,8,256]{2,1,0:T(8,128)S(1)}, u32[]{:S(2)}, u32[]{:S(2)}) collective-permute-start(f32[1,8,256]{2,1,0:T(8,128)S(1)} %get-tuple-element.250), channel_id=1, source_target_pairs={{8,0},{16,8},{24,16},{32,24},{40,32},{48,40},{56,48},{64,56},{72,6... | collective-permute-start | bytes 24584 | tf_op jit(solution)/shard_map/ppermute | solution.py:25
  97.2 10.0 %collective-permute-start.10 = (f32[1,16,512]{2,1,0:T(8,128)S(1)}, f32[1,16,512]{2,1,0:T(8,128)S(1)}, u32[]{:S(2)}, u32[]{:S(2)}) collective-permute-start(f32[1,16,512]{2,1,0:T(8,128)S(1)} %get-tuple-element.226), channel_id=1, source_target_pairs={{0,8},{8,16},{16,24},{24,32},{32,40},{40,48},{48,56},{56,64},{64,7... | collective-permute-start | bytes 98312 | tf_op jit(solution)/shard_map/ppermute | solution.py:23
  102.9 9.8 %collective-permute-start.16 = (f32[10,1,256]{2,1,0:T(1,128)S(1)}, f32[10,1,256]{2,1,0:T(1,128)S(1)}, u32[]{:S(2)}, u32[]{:S(2)}) collective-permute-start(f32[10,1,256]{2,1,0:T(1,128)S(1)} %get-tuple-element.241), channel_id=1, source_target_pairs={{0,1},{1,2},{2,3},{3,4},{4,5},{5,6},{6,7},{8,9},{9,10},{10,11},{11... | collective-permute-start | bytes 30728 | tf_op jit(solution)/shard_map/ppermute | solution.py:23
  105.1 7.6 collective-permute-start.17
  167.8 18.0 %collective-permute-start.18 = (f32[1,8,256]{2,1,0:T(8,128)}, f32[1,8,256]{2,1,0:T(8,128)}, u32[]{:S(2)}, u32[]{:S(2)}) collective-permute-start(f32[1,8,256]{2,1,0:T(8,128)} %get-tuple-element.248), channel_id=1, source_target_pairs={{0,8},{8,16},{16,24},{24,32},{32,40},{40,48},{48,56},{56,64},{64,7... | collective-permute-start | bytes 24584 | tf_op jit(solution)/shard_map/ppermute | solution.py:23
  173.2 12.6 %collective-permute-start.19 = (f32[1,8,256]{2,1,0:T(8,128)}, f32[1,8,256]{2,1,0:T(8,128)}, u32[]{:S(2)}, u32[]{:S(2)}) collective-permute-start(f32[1,8,256]{2,1,0:T(8,128)} %get-tuple-element.249), channel_id=1, source_target_pairs={{8,0},{16,8},{24,16},{32,24},{40,32},{48,40},{56,48},{64,56},{72,6... | collective-permute-start | bytes 24584 | tf_op jit(solution)/shard_map/ppermute | solution.py:25
  175.1 28.2 %collective-permute-start.26 = (f32[1,4,128]{2,1,0:T(4,128)}, f32[1,4,128]{2,1,0:T(4,128)}, u32[]{:S(2)}, u32[]{:S(2)}) collective-permute-start(f32[1,4,128]{2,1,0:T(4,128)} %get-tuple-element.271), channel_id=1, source_target_pairs={{0,8},{8,16},{16,24},{24,32},{32,40},{40,48},{48,56},{56,64},{64,7... | collective-permute-start | bytes 6152 | tf_op jit(solution)/shard_map/ppermute | solution.py:23
  181.5 21.9 %collective-permute-start.27 = (f32[1,4,128]{2,1,0:T(4,128)}, f32[1,4,128]{2,1,0:T(4,128)}, u32[]{:S(2)}, u32[]{:S(2)}) collective-permute-start(f32[1,4,128]{2,1,0:T(4,128)} %get-tuple-element.270), channel_id=1, source_target_pairs={{8,0},{16,8},{24,16},{32,24},{40,32},{48,40},{56,48},{64,56},{72,6... | collective-permute-start | bytes 6152 | tf_op jit(solution)/shard_map/ppermute | solution.py:25
  196.2 12.3 %collective-permute-start.22 = (f32[1,8,256]{2,1,0:T(8,128)S(1)}, f32[1,8,256]{2,1,0:T(8,128)S(1)}, u32[]{:S(2)}, u32[]{:S(2)}) collective-permute-start(f32[1,8,256]{2,1,0:T(8,128)S(1)} %get-tuple-element.246), channel_id=1, source_target_pairs={{0,8},{8,16},{16,24},{24,32},{32,40},{40,48},{48,56},{56,64},{64,7... | collective-permute-start | bytes 24584 | tf_op jit(solution)/shard_map/ppermute | solution.py:23
  204.1 9.8 %collective-permute-start.28 = (f32[6,1,128]{2,1,0:T(1,128)S(1)}, f32[6,1,128]{2,1,0:T(1,128)S(1)}, u32[]{:S(2)}, u32[]{:S(2)}) collective-permute-start(f32[6,1,128]{2,1,0:T(1,128)S(1)} %get-tuple-element.261), channel_id=1, source_target_pairs={{0,1},{1,2},{2,3},{3,4},{4,5},{5,6},{6,7},{8,9},{9,10},{10,11},{11... | collective-permute-start | bytes 9224 | tf_op jit(solution)/shard_map/ppermute | solution.py:23
  206.4 7.6 collective-permute-start.29
  227.8 15.7 %collective-permute-start.30 = (f32[1,4,128]{2,1,0:T(4,128)S(1)}, f32[1,4,128]{2,1,0:T(4,128)S(1)}, u32[]{:S(2)}, u32[]{:S(2)}) collective-permute-start(f32[1,4,128]{2,1,0:T(4,128)S(1)} %get-tuple-element.268), channel_id=1, source_target_pairs={{0,8},{8,16},{16,24},{24,32},{32,40},{40,48},{48,56},{56,64},{64,7... | collective-permute-start | bytes 6152 | tf_op jit(solution)/shard_map/ppermute | solution.py:23
  233.8 9.7 %collective-permute-start.31 = (f32[1,4,128]{2,1,0:T(4,128)S(1)}, f32[1,4,128]{2,1,0:T(4,128)S(1)}, u32[]{:S(2)}, u32[]{:S(2)}) collective-permute-start(f32[1,4,128]{2,1,0:T(4,128)S(1)} %get-tuple-element.269), channel_id=1, source_target_pairs={{8,0},{16,8},{24,16},{32,24},{40,32},{48,40},{56,48},{64,56},{72,6... | collective-permute-start | bytes 6152 | tf_op jit(solution)/shard_map/ppermute | solution.py:25
  235.8 12.3 %collective-permute-start.38 = (f32[1,2,64]{2,1,0:T(2,128)S(1)}, f32[1,2,64]{2,1,0:T(2,128)S(1)}, u32[]{:S(2)}, u32[]{:S(2)}) collective-permute-start(f32[1,2,64]{2,1,0:T(2,128)S(1)} %get-tuple-element.292), channel_id=1, source_target_pairs={{0,8},{8,16},{16,24},{24,32},{32,40},{40,48},{48,56},{56,64},{64,7... | collective-permute-start | bytes 1544 | tf_op jit(solution)/shard_map/ppermute | solution.py:23
  252.0 12.0 %collective-permute-start.34 = (f32[1,4,128]{2,1,0:T(4,128)S(1)}, f32[1,4,128]{2,1,0:T(4,128)S(1)}, u32[]{:S(2)}, u32[]{:S(2)}) collective-permute-start(f32[1,4,128]{2,1,0:T(4,128)S(1)} %get-tuple-element.266), channel_id=1, source_target_pairs={{0,8},{8,16},{16,24},{24,32},{32,40},{40,48},{48,56},{56,64},{64,7... | collective-permute-start | bytes 6152 | tf_op jit(solution)/shard_map/ppermute | solution.py:23
  259.7 10.5 %collective-permute-start.40 = (f32[4,1,64]{2,1,0:T(1,128)S(1)}, f32[4,1,64]{2,1,0:T(1,128)S(1)}, u32[]{:S(2)}, u32[]{:S(2)}) collective-permute-start(f32[4,1,64]{2,1,0:T(1,128)S(1)} %get-tuple-element.281), channel_id=1, source_target_pairs={{0,1},{1,2},{2,3},{3,4},{4,5},{5,6},{6,7},{8,9},{9,10},{10,11},{11... | collective-permute-start | bytes 3080 | tf_op jit(solution)/shard_map/ppermute | solution.py:23
  261.9 8.2 %collective-permute-start.41 = (f32[4,1,64]{2,1,0:T(1,128)S(1)}, f32[4,1,64]{2,1,0:T(1,128)S(1)}, u32[]{:S(2)}, u32[]{:S(2)}) collective-permute-start(f32[4,1,64]{2,1,0:T(1,128)S(1)} %get-tuple-element.280), channel_id=1, source_target_pairs={{1,0},{2,1},{3,2},{4,3},{5,4},{6,5},{7,6},{9,8},{10,9},{11,10},{12... | collective-permute-start | bytes 3080 | tf_op jit(solution)/shard_map/ppermute | solution.py:25
  302.6 12.2 %collective-permute-start.48 = (f32[1,2,64]{2,1,0:T(2,128)}, f32[1,2,64]{2,1,0:T(2,128)}, u32[]{:S(2)}, u32[]{:S(2)}) collective-permute-start(f32[1,2,64]{2,1,0:T(2,128)} %get-tuple-element.286), channel_id=1, source_target_pairs={{0,8},{8,16},{16,24},{24,32},{32,40},{40,48},{48,56},{56,64},{64,7... | collective-permute-start | bytes 1544 | tf_op jit(solution)/shard_map/ppermute | solution.py:23
  344.5 8.9 %collective-permute-start.46 = (f32[1,8,32]{2,1,0:T(8,128)}, f32[1,8,32]{2,1,0:T(8,128)}, u32[]{:S(2)}, u32[]{:S(2)}) collective-permute-start(f32[1,8,32]{2,1,0:T(8,128)} %reshape.75), channel_id=1, source_target_pairs={{0,8},{8,16},{16,24},{24,32},{32,40},{40,48},{48,56},{56,64},{64,7... | collective-permute-start | bytes 3080 | tf_op jit(solution)/shard_map/ppermute | solution.py:23
  378.7 7.4 collective-permute-start
  390.5 7.4 collective-permute-start
  402.3 7.6 collective-permute-start
  403.6 7.3 collective-permute-start.1
  414.3 7.6 collective-permute-start
  426.3 7.6 collective-permute-start
  427.6 7.3 collective-permute-start.1
  438.4 7.6 collective-permute-start
  439.7 7.3 collective-permute-start.1
  450.4 7.6 collective-permute-start
  451.7 7.3 collective-permute-start.1
  462.4 7.6 collective-permute-start
  463.7 7.3 collective-permute-start.1
  474.5 7.6 collective-permute-start
  486.5 7.6 collective-permute-start
  487.8 7.3 collective-permute-start.1
  498.5 7.9 %collective-permute-start = (f32[1,8,32]{2,1,0:T(8,128)}, f32[1,8,32]{2,1,0:T(8,128)S(1)}, u32[]{:S(2)}, u32[]{:S(2)}) collective-permute-start(f32[1,8,32]{2,1,0:T(8,128)} %broadcast_select_fusion.2), channel_id=1, source_target_pairs={{8,0},{16,8},{24,16},{32,24},{40,32},{48,40},{56,48},{64,56},{72,6... | collective-permute-start | bytes 3080 | tf_op jit(solution)/shard_map/while/body/eval_jaxpr/ppermute | solution.py:25
  499.8 7.6 collective-permute-start.1
  510.8 7.6 collective-permute-start
  522.9 7.6 collective-permute-start
  524.2 7.3 collective-permute-start.1
  534.9 7.6 collective-permute-start
  561.5 25.4 %collective-permute-start.54 = (f32[4,1,64]{2,1,0:T(1,128)S(1)}, f32[4,1,64]{2,1,0:T(1,128)S(1)}, u32[]{:S(2)}, u32[]{:S(2)}) collective-permute-start(f32[4,1,64]{2,1,0:T(1,128)S(1)} %get-tuple-element.274), channel_id=1, source_target_pairs={{0,1},{1,2},{2,3},{3,4},{4,5},{5,6},{6,7},{8,9},{9,10},{10,11},{11... | collective-permute-start | bytes 3080 | tf_op jit(solution)/shard_map/ppermute | solution.py:23
  590.4 7.3 collective-permute-start.56
  (109 other events, 1446.9 us)
where the time goes:
time: 797 us; the launch traced here: 789 us
  starting transfers between devices  382 us (48%)
  local copies, waits for them, and re-layouts  148 us (19%)
  other arithmetic  135 us (17%)
  waiting for transfers between devices  108 us (14%)
  blocking collectives  12.2 us (2%)
    ppermute x59, starting transfers between devices, padded_2(): lax.ppermute(tail, axis, [(i, (i + 1) % count) for i in range(ends)])  291 us
    ppermute x59, waiting for transfers between devices, padded_2(): lax.ppermute(head, axis, [((i + 1) % count, i) for i in range(ends)])  93.4 us
    ppermute x59, starting transfers between devices, padded_2(): lax.ppermute(head, axis, [((i + 1) % count, i) for i in range(ends)])  90.4 us
    reshape x4, local copies, waits for them, and re-layouts, coarsen(): array_in.reshape(extent_x // 2, 2, extent_y // 2, 2, extent_z // 2, 2)  79.5 us
    reduce_sum x9, other arithmetic, coarsen(): array_in.reshape(extent_x // 2, 2, extent_y // 2, 2, extent_z // 2, 2)  37.3 us
    reshape x3, local copies, waits for them, and re-layouts, refine(): return spread.reshape(2 * extent_x, 2 * extent_y, 2 * extent_z)  31 us
    concatenate x45, other arithmetic, padded_2(): jnp.concatenate([lax.ppermute(tail, axis, [(i, (i + 1) % count) for i in...  26.3 us
    add x16, other arithmetic, slab_turn(): iterate + OMEGA * (source_all - bottom_apply(iterate, slab_set)) / slab_s...  22.4 us
  transfers between devices with their start and end apart: 118, of which 48 were waited for; matrix products, arithmetic and copies ran while one was open for 10% of the time, Pallas kernels for 0%

commit v1 on v0

v1 whole, which is shorter than its diff:
```python
import functools

import jax
import jax.numpy as jnp
from jax import lax
from jax.experimental import pallas as pl
from jax.experimental.pallas import tpu as pltpu
from jax.sharding import PartitionSpec as P

F32 = jnp.float32
BF16 = jnp.bfloat16
OMEGA = 0.8
BOTTOM = 16
VMEM_LIMIT = 56 * 1024 * 1024

X0, Y0, Z0, OX0, OY0 = 22, 24, 512, 3, 4
X1, Y1, Z1, OX1, OY1 = 24, 24, 256, 8, 8
X2, Y2, Z2, OX2, OY2 = 12, 16, 128, 4, 4
Y3, Y4, LANES = 16, 8, 128


def iota(shape, dim):
    return lax.broadcasted_iota(jnp.int32, shape, dim)


def up_of(cells, dim):
    return pltpu.roll(cells, cells.shape[dim] - 1, dim)


def down_of(cells, dim):
    return pltpu.roll(cells, 1, dim)


def split_dot(cells, pick):
    high = cells.astype(BF16)
    rest = cells - high.astype(F32)
    mid = rest.astype(BF16)
    low = (rest - mid.astype(F32)).astype(BF16)
    dot = functools.partial(jnp.dot, preferred_element_type=F32)
    return dot(high, pick) + (dot(mid, pick) + dot(low, pick))


def split_dot_left(pick, cells):
    high = cells.astype(BF16)
    rest = cells - high.astype(F32)
    mid = rest.astype(BF16)
    low = (rest - mid.astype(F32)).astype(BF16)
    dot = functools.partial(jnp.dot, preferred_element_type=F32)
    return dot(pick, high) + (dot(pick, mid) + dot(pick, low))


def pair_sum_matrix(fine, coarse, offset=0):
    hit = (iota((fine, coarse), 0) // 2) + offset == iota((fine, coarse), 1)
    return hit.astype(F32).astype(BF16)


def copy_matrix(coarse, fine):
    hit = iota((coarse, fine), 0) == iota((coarse, fine), 1) // 2
    return hit.astype(F32).astype(BF16)


def inside(shape, dim, start, count):
    place = iota(shape, dim) + start
    return jnp.logical_and(place >= 0, place < count)


def flag(start, count):
    return jnp.where(jnp.logical_and(start >= 0, start < count), 1.0, 0.0).astype(F32)


def loop(first, last, body):
    def step(i, carry):
        body(i)
        return carry

    lax.fori_loop(first, last, step, 0)


def make_faces(c, wx, wy, wz, d, q, first, last, in_x, in_y, whole_y=0):
    rows, cells = c.shape[1], c.shape[2]
    end_z = iota((rows, cells), 1) == cells - 1
    start_z = iota((rows, cells), 1) == 0
    row = iota((rows, cells), 0)
    wx[first - 1] = 0.5 * (c[first - 1] + c[first])

    def body(i):
        here = c[i]
        after = c[i + 1]
        before = c[i - 1]
        y_up, y_down = up_of(here, 0), down_of(here, 0)
        if whole_y:
            y_up = jnp.where(row == rows - 1, 0.0, y_up)
            y_down = jnp.where(row == 0, 0.0, y_down)
        z_up = jnp.where(end_z, 0.0, up_of(here, 1))
        z_down = jnp.where(start_z, 0.0, down_of(here, 1))
        wx[i] = 0.5 * (here + after)
        side = 0.5 * (here + y_up)
        wy[i] = jnp.where(row == rows - 1, 0.0, side) if whole_y else side
        wz[i] = jnp.where(end_z, 0.0, 0.5 * (here + z_up))
        total = 3.0 * here + 0.5 * ((after + before) + (y_up + y_down) + (z_up + z_down))
        d[i] = total
        q[i] = (in_y * (OMEGA * in_x(i))) / jnp.maximum(total, 1e-30)

    loop(first, last, body)


def neighbours(v, wx, wy, wz, i):
    here = v[i]
    side_y, side_z = wy[i], wz[i]
    along_x = wx[i] * v[i + 1] + wx[i - 1] * v[i - 1]
    along_y = side_y * up_of(here, 0) + down_of(side_y * here, 0)
    along_z = side_z * up_of(here, 1) + down_of(side_z * here, 1)
    return here, along_x + along_y + along_z


def sweep(v, out, b, wx, wy, wz, q, first, last):
    def body(i):
        here, total = neighbours(v, wx, wy, wz, i)
        out[i] = (0.2 * here + b[i]) + q[i] * total

    loop(first, last, body)


def defect(v, source, wx, wy, wz, d, i):
    here, total = neighbours(v, wx, wy, wz, i)
    return (source[i] - d[i] * here) + total


def lanes(cells, k):
    return cells[:, LANES * k : LANES * k + LANES]


def keep(scratch, j, cells):
    for k in range(cells.shape[1] // LANES):
        scratch[j, k] = lanes(cells, k)


def halve_rows(scratch, j, start, count):
    parts = [
        scratch[j, k, pl.ds(start, count, stride=2), :] + scratch[j, k, pl.ds(start + 1, count, stride=2), :]
        for k in range(scratch.shape[1])
    ]
    return jnp.concatenate(parts, axis=1)


def double_rows(scratch, cells, start):
    for k in range(scratch.shape[0]):
        for odd in range(2):
            scratch[k, pl.ds(start + odd, cells.shape[0], stride=2), :] = lanes(cells, k)
    return jnp.concatenate([scratch[k] for k in range(scratch.shape[0])], axis=1)


def call(kernel, out_shape, scratch, in_specs=None, out_specs=None, flops=1000000, bytes_accessed=1000000):
    extra = {}
    if in_specs is not None:
        extra["in_specs"] = in_specs
    if out_specs is not None:
        extra["out_specs"] = out_specs
    return pl.pallas_call(
        kernel,
        out_shape=out_shape,
        scratch_shapes=scratch,
        compiler_params=pltpu.CompilerParams(vmem_limit_bytes=VMEM_LIMIT),
        cost_estimate=pl.CostEstimate(flops=flops, bytes_accessed=bytes_accessed, transcendentals=0),
        **extra,
    )


def struct(*shape):
    return jax.ShapeDtypeStruct(shape, F32)


def vmem(*shape):
    return pltpu.VMEM(shape, F32)


def coarsen_kernel(c_ref, out_ref, pairs):
    for i in range(8):
        keep(pairs, i, c_ref[2 * i] + c_ref[2 * i + 1])
    rows = jnp.concatenate([halve_rows(pairs, i, 0, 8) for i in range(8)], axis=0)
    out_ref[...] = (0.125 * split_dot(rows, pair_sum_matrix(Z0, Z1))).reshape(8, 8, Z1)


def coarsen_own(coefficient):
    return call(coarsen_kernel, struct(8, 8, Z1), [vmem(8, Z0 // LANES, 16, LANES)])(coefficient)


def edge_kernel(count_x, c_ref, g_ref, low_ref, high_ref, top_ref, bottom_ref):
    place = lax.axis_index("gx")
    first = jnp.where(place > 0, 1.0, 0.0).astype(F32)
    last = jnp.where(place < count_x - 1, 1.0, 0.0).astype(F32)
    row = iota((8, Z0), 0)

    def put(i, c, g):
        top_ref[i] = jnp.where(row < 4, pltpu.roll(c[8:16], 4, 0), g[8:16])
        bottom_ref[i] = jnp.where(row < 4, g[0:8], pltpu.roll(c[0:8], 4, 0))

    nothing = jnp.zeros((16, Z0), F32)
    for i in range(3):
        put(i, low_ref[i] * first, low_ref[i + 2] * first if i > 0 else nothing)
        put(19 + i, high_ref[i] * last, high_ref[i + 3] * last if i < 2 else nothing)

    def body(i):
        put(i + 3, c_ref[i], g_ref[i])

    loop(0, 16, body)


def edges_y(coefficient, right_side, low, high, count_x):
    return call(
        functools.partial(edge_kernel, count_x), [struct(X0, 8, Z0), struct(X0, 8, Z0)], []
    )(coefficient, right_side, low, high)


def down0_kernel(
    count_x, count_y,
    c_ref, g_ref, low_ref, high_ref, below_ref, above_ref,
    g1_ref, v_low_ref, v_high_ref, v_own_ref, *rest,
):
    stored, (c, g, wx, wy, wz, d, q, b, v, pairs, sems) = rest[:6], rest[6:]
    place_x, place_y = lax.axis_index("gx"), lax.axis_index("gy")
    first = jnp.where(place_x > 0, 1.0, 0.0).astype(F32)
    last = jnp.where(place_x < count_x - 1, 1.0, 0.0).astype(F32)
    low_y = jnp.where(place_y > 0, 1.0, 0.0).astype(F32)
    high_y = jnp.where(place_y < count_y - 1, 1.0, 0.0).astype(F32)
    row = iota((8, Z0), 0) < 4

    def put(frame, i, own, below, above):
        head, tail = pltpu.roll(own[0:8], 4, 0), pltpu.roll(own[8:16], 4, 0)
        frame[i, 0:8] = jnp.where(row, below, head)
        frame[i, 8:16] = jnp.where(row, head, tail)
        frame[i, 16:24] = jnp.where(row, tail, above)

    def put_both(i, own_c, own_g):
        below, above = below_ref[i] * low_y, above_ref[i] * high_y
        put(c, i, own_c, below, above)
        put(g, i, own_g, pltpu.roll(below, 4, 0), pltpu.roll(above, 4, 0))

    nothing = jnp.zeros((16, Z0), F32)
    for i in range(3):
        put_both(i, low_ref[i] * first, low_ref[i + 2] * first if i > 0 else nothing)
        put_both(19 + i, high_ref[i] * last, high_ref[i + 3] * last if i < 2 else nothing)

    def body(i):
        put_both(i + 3, c_ref[i], g_ref[i])

    loop(0, 16, body)

    in_y = inside((Y0, Z0), 0, place_y * 16 - OY0, 16 * count_y).astype(F32)
    make_faces(
        c, wx, wy, wz, d, q, 1, X0 - 1, lambda i: flag(place_x * 16 - OX0 + i, 16 * count_x), in_y
    )

    def begin(i):
        b[i] = q[i] * g[i]

    loop(1, X0 - 1, begin)
    copies = [
        pltpu.make_async_copy(here, there, sems.at[k])
        for k, (here, there) in enumerate(zip((wx, wy, wz, d, q, b), stored))
    ]
    for copy in copies:
        copy.start()
    sweep(b, v, b, wx, wy, wz, q, 2, X0 - 2)

    def own_of(i):
        own = pltpu.roll(v[i + 3], Y0 - OY0, 0)[0:16]
        v_own_ref[i] = own

    loop(0, 16, own_of)
    for i in range(3):
        v_high_ref[i] = v_own_ref[13 + i]
        v_low_ref[i] = v_own_ref[i]

    def restrict(j):
        i = 2 * j + OX0
        keep(pairs, j, defect(v, g, wx, wy, wz, d, i) + defect(v, g, wx, wy, wz, d, i + 1))

    loop(0, 8, restrict)
    rows = jnp.concatenate([halve_rows(pairs, i, 4, 8) for i in range(8)], axis=0)
    g1_ref[...] = (0.5 * split_dot(rows, pair_sum_matrix(Z0, Z1))).reshape(8, 8, Z1)
    for copy in copies:
        copy.wait()


def down0(count_x, count_y, *operands):
    frame = (X0, Y0, Z0)
    any_space = pl.BlockSpec(memory_space=pl.ANY)
    whole = pl.BlockSpec(memory_space=pltpu.VMEM)
    return call(
        functools.partial(down0_kernel, count_x, count_y),
        [struct(8, 8, Z1), struct(3, 16, Z0), struct(3, 16, Z0), struct(16, 16, Z0)] + [struct(*frame)] * 6,
        [vmem(*frame)] * 9 + [vmem(8, Z0 // LANES, Y0, LANES), pltpu.SemaphoreType.DMA((6,))],
        in_specs=[whole] * 6,
        out_specs=[whole] * 4 + [any_space] * 6,
    )(*operands)


def prepare_kernel(
    count_x, count_y, mid_ref, below_ref, above_ref,
    wx1, wy1, wz1, d1, q1, wx2, wy2, wz2, d2, q2, c3_ref, c1, c2, pairs,
):
    place_x, place_y = lax.axis_index("gx"), lax.axis_index("gy")
    low_y = jnp.where(place_y > 0, 1.0, 0.0).astype(F32)
    high_y = jnp.where(place_y < count_y - 1, 1.0, 0.0).astype(F32)
    c1[:, 0:8, :] = below_ref[...] * low_y
    c1[:, 8:16, :] = mid_ref[...]
    c1[:, 16:24, :] = above_ref[...] * high_y
    in_y = inside((Y1, Z1), 0, place_y * 8 - OY1, 8 * count_y).astype(F32)
    make_faces(
        c1, wx1, wy1, wz1, d1, q1, 2, X1 - 2, lambda i: flag(place_x * 8 - OX1 + i, 8 * count_x), in_y
    )
    for i in range(12):
        keep(pairs, i, c1[2 * i] + c1[2 * i + 1])
    blank = jnp.zeros((4, Z1), F32)
    rows = []
    for i in range(12):
        rows.append(halve_rows(pairs, i, 0, 12))
        rows.append(blank)
    c2[...] = (0.125 * split_dot(jnp.concatenate(rows, axis=0), pair_sum_matrix(Z1, Z2))).reshape(X2, Y2, Z2)
    in_y = inside((Y2, Z2), 0, place_y * 4 - OY2, 4 * count_y).astype(F32)
    make_faces(
        c2, wx2, wy2, wz2, d2, q2, 1, X2 - 1, lambda i: flag(place_x * 4 - OX2 + i, 4 * count_x), in_y
    )
    rows = jnp.concatenate([c2[4] + c2[5], c2[6] + c2[7]], axis=0)
    thin = 0.125 * split_dot(rows, pair_sum_matrix(Z2, LANES, 64))
    row = iota((8, LANES), 0)
    c3 = jnp.zeros((8, LANES), F32)
    for i in range(2):
        for j in range(2):
            at = 16 * i + 4 + 2 * j
            both = thin[at : at + 1] + thin[at + 1 : at + 2]
            c3 = jnp.where(row == 2 * i + j, jnp.broadcast_to(both, (8, LANES)), c3)
    c3_ref[...] = c3


def prepare(count_x, count_y, *operands):
    frame1, frame2 = (X1, Y1, Z1), (X2, Y2, Z2)
    return call(
        functools.partial(prepare_kernel, count_x, count_y),
        [struct(*frame1)] * 5 + [struct(*frame2)] * 5 + [struct(8, LANES)],
        [vmem(*frame1), vmem(*frame2), vmem(12, Z1 // LANES, Y1, LANES)],
    )(*operands)


def down1_kernel(
    count_x, count_y, mid_ref, below_ref, above_ref,
    wx1, wy1, wz1, d1, q1, wx2, wy2, wz2, d2, q2, c3_ref,
    v1_ref, b1_ref, send2_ref, send3_ref, g1, g2, b2, v2, pairs, thin,
):
    place_y = lax.axis_index("gy")
    low_y = jnp.where(place_y > 0, 1.0, 0.0).astype(F32)
    high_y = jnp.where(place_y < count_y - 1, 1.0, 0.0).astype(F32)
    g1[2:22, 0:8, :] = below_ref[...] * low_y
    g1[2:22, 8:16, :] = mid_ref[...]
    g1[2:22, 16:24, :] = above_ref[...] * high_y

    def begin1(i):
        b1_ref[i] = q1[i] * g1[i]

    loop(2, X1 - 2, begin1)
    sweep(b1_ref, v1_ref, b1_ref, wx1, wy1, wz1, q1, 3, X1 - 3)

    def restrict(j):
        i = 2 * j + 4
        after = defect(v1_ref, g1, wx1, wy1, wz1, d1, i + 1)
        keep(pairs, j, defect(v1_ref, g1, wx1, wy1, wz1, d1, i) + after)

    loop(0, 8, restrict)
    rows = jnp.concatenate([halve_rows(pairs, i, 4, 8) for i in range(8)], axis=0)
    small = 0.5 * split_dot(rows, pair_sum_matrix(Z1, Z2))
    g2[...] = jnp.zeros((X2, Y2, Z2), F32)
    for i in range(8):
        g2[2 + i, 2:10, :] = small[8 * i : 8 * i + 8]
    for i in range(2, X2 - 2):
        b2[i] = q2[i] * g2[i]
    sweep(b2, v2, b2, wx2, wy2, wz2, q2, 3, X2 - 3)
    row = iota((8, Z2), 0) < 4
    for i in range(4):
        send2_ref[i] = jnp.where(row, pltpu.roll(v2[4 + i, 0:8, :], 4, 0), g2[4 + i, 0:8, :])
    halves = [
        defect(v2, g2, wx2, wy2, wz2, d2, 4 + 2 * i) + defect(v2, g2, wx2, wy2, wz2, d2, 5 + 2 * i)
        for i in range(2)
    ]
    thin[...] = 0.5 * split_dot(jnp.concatenate(halves, axis=0), pair_sum_matrix(Z2, LANES))
    row = iota((8, LANES), 0)
    source = jnp.zeros((8, LANES), F32)
    for i in range(2):
        for j in range(2):
            at = 16 * i + 4 + 2 * j
            both = thin[at : at + 1, :] + thin[at + 1 : at + 2, :]
            source = jnp.where(row == 2 * i + j, jnp.broadcast_to(both, (8, LANES)), source)
    source = source + c3_ref[...]
    double = jnp.where(row < 4, source, pltpu.roll(source, 4, 0))
    for i in range(count_x * count_y // 2):
        send3_ref[8 * i : 8 * i + 8, :] = double


def down1(count_x, count_y, *operands):
    frame1, frame2 = (X1, Y1, Z1), (X2, Y2, Z2)
    return call(
        functools.partial(down1_kernel, count_x, count_y),
        [struct(*frame1), struct(*frame1), struct(4, 8, Z2), struct(4 * count_x * count_y, LANES)],
        [vmem(*frame1)] + [vmem(*frame2)] * 3 + [vmem(8, Z1 // LANES, Y1, LANES), vmem(32, LANES)],
    )(*operands)


def iterate_edge_kernel(count_x, own_ref, low_ref, high_ref, top_ref, bottom_ref):
    place = lax.axis_index("gx")
    first = jnp.where(place > 0, 1.0, 0.0).astype(F32)
    last = jnp.where(place < count_x - 1, 1.0, 0.0).astype(F32)
    row = iota((8, Z0), 0) < 4

    def slab(i):
        if i < 3:
            return low_ref[i] * first
        if i < 19:
            return own_ref[i - 3]
        return high_ref[i - 19] * last

    for j in range(X0 // 2):
        even, odd = slab(2 * j), slab(2 * j + 1)
        top_ref[j] = jnp.where(row, pltpu.roll(even[8:16], 4, 0), odd[8:16])
        bottom_ref[j] = jnp.where(row, even[0:8], pltpu.roll(odd[0:8], 4, 0))


def iterate_edges(count_x, own, low, high):
    return call(
        functools.partial(iterate_edge_kernel, count_x), [struct(X0 // 2, 8, Z0), struct(X0 // 2, 8, Z0)], []
    )(own, low, high)


def up_kernel(
    count_x, count_y,
    all_ref, mid2, below2, above2, wx2, wy2, wz2, q2,
    v1, b1, wx1, wy1, wz1, q1,
    v_own, v_low, v_high, v_below, v_above, g_ref,
    wx0_hbm, wy0_hbm, wz0_hbm, d0_hbm, q0_hbm, b0_hbm,
    solution_ref, residual_ref,
    c3, wx3, wy3, wz3, d3, q3, b3, v3, w3, thin3,
    c4, wx4, wy4, wz4, d4, q4, g4, v4, w4, thin4,
    v2, w2, b2, w1, spread1, wx0, wy0, wz0, d0, q0, b0, v0, w0, spread0, sems,
):
    place_x, place_y = lax.axis_index("gx"), lax.axis_index("gy")
    copies = [
        pltpu.make_async_copy(there, here, sems.at[k])
        for k, (there, here) in enumerate(
            zip((wx0_hbm, wy0_hbm, wz0_hbm, d0_hbm, q0_hbm, b0_hbm), (wx0, wy0, wz0, d0, q0, b0))
        )
    ]
    for copy in copies:
        copy.start()
    n3, n4 = 2 * count_x, count_x

    c3[...] = jnp.zeros(c3.shape, F32)
    b3[...] = jnp.zeros(b3.shape, F32)
    v3[...] = jnp.zeros(v3.shape, F32)
    w3[...] = jnp.zeros(w3.shape, F32)
    lane = iota((count_y, LANES), 1) < 64
    for i in range(n3):
        base = (i // 2) * count_y * 4 + 2 * (i % 2)
        for j in range(2):
            part = all_ref[pl.ds(base + j, count_y, stride=4), :]
            b3[1 + i, pl.ds(j, count_y, stride=2), :] = jnp.where(lane, part, 0.0)
            c3[1 + i, pl.ds(j, count_y, stride=2), :] = jnp.where(lane, pltpu.roll(part, 64, 1), 0.0)
    in_y = jnp.logical_and(iota((Y3, LANES), 0) < 2 * count_y, iota((Y3, LANES), 1) < 64).astype(F32)
    make_faces(c3, wx3, wy3, wz3, d3, q3, 1, n3 + 1, lambda i: 1.0, in_y, whole_y=1)

    def begin3(i):
        v3[i] = q3[i] * b3[i]

    loop(1, n3 + 1, begin3)

    def sweep3(i):
        here, total = neighbours(v3, wx3, wy3, wz3, i)
        w3[i] = 0.2 * here + q3[i] * (b3[i] + total)

    loop(1, n3 + 1, sweep3)

    def restrict3(j):
        i = 2 * j + 1
        thin3[j] = defect(w3, b3, wx3, wy3, wz3, d3, i) + defect(w3, b3, wx3, wy3, wz3, d3, i + 1)

    loop(0, n4, restrict3)
    valid = iota((Y4, LANES), 0) < count_y
    rows = jnp.concatenate(
        [thin3[i, pl.ds(0, Y4, stride=2), :] + thin3[i, pl.ds(1, Y4, stride=2), :] for i in range(n4)], axis=0
    )
    pick = pair_sum_matrix(LANES, LANES)
    g4[...] = (0.5 * split_dot(rows, pick)).reshape(n4, Y4, LANES)
    for i in range(n4):
        thin3[i] = c3[2 * i + 1] + c3[2 * i + 2]
    rows = jnp.concatenate(
        [thin3[i, pl.ds(0, Y4, stride=2), :] + thin3[i, pl.ds(1, Y4, stride=2), :] for i in range(n4)], axis=0
    )
    c4[...] = jnp.zeros(c4.shape, F32)
    c4[1 : n4 + 1] = (0.125 * split_dot(rows, pick)).reshape(n4, Y4, LANES)
    in_y = jnp.logical_and(valid, iota((Y4, LANES), 1) < 32).astype(F32)
    make_faces(c4, wx4, wy4, wz4, d4, q4, 1, n4 + 1, lambda i: 1.0, in_y, whole_y=1)
    v4[...] = jnp.zeros(v4.shape, F32)
    w4[...] = jnp.zeros(w4.shape, F32)
    for i in range(n4):
        g4[i] = q4[1 + i] * g4[i]
        v4[1 + i] = g4[i]

    def bottom(source, target):
        for i in range(n4):
            here, total = neighbours(source, wx4, wy4, wz4, 1 + i)
            target[1 + i] = (0.2 * here + g4[i]) + q4[1 + i] * total

    def two(step):
        bottom(v4, w4)
        bottom(w4, v4)

    loop(0, (BOTTOM - 2) // 2, two)
    bottom(v4, w4)

    wide = split_dot(w4[1 : n4 + 1].reshape(n4 * Y4, LANES), copy_matrix(LANES, LANES)).reshape(n4, Y4, LANES)
    for i in range(n4):
        thin4[pl.ds(0, Y4, stride=2), :] = wide[i]
        thin4[pl.ds(1, Y4, stride=2), :] = wide[i]
        extra = thin4[...]
        v3[1 + 2 * i] = w3[1 + 2 * i] + extra
        v3[2 + 2 * i] = w3[2 + 2 * i] + extra

    loop(1, n3 + 1, sweep3)

    def sweep3_again(i):
        here, total = neighbours(w3, wx3, wy3, wz3, i)
        v3[i] = 0.2 * here + q3[i] * (b3[i] + total)

    loop(1, n3 + 1, sweep3_again)

    low_y = jnp.where(place_y > 0, 1.0, 0.0).astype(F32)
    high_y = jnp.where(place_y < count_y - 1, 1.0, 0.0).astype(F32)
    near = jnp.zeros((6, Y3, LANES), F32)
    slabs = []
    for j in range(6):
        at = 2 * place_x - 2 + j
        slabs.append(v3[1 + jnp.clip(at, 0, n3 - 1)] * flag(at, n3))
    wide = split_dot(jnp.concatenate(slabs, axis=0), copy_matrix(LANES, LANES))
    target, origin = iota((Y2, Y3), 0), iota((Y2, Y3), 1)
    rows = jnp.logical_and(origin == 2 * place_y - 2 + target // 2, target < 12).astype(F32).astype(BF16)
    half = iota((8, Z2), 0) < 4
    for j in range(6):
        extra = split_dot_left(rows, wide[Y3 * j : Y3 * j + Y3])
        for k in range(2):
            i = 2 * j + k
            below, mid, above = below2[i] * low_y, mid2[i], above2[i] * high_y
            v2[i, 0:8] = jnp.where(half, below, pltpu.roll(mid, 4, 0)) + extra[0:8]
            v2[i, 8:16] = jnp.where(half, above, 0.0) + extra[8:16]
            b2[i, 0:8] = jnp.where(half, pltpu.roll(below, 4, 0), mid)
            b2[i, 8:16] = jnp.where(half, pltpu.roll(above, 4, 0), 0.0)
    for i in range(1, X2 - 1):
        b2[i] = q2[i] * b2[i]
    sweep(v2, w2, b2, wx2, wy2, wz2, q2, 1, X2 - 1)
    sweep(w2, v2, b2, wx2, wy2, wz2, q2, 2, X2 - 2)

    wide = split_dot(v2[2:10].reshape(8 * Y2, Z2), copy_matrix(Z2, Z1)).reshape(8, Y2, Z1)
    spread1[...] = jnp.zeros(spread1.shape, F32)
    for j in range(8):
        extra = double_rows(spread1, wide[j, 2:10], 4)
        for k in range(2):
            i = 4 + 2 * j + k
            v1[i] = v1[i] + extra
    sweep(v1, w1, b1, wx1, wy1, wz1, q1, 5, X1 - 5)
    sweep(w1, v1, b1, wx1, wy1, wz1, q1, 6, X1 - 6)

    wide = split_dot(v1[6:18].reshape(12 * Y1, Z1), copy_matrix(Z1, Z0)).reshape(12, Y1, Z0)
    first = jnp.where(place_x > 0, 1.0, 0.0).astype(F32)
    last = jnp.where(place_x < count_x - 1, 1.0, 0.0).astype(F32)
    half = iota((8, Z0), 0) < 4
    for copy in copies:
        copy.wait()
    for j in range(12):
        extra = double_rows(spread0, wide[j, 6:18], 0)
        for k in range(2):
            i = 2 * j - 1 + k
            if i < 0 or i >= X0:
                continue
            own = v_low[i] * first if i < 3 else v_own[i - 3] if i < 19 else v_high[i - 19] * last
            below, above = v_below[i // 2] * low_y, v_above[i // 2] * high_y
            if i % 2:
                below = pltpu.roll(below, 4, 0)
            else:
                above = pltpu.roll(above, 4, 0)
            head, tail = pltpu.roll(own[0:8], 4, 0), pltpu.roll(own[8:16], 4, 0)
            v0[i, 0:8] = jnp.where(half, below, head) + extra[0:8]
            v0[i, 8:16] = jnp.where(half, head, tail) + extra[8:16]
            v0[i, 16:24] = jnp.where(half, tail, above) + extra[16:24]
    sweep(v0, w0, b0, wx0, wy0, wz0, q0, 1, X0 - 1)
    sweep(w0, v0, b0, wx0, wy0, wz0, q0, 2, X0 - 2)

    def finish(i):
        here, total = neighbours(v0, wx0, wy0, wz0, i + OX0)
        solution_ref[i] = pltpu.roll(here, Y0 - OY0, 0)[0:16]
        residual_ref[i] = g_ref[i] + pltpu.roll(total - d0[i + OX0] * here, Y0 - OY0, 0)[0:16]

    loop(0, 16, finish)


def up(count_x, count_y, *operands):
    any_space = pl.BlockSpec(memory_space=pl.ANY)
    whole = pl.BlockSpec(memory_space=pltpu.VMEM)
    frame0, frame1, frame2 = (X0, Y0, Z0), (X1, Y1, Z1), (X2, Y2, Z2)
    frame3, frame4 = (2 * count_x + 2, Y3, LANES), (count_x + 2, Y4, LANES)
    return call(
        functools.partial(up_kernel, count_x, count_y),
        [struct(16, 16, Z0), struct(16, 16, Z0)],
        [vmem(*frame3)] * 9 + [vmem(count_x, Y3, LANES)]
        + [vmem(*frame4)] * 6 + [vmem(count_x, Y4, LANES)] + [vmem(*frame4)] * 2 + [vmem(Y3, LANES)]
        + [vmem(*frame2)] * 3 + [vmem(*frame1), vmem(Z1 // LANES, Y1, LANES)]
        + [vmem(*frame0)] * 8 + [vmem(Z0 // LANES, Y0, LANES), pltpu.SemaphoreType.DMA((6,))],
        in_specs=[whole] * (len(operands) - 6) + [any_space] * 6,
        out_specs=[whole] * 2,
    )(*operands)


def to_next(cells, axis):
    count = lax.axis_size(axis)
    return lax.ppermute(cells, axis, [(i, (i + 1) % count) for i in range(count)])


def to_previous(cells, axis):
    count = lax.axis_size(axis)
    return lax.ppermute(cells, axis, [((i + 1) % count, i) for i in range(count)])


def shards(right_side, coefficient):
    count_x, count_y = lax.axis_size("gx"), lax.axis_size("gy")
    place_x = lax.axis_index("gx")

    def with_sides(low, cells, high):
        low = jnp.where(place_x > 0, low, 0.0)
        high = jnp.where(place_x < count_x - 1, high, 0.0)
        return jnp.concatenate([low, cells, high], axis=0)

    low = to_next(jnp.concatenate([coefficient[13:16], right_side[14:16]], axis=0), "gx")
    high = to_previous(jnp.concatenate([coefficient[0:3], right_side[0:2]], axis=0), "gx")
    c1 = coarsen_own(coefficient)
    c1_low, c1_high = to_next(c1, "gx"), to_previous(c1, "gx")
    top, bottom = edges_y(coefficient, right_side, low, high, count_x)
    below, above = to_next(top, "gy"), to_previous(bottom, "gy")
    c1_mid = with_sides(c1_low, c1, c1_high)
    c1_below, c1_above = to_next(c1_mid, "gy"), to_previous(c1_mid, "gy")

    g1, v_first, v_last, v_own, wx0, wy0, wz0, d0, q0, b0 = down0(
        count_x, count_y, coefficient, right_side, low, high, below, above
    )

    g1_low, g1_high = to_next(g1[2:8], "gx"), to_previous(g1[0:6], "gx")
    levels = prepare(count_x, count_y, c1_mid, c1_below, c1_above)
    wx1, wy1, wz1, d1, q1, wx2, wy2, wz2, d2, q2, c3 = levels
    g1_mid = with_sides(g1_low, g1, g1_high)
    g1_below, g1_above = to_next(g1_mid, "gy"), to_previous(g1_mid, "gy")
    v_low, v_high = to_next(v_last, "gx"), to_previous(v_first, "gx")
    v_top, v_bottom = iterate_edges(count_x, v_own, v_low, v_high)
    v_below, v_above = to_next(v_top, "gy"), to_previous(v_bottom, "gy")
    v1, b1, send2, send3 = down1(count_x, count_y, g1_mid, g1_below, g1_above, *levels)

    everything = lax.all_to_all(send3, ("gx", "gy"), split_axis=0, concat_axis=0, tiled=True)
    mid2 = with_sides(to_next(send2, "gx"), send2, to_previous(send2, "gx"))
    below2, above2 = to_next(mid2, "gy"), to_previous(mid2, "gy")
    return tuple(
        up(
            count_x, count_y, everything, mid2, below2, above2, wx2, wy2, wz2, q2,
            v1, b1, wx1, wy1, wz1, q1, v_own, v_low, v_high, v_below, v_above, right_side,
            wx0, wy0, wz0, d0, q0, b0,
        )
    )


def solution(mesh):
    specs = (P("gx", "gy", None), P("gx", "gy", None))
    return jax.shard_map(shards, mesh=mesh, in_specs=specs, out_specs=specs, check_vma=False)
```

time: 797 us -> 123 us (0.15)
  starting transfers between devices: 382 us -> 39.2 us
  local copies, waits for them, and re-layouts: 148 us -> 7.52 us
  other arithmetic: 135 us -> 0.94 us
  waiting for transfers between devices: 108 us -> 17.6 us
  Pallas kernels: 0 us -> 56 us
  blocking collectives: 12.2 us -> 0 us
    ppermute x118 -> x20, starting transfers between devices: 382 us -> 30.1 us  [the longest x10 22.2 us: to_previous(): lax.ppermute(cells, axis, [((i + 1) % count, i) for i in range(count)])]
    reshape x7 -> x0, local copies, waits for them, and re-layouts: 111 us -> none  [the longest x4 79.5 us: coarsen(): array_in.reshape(extent_x // 2, 2, extent_y // 2, 2, extent_z // 2, 2)]
    ppermute x118 -> x20, waiting for transfers between devices: 108 us -> 11.1 us  [the longest x10 5.86 us: to_previous(): lax.ppermute(cells, axis, [((i + 1) % count, i) for i in range(count)])]
    pallas_call x0 -> x7, Pallas kernels: none -> 56 us  [the longest x1 29.5 us: up(): call(functools.partial(up_kernel, count_x, count_y), [struct(16, 16, Z0),...]
    reduce_sum x9 -> x0, other arithmetic: 37.3 us -> none  [coarsen(): array_in.reshape(extent_x // 2, 2, extent_y // 2, 2, extent_z // 2, 2)]
    add x32 -> x0, other arithmetic: 35.5 us -> none  [the longest x16 22.4 us: slab_turn(): iterate + OMEGA * (source_all - bottom_apply(iterate, slab_set)) / slab_s...]
    concatenate x45 -> x5, other arithmetic: 26.3 us -> 0.9 us  [the longest x3 0.87 us: with_sides(): return jnp.concatenate([low, cells, high], axis=0)]
    while x16 -> x0, other arithmetic: 19.8 us -> none
  transfers between devices with their start and end apart: 118 -> 21, of which waited for: 48 -> 7; matrix products, arithmetic and copies ran while one was open for 10% -> 1% of each run, Pallas kernels for 0% -> 15%
where the time goes in v1:
time: 123 us; the launch traced here: 122 us
  Pallas kernels  56 us (46%)
  starting transfers between devices  39.2 us (32%)
  waiting for transfers between devices  17.6 us (14%)
  local copies, waits for them, and re-layouts  7.52 us (6%)
    pallas_call x1, Pallas kernels, up(): call(functools.partial(up_kernel, count_x, count_y), [struct(16, 16, Z0),...  29.5 us
    ppermute x10, starting transfers between devices, to_previous(): lax.ppermute(cells, axis, [((i + 1) % count, i) for i in range(count)])  22.2 us
    all_to_all x1, starting transfers between devices, shards(): lax.all_to_all(send3, ('gx', 'gy'), split_axis=0, concat_axis=0, tiled=True)  9.16 us
    pallas_call x1, Pallas kernels, down0(): call(functools.partial(down0_kernel, count_x, count_y), [struct(8, 8, Z1)...  8.22 us
    ppermute x10, starting transfers between devices, to_next(): lax.ppermute(cells, axis, [(i, (i + 1) % count) for i in range(count)])  7.88 us
    all_to_all x1, waiting for transfers between devices, shards(): lax.all_to_all(send3, ('gx', 'gy'), split_axis=0, concat_axis=0, tiled=True)  6.41 us
    pallas_call x1, Pallas kernels, down1(): call(functools.partial(down1_kernel, count_x, count_y), [struct(*frame1),...  6.34 us
    ppermute x10, waiting for transfers between devices, to_previous(): lax.ppermute(cells, axis, [((i + 1) % count, i) for i in range(count)])  5.86 us
  transfers between devices with their start and end apart: 21, of which 7 were waited for; matrix products, arithmetic and copies ran while one was open for 1% of the time, Pallas kernels for 15%

profile of v1, /device:TPU:1, one launch (start us, length us, event | category | flops | bytes accessed | tf_op | source)
XLA Modules:
  0.0 122.2 jit_solution(17863823210464116997)
XLA Ops:
  0.6 0.9 fusion.1
  1.5 1.0 fusion
  2.5 2.1 %collective-permute-start = (f32[5,16,512]{2,1,0:T(8,128)S(1)}, f32[5,16,512]{2,1,0:T(8,128)S(1)}, u32[]{:S(2)}, u32[]{:S(2)}) collective-permute-start(f32[5,16,512]{2,1,0:T(8,128)S(1)} %pad_maximum_fusion.1), channel_id=1, source_target_pairs={{0,8},{8,16},{16,24},{24,32},{32,40},{40,48},{48,56},{56,64},{64,7... | collective-permute-start | bytes 491528 | tf_op jit(solution)/shard_map/ppermute | solution.py:621
  4.6 3.8 %collective-permute-start.1 = (f32[5,16,512]{2,1,0:T(8,128)S(1)}, f32[5,16,512]{2,1,0:T(8,128)S(1)}, u32[]{:S(2)}, u32[]{:S(2)}) collective-permute-start(f32[5,16,512]{2,1,0:T(8,128)S(1)} %pad_maximum_fusion.2), channel_id=1, source_target_pairs={{8,0},{16,8},{24,16},{32,24},{40,32},{48,40},{56,48},{64,56},{72,6... | collective-permute-start | bytes 491528 | tf_op jit(solution)/shard_map/ppermute | solution.py:626
  8.4 1.9 %shard_map.43 = f32[8,8,256]{2,1,0:T(8,128)} custom-call(f32[16,16,512]{2,1,0:T(8,128)} %c_ref.5), custom_call_target="tpu_custom_call" | custom-call | flops 1000000 | bytes 1000000 | tf_op jit(solution)/shard_map/pallas_call | solution.py:185
  10.4 1.4 %collective-permute-start.9 = (f32[8,8,256]{2,1,0:T(8,128)}, f32[8,8,256]{2,1,0:T(8,128)S(1)}, u32[]{:S(2)}, u32[]{:S(2)}) collective-permute-start(f32[8,8,256]{2,1,0:T(8,128)} %shard_map.43), channel_id=1, source_target_pairs={{8,0},{16,8},{24,16},{32,24},{40,32},{48,40},{56,48},{64,56},{72,6... | collective-permute-start | bytes 196616 | tf_op jit(solution)/shard_map/ppermute | solution.py:626
  11.8 0.0 collective-permute-start.8
  11.8 0.4 collective-permute-done.low_ref
  12.2 0.0 collective-permute-done.1.high_ref
  12.2 0.7 copy-done.3
  12.9 0.7 copy-done.4
  13.5 2.3 %shard_map.41 = (f32[22,8,512]{2,1,0:T(8,128)}, f32[22,8,512]{2,1,0:T(8,128)}) custom-call(f32[16,16,512]{2,1,0:T(8,128)} %c_ref.5, f32[16,16,512]{2,1,0:T(8,128)} %g_ref.5, f32[5,16,512]{2,1,0:T(8,128)} %copy-done.3, f32[5,16,512]{2,1,0:T(8,128)} %copy-done.4), custom_call_target="tpu_custom_call" | custom-call | flops 1000000 | bytes 1000000 | tf_op jit(solution)/shard_map/pallas_call | solution.py:210
  15.8 2.8 %collective-permute-start.2 = (f32[22,8,512]{2,1,0:T(8,128)}, f32[22,8,512]{2,1,0:T(8,128)S(1)}, u32[]{:S(2)}, u32[]{:S(2)}) collective-permute-start(f32[22,8,512]{2,1,0:T(8,128)} %get-tuple-element.31), channel_id=1, source_target_pairs={{0,1},{1,2},{2,3},{3,4},{4,5},{5,6},{6,7},{7,0},{8,9},{9,10},{10,1... | collective-permute-start | bytes 1081352 | tf_op jit(solution)/shard_map/ppermute | solution.py:621
  18.7 4.6 %collective-permute-done.2.below_ref = f32[22,8,512]{2,1,0:T(8,128)S(1)} collective-permute-done((f32[22,8,512]{2,1,0:T(8,128)}, f32[22,8,512]{2,1,0:T(8,128)S(1)}, u32[]{:S(2)}, u32[]{:S(2)}) %collective-permute-start.2) | collective-permute-done | bytes 360480 | tf_op jit(solution)/shard_map/ppermute | solution.py:621
  23.3 2.4 %collective-permute-done.3.above_ref = f32[22,8,512]{2,1,0:T(8,128)S(1)} collective-permute-done((f32[22,8,512]{2,1,0:T(8,128)}, f32[22,8,512]{2,1,0:T(8,128)S(1)}, u32[]{:S(2)}, u32[]{:S(2)}) %collective-permute-start.3) | collective-permute-done | bytes 360480 | tf_op jit(solution)/shard_map/ppermute | solution.py:626
  25.7 0.7 copy-done.8
  26.4 8.2 %shard_map.42 = (f32[8,8,256]{2,1,0:T(8,128)}, f32[3,16,512]{2,1,0:T(8,128)}, f32[3,16,512]{2,1,0:T(8,128)}, f32[16,16,512]{2,1,0:T(8,128)}, f32[22,24,512]{2,1,...) custom-call(f32[16,16,512]{2,1,0:T(8,128)} %c_ref.5, ...), custom_call_target="tpu_custom_call" | custom-call | flops 1000000 | bytes 1000000 | tf_op jit(solution)/shard_map/pallas_call | solution.py:290
  34.7 0.9 fusion.2
  35.5 0.1 collective-permute-start.4
  35.6 0.0 copy-start.1
  35.6 0.4 collective-permute-start.11
  36.1 1.3 %collective-permute-start.10 = (f32[24,8,256]{2,1,0:T(8,128)S(1)}, f32[24,8,256]{2,1,0:T(8,128)S(1)}, u32[]{:S(2)}, u32[]{:S(2)}) collective-permute-start(f32[24,8,256]{2,1,0:T(8,128)S(1)} %pad_maximum_fusion.mid_ref), channel_id=1, source_target_pairs={{0,1},{1,2},{2,3},{3,4},{4,5},{5,6},{6,7},{7,0},{8,9},{9,10},{10,1... | collective-permute-start | bytes 589832 | tf_op jit(solution)/shard_map/ppermute | solution.py:621
  37.4 4.9 %collective-permute-start.5 = (f32[6,8,256]{2,1,0:T(8,128)S(1)}, f32[6,8,256]{2,1,0:T(8,128)S(1)}, u32[]{:S(2)}, u32[]{:S(2)}) collective-permute-start(f32[6,8,256]{2,1,0:T(8,128)S(1)} %get-tuple-element.65), channel_id=1, source_target_pairs={{8,0},{16,8},{24,16},{32,24},{40,32},{48,40},{56,48},{64,56},{72,6... | collective-permute-start | bytes 147464 | tf_op jit(solution)/shard_map/ppermute | solution.py:626
  42.3 1.2 collective-permute-done.5
  43.5 0.9 pad_maximum_fusion.3.mid_ref
  44.4 1.8 %collective-permute-start.7 = (f32[20,8,256]{2,1,0:T(8,128)S(1)}, f32[20,8,256]{2,1,0:T(8,128)S(1)}, u32[]{:S(2)}, u32[]{:S(2)}) collective-permute-start(f32[20,8,256]{2,1,0:T(8,128)S(1)} %pad_maximum_fusion.3.mid_ref), channel_id=1, source_target_pairs={{1,0},{2,1},{3,2},{4,3},{5,4},{6,5},{7,6},{0,7},{9,8},{10,9},{11,1... | collective-permute-start | bytes 491528 | tf_op jit(solution)/shard_map/ppermute | solution.py:626
  46.2 5.4 %collective-permute-start.17 = (f32[3,16,512]{2,1,0:T(8,128)S(1)}, f32[3,16,512]{2,1,0:T(8,128)S(1)}, u32[]{:S(2)}, u32[]{:S(2)}) collective-permute-start(f32[3,16,512]{2,1,0:T(8,128)S(1)} %copy-done.20), channel_id=1, source_target_pairs={{8,0},{16,8},{24,16},{32,24},{40,32},{48,40},{56,48},{64,56},{72,6... | collective-permute-start | bytes 294920 | tf_op jit(solution)/shard_map/ppermute | solution.py:626
  51.6 0.0 copy-start.12
  51.6 0.7 copy-done.12
  52.3 5.9 %shard_map.44 = (f32[24,24,256]{2,1,0:T(8,128)}, f32[24,24,256]{2,1,0:T(8,128)}, f32[24,24,256]{2,1,0:T(8,128)}, f32[24,24,256]{2,1,0:T(8,128)}, f32[24,24,256]{...) custom-call(f32[24,8,256]{2,1,0:T(8,128)} %copy-done.1, ...), custom_call_target="tpu_custom_call" | custom-call | flops 1000000 | bytes 1000000 | tf_op jit(solution)/shard_map/pallas_call | solution.py:339
  58.2 0.0 copy-start.16
  58.2 0.6 copy-done.15
  58.8 0.1 copy-done.16
  58.9 6.3 %shard_map.45 = (f32[24,24,256]{2,1,0:T(8,128)}, f32[24,24,256]{2,1,0:T(8,128)}, f32[4,8,128]{2,1,0:T(8,128)}, f32[512,128]{1,0:T(8,128)}) custom-call(f32[20,8,256]{2,1,0:T(8,128)} %copy-done.2, f32[20,8,256]{2,1,0:T(8,128)} %copy-done.16, f32[20,8,256]{2,1,0:T(8,128)} %copy-done.15, f32[24,24,256]{2,1,0:T(8,128)} %get-tuple-element.34.wx1, ...), custom_call_target="tpu_custom_call" | custom-call | flops 1000000 | bytes 1000000 | tf_op jit(solution)/shard_map/pallas_call | solution.py:401
  65.2 1.5 %collective-permute-start.13 = (f32[4,8,128]{2,1,0:T(8,128)}, f32[4,8,128]{2,1,0:T(8,128)S(1)}, u32[]{:S(2)}, u32[]{:S(2)}) collective-permute-start(f32[4,8,128]{2,1,0:T(8,128)} %get-tuple-element.46), channel_id=1, source_target_pairs={{8,0},{16,8},{24,16},{32,24},{40,32},{48,40},{56,48},{64,56},{72,6... | collective-permute-start | bytes 49160 | tf_op jit(solution)/shard_map/ppermute | solution.py:626
  66.7 0.6 copy-done.5
  67.3 0.1 copy-done.6
  67.4 1.9 %shard_map.46 = (f32[11,8,512]{2,1,0:T(8,128)}, f32[11,8,512]{2,1,0:T(8,128)}) custom-call(f32[16,16,512]{2,1,0:T(8,128)} %get-tuple-element.49.own_ref.v_own, f32[3,16,512]{2,1,0:T(8,128)} %copy-done.5, f32[3,16,512]{2,1,0:T(8,128)} %copy-done.6), custom_call_target="tpu_custom_call" | custom-call | flops 1000000 | bytes 1000000 | tf_op jit(solution)/shard_map/pallas_call | solution.py:428
  69.3 0.8 collective-permute-start.18
  70.1 1.8 %collective-permute-start.19 = (f32[11,8,512]{2,1,0:T(8,128)}, f32[11,8,512]{2,1,0:T(8,128)S(1)}, u32[]{:S(2)}, u32[]{:S(2)}) collective-permute-start(f32[11,8,512]{2,1,0:T(8,128)} %get-tuple-element.53), channel_id=1, source_target_pairs={{1,0},{2,1},{3,2},{4,3},{5,4},{6,5},{7,6},{0,7},{9,8},{10,9},{11,1... | collective-permute-start | bytes 540680 | tf_op jit(solution)/shard_map/ppermute | solution.py:626
  71.9 9.2 %all-to-all-start = ((f32[128,4,128]{2,1,0:T(4,128)}), f32[128,4,128]{2,1,0:T(4,128)S(1)}, u32[]{:S(2)}, u32[]{:S(2)}) async-start(f32[128,4,128]{2,1,0:T(4,128)} %bitcast.3), calls=%async_computation | async-start | bytes 524288 | tf_op jit(solution)/shard_map/all_to_all | solution.py:661
  81.2 1.1 collective-permute-start.15
  82.2 0.7 collective-permute-start.14
  83.0 2.3 %collective-permute-done.15.above2 = f32[12,8,128]{2,1,0:T(8,128)S(1)} collective-permute-done((f32[12,8,128]{2,1,0:T(8,128)S(1)}, f32[12,8,128]{2,1,0:T(8,128)S(1)}, u32[]{:S(2)}, u32[]{:S(2)}) %collective-permute-start.15) | collective-permute-done | bytes 49184 | tf_op jit(solution)/shard_map/ppermute | solution.py:626
  85.3 0.3 collective-permute-done.14.below2
  85.6 6.4 %all-to-all-done = f32[128,4,128]{2,1,0:T(4,128)S(1)} async-done(((f32[128,4,128]{2,1,0:T(4,128)}), f32[128,4,128]{2,1,0:T(4,128)S(1)}, u32[]{:S(2)}, u32[]{:S(2)}) %all-to-all-start) | async-done | bytes 262176 | tf_op jit(solution)/shard_map/all_to_all | solution.py:661
  92.0 0.7 copy-done
  92.7 29.5 %shard_map.47 = (f32[16,16,512]{2,1,0:T(8,128)}, f32[16,16,512]{2,1,0:T(8,128)}) custom-call(f32[512,128]{1,0:T(8,128)} %bitcast.2, f32[12,8,128]{2,1,0:T(8,128)} %copy-done.10, f32[12,8,128]{2,1,0:T(8,128)} %copy-done.18, f32[12,8,128]{2,1,0:T(8,128)} %copy-done.17, f32[12,16,128]{2,1,0:T(8,128)} %get-tuple-element.39.wx2, ...), custom_call_target="tpu_custom_call" | custom-call | flops 1000000 | bytes 1000000 | tf_op jit(solution)/shard_map/pallas_call | solution.py:607
  (59 shorter events, 0.2 us)
Async XLA Ops:
  2.5 9.7 %collective-permute-start = (f32[5,16,512]{2,1,0:T(8,128)S(1)}, f32[5,16,512]{2,1,0:T(8,128)S(1)}, u32[]{:S(2)}, u32[]{:S(2)}) collective-permute-start(f32[5,16,512]{2,1,0:T(8,128)S(1)} %pad_maximum_fusion.1), channel_id=1, source_target_pairs={{0,8},{8,16},{16,24},{24,32},{32,40},{40,48},{48,56},{56,64},{64,7... | collective-permute-start | bytes 491528 | tf_op jit(solution)/shard_map/ppermute | solution.py:621
  4.6 7.6 %collective-permute-start.1 = (f32[5,16,512]{2,1,0:T(8,128)S(1)}, f32[5,16,512]{2,1,0:T(8,128)S(1)}, u32[]{:S(2)}, u32[]{:S(2)}) collective-permute-start(f32[5,16,512]{2,1,0:T(8,128)S(1)} %pad_maximum_fusion.2), channel_id=1, source_target_pairs={{8,0},{16,8},{24,16},{32,24},{40,32},{48,40},{56,48},{64,56},{72,6... | collective-permute-start | bytes 491528 | tf_op jit(solution)/shard_map/ppermute | solution.py:626
  10.4 8.3 %collective-permute-start.9 = (f32[8,8,256]{2,1,0:T(8,128)}, f32[8,8,256]{2,1,0:T(8,128)S(1)}, u32[]{:S(2)}, u32[]{:S(2)}) collective-permute-start(f32[8,8,256]{2,1,0:T(8,128)} %shard_map.43), channel_id=1, source_target_pairs={{8,0},{16,8},{24,16},{32,24},{40,32},{48,40},{56,48},{64,56},{72,6... | collective-permute-start | bytes 196616 | tf_op jit(solution)/shard_map/ppermute | solution.py:626
  11.8 6.8 %collective-permute-start.8 = (f32[8,8,256]{2,1,0:T(8,128)}, f32[8,8,256]{2,1,0:T(8,128)S(1)}, u32[]{:S(2)}, u32[]{:S(2)}) collective-permute-start(f32[8,8,256]{2,1,0:T(8,128)} %shard_map.43), channel_id=1, source_target_pairs={{0,8},{8,16},{16,24},{24,32},{32,40},{40,48},{48,56},{56,64},{64,7... | collective-permute-start | bytes 196616 | tf_op jit(solution)/shard_map/ppermute | solution.py:621
  12.2 0.7 copy-start.3
  12.9 0.7 copy-start.4
  15.8 7.5 %collective-permute-start.2 = (f32[22,8,512]{2,1,0:T(8,128)}, f32[22,8,512]{2,1,0:T(8,128)S(1)}, u32[]{:S(2)}, u32[]{:S(2)}) collective-permute-start(f32[22,8,512]{2,1,0:T(8,128)} %get-tuple-element.31), channel_id=1, source_target_pairs={{0,1},{1,2},{2,3},{3,4},{4,5},{5,6},{6,7},{7,0},{8,9},{9,10},{10,1... | collective-permute-start | bytes 1081352 | tf_op jit(solution)/shard_map/ppermute | solution.py:621
  18.6 7.1 %collective-permute-start.3 = (f32[22,8,512]{2,1,0:T(8,128)}, f32[22,8,512]{2,1,0:T(8,128)S(1)}, u32[]{:S(2)}, u32[]{:S(2)}) collective-permute-start(f32[22,8,512]{2,1,0:T(8,128)} %get-tuple-element.32), channel_id=1, source_target_pairs={{1,0},{2,1},{3,2},{4,3},{5,4},{6,5},{7,6},{0,7},{9,8},{10,9},{11,1... | collective-permute-start | bytes 1081352 | tf_op jit(solution)/shard_map/ppermute | solution.py:626
  18.7 16.9 %copy-start.9 = (f32[8,8,256]{2,1,0:T(8,128)S(1)}, f32[8,8,256]{2,1,0:T(8,128)}, u32[]{:S(2)}) copy-start(f32[8,8,256]{2,1,0:T(8,128)} %shard_map.43) | copy-start | bytes 196612
  23.3 2.4 %copy-start.7 = (f32[22,8,512]{2,1,0:T(8,128)}, f32[22,8,512]{2,1,0:T(8,128)S(1)}, u32[]{:S(2)}) copy-start(f32[22,8,512]{2,1,0:T(8,128)S(1)} %collective-permute-done.2.below_ref) | copy-start | bytes 1081348
  25.7 0.7 copy-start.8
  34.6 11.5 %copy-start.21 = (f32[3,16,512]{2,1,0:T(8,128)S(1)}, f32[3,16,512]{2,1,0:T(8,128)}, u32[]{:S(2)}) copy-start(f32[3,16,512]{2,1,0:T(8,128)} %get-tuple-element.50) | copy-start | bytes 294916
  34.6 11.5 %copy-start.20 = (f32[3,16,512]{2,1,0:T(8,128)S(1)}, f32[3,16,512]{2,1,0:T(8,128)}, u32[]{:S(2)}) copy-start(f32[3,16,512]{2,1,0:T(8,128)} %get-tuple-element.51) | copy-start | bytes 294916
  35.5 6.8 %collective-permute-start.4 = (f32[6,8,256]{2,1,0:T(8,128)S(1)}, f32[6,8,256]{2,1,0:T(8,128)S(1)}, u32[]{:S(2)}, u32[]{:S(2)}) collective-permute-start(f32[6,8,256]{2,1,0:T(8,128)S(1)} %get-tuple-element.64), channel_id=1, source_target_pairs={{0,8},{8,16},{16,24},{24,32},{32,40},{40,48},{48,56},{56,64},{64,7... | collective-permute-start | bytes 147464 | tf_op jit(solution)/shard_map/ppermute | solution.py:621
  35.6 16.0 %copy-start.1 = (f32[24,8,256]{2,1,0:T(8,128)}, f32[24,8,256]{2,1,0:T(8,128)S(1)}, u32[]{:S(2)}) copy-start(f32[24,8,256]{2,1,0:T(8,128)S(1)} %pad_maximum_fusion.mid_ref) | copy-start | bytes 589828
  35.6 10.5 %collective-permute-start.11 = (f32[24,8,256]{2,1,0:T(8,128)S(1)}, f32[24,8,256]{2,1,0:T(8,128)S(1)}, u32[]{:S(2)}, u32[]{:S(2)}) collective-permute-start(f32[24,8,256]{2,1,0:T(8,128)S(1)} %pad_maximum_fusion.mid_ref), channel_id=1, source_target_pairs={{1,0},{2,1},{3,2},{4,3},{5,4},{6,5},{7,6},{0,7},{9,8},{10,9},{11,1... | collective-permute-start | bytes 589832 | tf_op jit(solution)/shard_map/ppermute | solution.py:626
  36.1 15.5 %collective-permute-start.10 = (f32[24,8,256]{2,1,0:T(8,128)S(1)}, f32[24,8,256]{2,1,0:T(8,128)S(1)}, u32[]{:S(2)}, u32[]{:S(2)}) collective-permute-start(f32[24,8,256]{2,1,0:T(8,128)S(1)} %pad_maximum_fusion.mid_ref), channel_id=1, source_target_pairs={{0,1},{1,2},{2,3},{3,4},{4,5},{5,6},{6,7},{7,0},{8,9},{9,10},{10,1... | collective-permute-start | bytes 589832 | tf_op jit(solution)/shard_map/ppermute | solution.py:621
  37.4 6.1 %collective-permute-start.5 = (f32[6,8,256]{2,1,0:T(8,128)S(1)}, f32[6,8,256]{2,1,0:T(8,128)S(1)}, u32[]{:S(2)}, u32[]{:S(2)}) collective-permute-start(f32[6,8,256]{2,1,0:T(8,128)S(1)} %get-tuple-element.65), channel_id=1, source_target_pairs={{8,0},{16,8},{24,16},{32,24},{40,32},{48,40},{56,48},{64,56},{72,6... | collective-permute-start | bytes 147464 | tf_op jit(solution)/shard_map/ppermute | solution.py:626
  44.4 13.8 %copy-start.2 = (f32[20,8,256]{2,1,0:T(8,128)}, f32[20,8,256]{2,1,0:T(8,128)S(1)}, u32[]{:S(2)}) copy-start(f32[20,8,256]{2,1,0:T(8,128)S(1)} %pad_maximum_fusion.3.mid_ref) | copy-start | bytes 491524
  44.4 13.8 %collective-permute-start.7 = (f32[20,8,256]{2,1,0:T(8,128)S(1)}, f32[20,8,256]{2,1,0:T(8,128)S(1)}, u32[]{:S(2)}, u32[]{:S(2)}) collective-permute-start(f32[20,8,256]{2,1,0:T(8,128)S(1)} %pad_maximum_fusion.3.mid_ref), channel_id=1, source_target_pairs={{1,0},{2,1},{3,2},{4,3},{5,4},{6,5},{7,6},{0,7},{9,8},{10,9},{11,1... | collective-permute-start | bytes 491528 | tf_op jit(solution)/shard_map/ppermute | solution.py:626
  46.1 12.0 %collective-permute-start.6 = (f32[20,8,256]{2,1,0:T(8,128)S(1)}, f32[20,8,256]{2,1,0:T(8,128)S(1)}, u32[]{:S(2)}, u32[]{:S(2)}) collective-permute-start(f32[20,8,256]{2,1,0:T(8,128)S(1)} %pad_maximum_fusion.3.mid_ref), channel_id=1, source_target_pairs={{0,1},{1,2},{2,3},{3,4},{4,5},{5,6},{6,7},{7,0},{8,9},{9,10},{10,1... | collective-permute-start | bytes 491528 | tf_op jit(solution)/shard_map/ppermute | solution.py:621
  46.1 20.6 %collective-permute-start.16 = (f32[3,16,512]{2,1,0:T(8,128)S(1)}, f32[3,16,512]{2,1,0:T(8,128)S(1)}, u32[]{:S(2)}, u32[]{:S(2)}) collective-permute-start(f32[3,16,512]{2,1,0:T(8,128)S(1)} %copy-done.21), channel_id=1, source_target_pairs={{0,8},{8,16},{16,24},{24,32},{32,40},{40,48},{48,56},{56,64},{64,7... | collective-permute-start | bytes 294920 | tf_op jit(solution)/shard_map/ppermute | solution.py:621
  46.2 5.5 %copy-start.11 = (f32[24,8,256]{2,1,0:T(8,128)}, f32[24,8,256]{2,1,0:T(8,128)S(1)}, u32[]{:S(2)}) copy-start(f32[24,8,256]{2,1,0:T(8,128)S(1)} %collective-permute-done.11.above_ref) | copy-start | bytes 589828
  46.2 20.5 %collective-permute-start.17 = (f32[3,16,512]{2,1,0:T(8,128)S(1)}, f32[3,16,512]{2,1,0:T(8,128)S(1)}, u32[]{:S(2)}, u32[]{:S(2)}) collective-permute-start(f32[3,16,512]{2,1,0:T(8,128)S(1)} %copy-done.20), channel_id=1, source_target_pairs={{8,0},{16,8},{24,16},{32,24},{40,32},{48,40},{56,48},{64,56},{72,6... | collective-permute-start | bytes 294920 | tf_op jit(solution)/shard_map/ppermute | solution.py:626
  51.6 0.7 copy-start.12
  58.2 0.7 copy-start.15
  58.2 0.7 copy-start.16
  65.2 15.9 %copy-start.19 = (f32[4,8,128]{2,1,0:T(8,128)S(1)}, f32[4,8,128]{2,1,0:T(8,128)}, u32[]{:S(2)}) copy-start(f32[4,8,128]{2,1,0:T(8,128)} %get-tuple-element.46) | copy-start | bytes 49156
  65.2 15.9 %collective-permute-start.13 = (f32[4,8,128]{2,1,0:T(8,128)}, f32[4,8,128]{2,1,0:T(8,128)S(1)}, u32[]{:S(2)}, u32[]{:S(2)}) collective-permute-start(f32[4,8,128]{2,1,0:T(8,128)} %get-tuple-element.46), channel_id=1, source_target_pairs={{8,0},{16,8},{24,16},{32,24},{40,32},{48,40},{56,48},{64,56},{72,6... | collective-permute-start | bytes 49160 | tf_op jit(solution)/shard_map/ppermute | solution.py:626
  66.7 0.6 copy-start.5
  66.7 0.7 copy-start.6
  69.3 13.7 %collective-permute-start.18 = (f32[11,8,512]{2,1,0:T(8,128)}, f32[11,8,512]{2,1,0:T(8,128)S(1)}, u32[]{:S(2)}, u32[]{:S(2)}) collective-permute-start(f32[11,8,512]{2,1,0:T(8,128)} %get-tuple-element.52), channel_id=1, source_target_pairs={{0,1},{1,2},{2,3},{3,4},{4,5},{5,6},{6,7},{7,0},{8,9},{9,10},{10,1... | collective-permute-start | bytes 540680 | tf_op jit(solution)/shard_map/ppermute | solution.py:621
  70.1 12.9 %collective-permute-start.19 = (f32[11,8,512]{2,1,0:T(8,128)}, f32[11,8,512]{2,1,0:T(8,128)S(1)}, u32[]{:S(2)}, u32[]{:S(2)}) collective-permute-start(f32[11,8,512]{2,1,0:T(8,128)} %get-tuple-element.53), channel_id=1, source_target_pairs={{1,0},{2,1},{3,2},{4,3},{5,4},{6,5},{7,6},{0,7},{9,8},{10,9},{11,1... | collective-permute-start | bytes 540680 | tf_op jit(solution)/shard_map/ppermute | solution.py:626
  71.9 9.2 %collective-permute-start.12 = (f32[4,8,128]{2,1,0:T(8,128)}, f32[4,8,128]{2,1,0:T(8,128)S(1)}, u32[]{:S(2)}, u32[]{:S(2)}) collective-permute-start(f32[4,8,128]{2,1,0:T(8,128)} %get-tuple-element.46), channel_id=1, source_target_pairs={{0,8},{8,16},{16,24},{24,32},{32,40},{40,48},{48,56},{56,64},{64,7... | collective-permute-start | bytes 49160 | tf_op jit(solution)/shard_map/ppermute | solution.py:621
  71.9 20.1 %all-to-all-start = ((f32[128,4,128]{2,1,0:T(4,128)}), f32[128,4,128]{2,1,0:T(4,128)S(1)}, u32[]{:S(2)}, u32[]{:S(2)}) async-start(f32[128,4,128]{2,1,0:T(4,128)} %bitcast.3), calls=%async_computation | async-start | bytes 524288 | tf_op jit(solution)/shard_map/all_to_all | solution.py:661
  81.2 10.8 %copy-start.10 = (f32[12,8,128]{2,1,0:T(8,128)}, f32[12,8,128]{2,1,0:T(8,128)S(1)}, u32[]{:S(2)}) copy-start(f32[12,8,128]{2,1,0:T(8,128)S(1)} %pad_maximum_fusion.4.mid2) | copy-start | bytes 147460
  81.2 4.1 %collective-permute-start.15 = (f32[12,8,128]{2,1,0:T(8,128)S(1)}, f32[12,8,128]{2,1,0:T(8,128)S(1)}, u32[]{:S(2)}, u32[]{:S(2)}) collective-permute-start(f32[12,8,128]{2,1,0:T(8,128)S(1)} %pad_maximum_fusion.4.mid2), channel_id=1, source_target_pairs={{1,0},{2,1},{3,2},{4,3},{5,4},{6,5},{7,6},{0,7},{9,8},{10,9},{11,1... | collective-permute-start | bytes 147464 | tf_op jit(solution)/shard_map/ppermute | solution.py:626
  82.2 3.3 %collective-permute-start.14 = (f32[12,8,128]{2,1,0:T(8,128)S(1)}, f32[12,8,128]{2,1,0:T(8,128)S(1)}, u32[]{:S(2)}, u32[]{:S(2)}) collective-permute-start(f32[12,8,128]{2,1,0:T(8,128)S(1)} %pad_maximum_fusion.4.mid2), channel_id=1, source_target_pairs={{0,1},{1,2},{2,3},{3,4},{4,5},{5,6},{6,7},{7,0},{8,9},{9,10},{10,1... | collective-permute-start | bytes 147464 | tf_op jit(solution)/shard_map/ppermute | solution.py:621
  83.0 9.0 %copy-start.13 = (f32[11,8,512]{2,1,0:T(8,128)}, f32[11,8,512]{2,1,0:T(8,128)S(1)}, u32[]{:S(2)}) copy-start(f32[11,8,512]{2,1,0:T(8,128)S(1)} %collective-permute-done.18.v_below) | copy-start | bytes 540676
  83.0 9.0 %copy-start.14 = (f32[11,8,512]{2,1,0:T(8,128)}, f32[11,8,512]{2,1,0:T(8,128)S(1)}, u32[]{:S(2)}) copy-start(f32[11,8,512]{2,1,0:T(8,128)S(1)} %collective-permute-done.19.v_above) | copy-start | bytes 540676
  85.3 6.7 %copy-start.17 = (f32[12,8,128]{2,1,0:T(8,128)}, f32[12,8,128]{2,1,0:T(8,128)S(1)}, u32[]{:S(2)}) copy-start(f32[12,8,128]{2,1,0:T(8,128)S(1)} %collective-permute-done.15.above2) | copy-start | bytes 147460
  85.6 6.4 %copy-start.18 = (f32[12,8,128]{2,1,0:T(8,128)}, f32[12,8,128]{2,1,0:T(8,128)S(1)}, u32[]{:S(2)}) copy-start(f32[12,8,128]{2,1,0:T(8,128)S(1)} %collective-permute-done.14.below2) | copy-start | bytes 147460
  92.0 0.7 copy-start

commit v2 on v1

v2 whole, which is shorter than its diff:
```python
import functools

import jax
import jax.numpy as jnp
from jax import lax
from jax.experimental import pallas as pl
from jax.experimental.pallas import tpu as pltpu
from jax.sharding import PartitionSpec as P

F32 = jnp.float32
BF16 = jnp.bfloat16
OMEGA = 0.8
BOTTOM = 16
MIB = 1024 * 1024

X0, Y0, Z0, OX0, OY0 = 22, 24, 512, 3, 4
X1, Y1, Z1, OX1, OY1 = 24, 24, 256, 8, 8
X2, Y2, Z2, OX2, OY2 = 12, 16, 128, 4, 4
Y3, Y4, LANES = 16, 8, 128


def iota(shape, dim):
    return lax.broadcasted_iota(jnp.int32, shape, dim)


def up_of(cells, dim):
    return pltpu.roll(cells, cells.shape[dim] - 1, dim)


def down_of(cells, dim):
    return pltpu.roll(cells, 1, dim)


def split_dot(cells, pick):
    high = cells.astype(BF16)
    rest = cells - high.astype(F32)
    mid = rest.astype(BF16)
    low = (rest - mid.astype(F32)).astype(BF16)
    dot = functools.partial(jnp.dot, preferred_element_type=F32)
    return dot(high, pick) + (dot(mid, pick) + dot(low, pick))


def split_dot_left(pick, cells):
    high = cells.astype(BF16)
    rest = cells - high.astype(F32)
    mid = rest.astype(BF16)
    low = (rest - mid.astype(F32)).astype(BF16)
    dot = functools.partial(jnp.dot, preferred_element_type=F32)
    return dot(pick, high) + (dot(pick, mid) + dot(pick, low))


def pair_sum_matrix(fine, coarse, offset=0):
    hit = (iota((fine, coarse), 0) // 2) + offset == iota((fine, coarse), 1)
    return hit.astype(F32).astype(BF16)


def copy_matrix(coarse, fine):
    hit = iota((coarse, fine), 0) == iota((coarse, fine), 1) // 2
    return hit.astype(F32).astype(BF16)


def inside(shape, dim, start, count):
    place = iota(shape, dim) + start
    return jnp.logical_and(place >= 0, place < count)


def flag(start, count):
    return jnp.where(jnp.logical_and(start >= 0, start < count), 1.0, 0.0).astype(F32)


def loop(first, last, body, width=1):
    def run(i, count):
        stores = [store for j in range(count) for store in body(i + j)]
        for ref, at, value in stores:
            ref[at] = value

    count = (last - first) // width

    def step(t, carry):
        run(first + t * width, width)
        return carry

    if count == 1:
        run(first, width)
    else:
        lax.fori_loop(0, count, step, 0)
    if (last - first) % width:
        run(first + count * width, (last - first) % width)


def make_faces(c, wx, wy, wz, d, q, first, last, in_x, in_y, width, whole_y=0):
    rows, cells = c.shape[1], c.shape[2]
    end_z = iota((rows, cells), 1) == cells - 1
    start_z = iota((rows, cells), 1) == 0
    row = iota((rows, cells), 0)
    wx[first - 1] = 0.5 * (c[first - 1] + c[first])

    def body(i):
        here = c[i]
        after = c[i + 1]
        before = c[i - 1]
        y_up, y_down = up_of(here, 0), down_of(here, 0)
        if whole_y:
            y_up = jnp.where(row == rows - 1, 0.0, y_up)
            y_down = jnp.where(row == 0, 0.0, y_down)
        z_up = jnp.where(end_z, 0.0, up_of(here, 1))
        z_down = jnp.where(start_z, 0.0, down_of(here, 1))
        side = 0.5 * (here + y_up)
        side = jnp.where(row == rows - 1, 0.0, side) if whole_y else side
        total = 3.0 * here + 0.5 * ((after + before) + (y_up + y_down) + (z_up + z_down))
        return [
            (wx, i, 0.5 * (here + after)),
            (wy, i, side),
            (wz, i, jnp.where(end_z, 0.0, 0.5 * (here + z_up))),
            (d, i, total),
            (q, i, (in_y * (OMEGA * in_x(i))) / jnp.maximum(total, 1e-30)),
        ]

    loop(first, last, body, width)


def neighbours(v, wx, wy, wz, i):
    here = v[i]
    side_y, side_z = wy[i], wz[i]
    along_x = wx[i] * v[i + 1] + wx[i - 1] * v[i - 1]
    along_y = side_y * up_of(here, 0) + down_of(side_y * here, 0)
    along_z = side_z * up_of(here, 1) + down_of(side_z * here, 1)
    return here, along_x + along_y + along_z


def sweep(v, out, b, wx, wy, wz, q, first, last, width):
    def body(i):
        here, total = neighbours(v, wx, wy, wz, i)
        return [(out, i, (0.2 * here + b[i]) + q[i] * total)]

    loop(first, last, body, width)


def defect(v, source, wx, wy, wz, d, i):
    here, total = neighbours(v, wx, wy, wz, i)
    return (source[i] - d[i] * here) + total


def lanes(cells, k):
    return cells[:, LANES * k : LANES * k + LANES]


def keep(scratch, j, cells):
    for k in range(cells.shape[1] // LANES):
        scratch[j, k] = lanes(cells, k)


def halve_rows(scratch, j, start, count):
    parts = [
        scratch[j, k, pl.ds(start, count, stride=2), :] + scratch[j, k, pl.ds(start + 1, count, stride=2), :]
        for k in range(scratch.shape[1])
    ]
    return jnp.concatenate(parts, axis=1)


def double_rows(scratch, cells, start):
    for k in range(scratch.shape[0]):
        for odd in range(2):
            scratch[k, pl.ds(start + odd, cells.shape[0], stride=2), :] = lanes(cells, k)
    return jnp.concatenate([scratch[k] for k in range(scratch.shape[0])], axis=1)


def call(kernel, out_shape, scratch, limit, in_specs=None, out_specs=None, flops=1000000, bytes_accessed=1000000):
    extra = {}
    if in_specs is not None:
        extra["in_specs"] = in_specs
    if out_specs is not None:
        extra["out_specs"] = out_specs
    return pl.pallas_call(
        kernel,
        out_shape=out_shape,
        scratch_shapes=scratch,
        compiler_params=pltpu.CompilerParams(vmem_limit_bytes=limit * MIB),
        cost_estimate=pl.CostEstimate(flops=flops, bytes_accessed=bytes_accessed, transcendentals=0),
        **extra,
    )


def struct(*shape):
    return jax.ShapeDtypeStruct(shape, F32)


def vmem(*shape):
    return pltpu.VMEM(shape, F32)


def place_of(i):
    row, cell = 8 * ((i // 2) % 2), Z1 * (i % 2)
    return 5 + i // 4, slice(row, row + 8), slice(cell, cell + Z1)


def begin_kernel(c_ref, g_ref, next_ref, previous_ref, c1_ref, pairs):
    for i in range(8):
        keep(pairs, i, c_ref[2 * i] + c_ref[2 * i + 1])
    for i in range(3):
        next_ref[i] = c_ref[13 + i]
        previous_ref[i] = c_ref[i]
    for i in range(2):
        next_ref[3 + i] = g_ref[14 + i]
        previous_ref[3 + i] = g_ref[i]
    rows = jnp.concatenate([halve_rows(pairs, i, 0, 8) for i in range(8)], axis=0)
    small = 0.125 * split_dot(rows, pair_sum_matrix(Z0, Z1))
    for i in range(8):
        block = small[8 * i : 8 * i + 8]
        c1_ref[i] = block
        next_ref[place_of(i)] = block
        previous_ref[place_of(i)] = block


def begin(coefficient, right_side):
    return call(
        begin_kernel, [struct(7, 16, Z0), struct(7, 16, Z0), struct(8, 8, Z1)], [vmem(8, Z0 // LANES, 16, LANES)], 60
    )(coefficient, right_side)


def edge_kernel(count_x, c_ref, g_ref, c1_ref, low_ref, high_ref, top_ref, bottom_ref):
    place = lax.axis_index("gx")
    first = jnp.where(place > 0, 1.0, 0.0).astype(F32)
    last = jnp.where(place < count_x - 1, 1.0, 0.0).astype(F32)
    row = iota((8, Z0), 0)

    def put(i, c, g):
        return [
            (top_ref, i, jnp.where(row < 4, pltpu.roll(c[8:16], 4, 0), g[8:16])),
            (bottom_ref, i, jnp.where(row < 4, g[0:8], pltpu.roll(c[0:8], 4, 0))),
        ]

    def put_now(*what):
        for ref, at, value in put(*what):
            ref[at] = value

    nothing = jnp.zeros((16, Z0), F32)
    for i in range(3):
        put_now(i, low_ref[i] * first, low_ref[i + 2] * first if i > 0 else nothing)
        put_now(19 + i, high_ref[i] * last, high_ref[i + 3] * last if i < 2 else nothing)

    def body(i):
        return put(i + 3, c_ref[i], g_ref[i])

    loop(0, 16, body, 2)
    for i in range(24):
        part = low_ref[place_of(i)] * first if i < 8 else c1_ref[i - 8] if i < 16 else high_ref[place_of(i - 16)] * last
        for ref in (top_ref, bottom_ref):
            ref[X0 + i // 2, :, Z1 * (i % 2) : Z1 * (i % 2) + Z1] = part


def edges_y(count_x, *operands):
    return call(
        functools.partial(edge_kernel, count_x), [struct(X0 + 12, 8, Z0), struct(X0 + 12, 8, Z0)], [], 8
    )(*operands)


def ends(axis, count):
    place = lax.axis_index(axis)
    low = jnp.where(place > 0, 1.0, 0.0).astype(F32)
    return low, jnp.where(place < count - 1, 1.0, 0.0).astype(F32)


def window0(low_ref, high_ref, below_ref, above_ref, c_ref, g_ref, first, last, low_y, high_y):
    row = iota((8, Z0), 0) < 4
    nothing = jnp.zeros((16, Z0), F32)

    def put(own, below, above):
        head, tail = pltpu.roll(own[0:8], 4, 0), pltpu.roll(own[8:16], 4, 0)
        parts = [jnp.where(row, below, head), jnp.where(row, head, tail), jnp.where(row, tail, above)]
        return jnp.concatenate(parts, axis=0)

    def c_slab(i, own):
        return put(own, below_ref[i] * low_y, above_ref[i] * high_y)

    def g_slab(i, own):
        return put(own, pltpu.roll(below_ref[i], 4, 0) * low_y, pltpu.roll(above_ref[i], 4, 0) * high_y)

    def fill(c, g):
        for i in range(3):
            c[i] = c_slab(i, low_ref[i] * first)
            c[19 + i] = c_slab(19 + i, high_ref[i] * last)
            g[i] = g_slab(i, low_ref[i + 2] * first if i > 0 else nothing)
            g[19 + i] = g_slab(19 + i, high_ref[i + 3] * last if i < 2 else nothing)

        def body(i):
            return [(c, i + 3, c_slab(i + 3, c_ref[i])), (g, i + 3, g_slab(i + 3, g_ref[i]))]

        loop(0, 16, body)

    return fill


def down0_kernel(
    count_x, count_y,
    c_ref, g_ref, low_ref, high_ref, below_ref, above_ref,
    g1_ref, v_own_ref, c, g, wx, wy, wz, d, q, b, v, pairs,
):
    place_x, place_y = lax.axis_index("gx"), lax.axis_index("gy")
    sides = ends("gx", count_x) + ends("gy", count_y)
    window0(low_ref, high_ref, below_ref, above_ref, c_ref, g_ref, *sides)(c, g)
    in_y = inside((Y0, Z0), 0, place_y * 16 - OY0, 16 * count_y).astype(F32)
    make_faces(
        c, wx, wy, wz, d, q, 1, X0 - 1, lambda i: flag(place_x * 16 - OX0 + i, 16 * count_x), in_y, 1
    )

    def begin(i):
        return [(b, i, q[i] * g[i])]

    loop(1, X0 - 1, begin, 2)
    sweep(b, v, b, wx, wy, wz, q, 2, X0 - 2, 2)

    def own_of(i):
        return [(v_own_ref, i, pltpu.roll(v[i + 3], Y0 - OY0, 0)[0:16])]

    loop(0, 16, own_of, 2)

    def restrict(j):
        i = 2 * j + OX0
        both = defect(v, g, wx, wy, wz, d, i) + defect(v, g, wx, wy, wz, d, i + 1)
        return [(pairs, (j, k), lanes(both, k)) for k in range(Z0 // LANES)]

    loop(0, 8, restrict)
    rows = jnp.concatenate([halve_rows(pairs, i, 4, 8) for i in range(8)], axis=0)
    g1_ref[...] = (0.5 * split_dot(rows, pair_sum_matrix(Z0, Z1))).reshape(8, 8, Z1)


def down0(count_x, count_y, *operands):
    frame = (X0, Y0, Z0)
    return call(
        functools.partial(down0_kernel, count_x, count_y),
        [struct(8, 8, Z1), struct(16, 16, Z0)],
        [vmem(*frame)] * 9 + [vmem(8, Z0 // LANES, Y0, LANES)],
        18,
    )(*operands)


def fill_c1(c1, c1_ref, low_ref, high_ref, below_ref, above_ref, first, last, low_y, high_y):
    for i in range(24):
        at = X0 + i // 2, slice(0, 8), slice(Z1 * (i % 2), Z1 * (i % 2) + Z1)
        part = low_ref[place_of(i)] * first if i < 8 else c1_ref[i - 8] if i < 16 else high_ref[place_of(i - 16)] * last
        c1[i, 0:8, :] = below_ref[at] * low_y
        c1[i, 8:16, :] = part
        c1[i, 16:24, :] = above_ref[at] * high_y


def prepare_kernel(
    count_x, count_y, c1_ref, low_ref, high_ref, below_ref, above_ref,
    wx1, wy1, wz1, d1, q1, wx2, wy2, wz2, d2, q2, c3_ref, c1, c2, pairs,
):
    place_x, place_y = lax.axis_index("gx"), lax.axis_index("gy")
    sides = ends("gx", count_x) + ends("gy", count_y)
    fill_c1(c1, c1_ref, low_ref, high_ref, below_ref, above_ref, *sides)
    in_y = inside((Y1, Z1), 0, place_y * 8 - OY1, 8 * count_y).astype(F32)
    make_faces(
        c1, wx1, wy1, wz1, d1, q1, 2, X1 - 2, lambda i: flag(place_x * 8 - OX1 + i, 8 * count_x), in_y, 2
    )
    for i in range(12):
        keep(pairs, i, c1[2 * i] + c1[2 * i + 1])
    blank = jnp.zeros((4, Z1), F32)
    rows = []
    for i in range(12):
        rows.append(halve_rows(pairs, i, 0, 12))
        rows.append(blank)
    c2[...] = (0.125 * split_dot(jnp.concatenate(rows, axis=0), pair_sum_matrix(Z1, Z2))).reshape(X2, Y2, Z2)
    in_y = inside((Y2, Z2), 0, place_y * 4 - OY2, 4 * count_y).astype(F32)
    make_faces(
        c2, wx2, wy2, wz2, d2, q2, 1, X2 - 1, lambda i: flag(place_x * 4 - OX2 + i, 4 * count_x), in_y, 10
    )
    rows = jnp.concatenate([c2[4] + c2[5], c2[6] + c2[7]], axis=0)
    thin = 0.125 * split_dot(rows, pair_sum_matrix(Z2, LANES, 64))
    row = iota((8, LANES), 0)
    c3 = jnp.zeros((8, LANES), F32)
    for i in range(2):
        for j in range(2):
            at = 16 * i + 4 + 2 * j
            both = thin[at : at + 1] + thin[at + 1 : at + 2]
            c3 = jnp.where(row == 2 * i + j, jnp.broadcast_to(both, (8, LANES)), c3)
    c3_ref[...] = c3


def prepare(count_x, count_y, *operands):
    frame1, frame2 = (X1, Y1, Z1), (X2, Y2, Z2)
    return call(
        functools.partial(prepare_kernel, count_x, count_y),
        [struct(*frame1)] * 5 + [struct(*frame2)] * 5 + [struct(8, LANES)],
        [vmem(*frame1), vmem(*frame2), vmem(12, Z1 // LANES, Y1, LANES)],
        8,
    )(*operands)


def fill_g1(g1, mid_ref, below_ref, above_ref, low_y, high_y):
    g1[2:22, 0:8, :] = below_ref[...] * low_y
    g1[2:22, 8:16, :] = mid_ref[...]
    g1[2:22, 16:24, :] = above_ref[...] * high_y


def down1_kernel(
    count_x, count_y, v_own_ref, mid_ref, below_ref, above_ref,
    wx1, wy1, wz1, d1, q1, wx2, wy2, wz2, d2, q2, c3_ref,
    v_far, next_ref, previous_ref, send2_ref, send3_ref, v1_ref, b1_ref, g1, g2, b2, v2, pairs, thin,
):
    place_y = lax.axis_index("gy")
    low_y = jnp.where(place_y > 0, 1.0, 0.0).astype(F32)
    high_y = jnp.where(place_y < count_y - 1, 1.0, 0.0).astype(F32)
    fill_g1(g1, mid_ref, below_ref, above_ref, low_y, high_y)

    def begin1(i):
        return [(b1_ref, i, q1[i] * g1[i])]

    loop(2, X1 - 2, begin1, 4)
    sweep(b1_ref, v1_ref, b1_ref, wx1, wy1, wz1, q1, 3, X1 - 3, 3)

    def restrict(j):
        i = 2 * j + 4
        after = defect(v1_ref, g1, wx1, wy1, wz1, d1, i + 1)
        both = defect(v1_ref, g1, wx1, wy1, wz1, d1, i) + after
        return [(pairs, (j, k), lanes(both, k)) for k in range(Z1 // LANES)]

    loop(0, 8, restrict, 2)
    rows = jnp.concatenate([halve_rows(pairs, i, 4, 8) for i in range(8)], axis=0)
    small = 0.5 * split_dot(rows, pair_sum_matrix(Z1, Z2))
    g2[...] = jnp.zeros((X2, Y2, Z2), F32)
    for i in range(8):
        g2[2 + i, 2:10, :] = small[8 * i : 8 * i + 8]
    for i in range(2, X2 - 2):
        b2[i] = q2[i] * g2[i]
    sweep(b2, v2, b2, wx2, wy2, wz2, q2, 3, X2 - 3, 6)
    row = iota((8, Z2), 0) < 4
    for i in range(4):
        both = jnp.where(row, pltpu.roll(v2[4 + i, 0:8, :], 4, 0), g2[4 + i, 0:8, :])
        send2_ref[:, LANES * i : LANES * i + LANES] = both
        next_ref[6, :, LANES * i : LANES * i + LANES] = both
        previous_ref[6, :, LANES * i : LANES * i + LANES] = both
    for i in range(3):
        for half in range(2):
            next_ref[2 * i + half] = v_own_ref[13 + i, 8 * half : 8 * half + 8, :]
            previous_ref[2 * i + half] = v_own_ref[i, 8 * half : 8 * half + 8, :]
    halves = [
        defect(v2, g2, wx2, wy2, wz2, d2, 4 + 2 * i) + defect(v2, g2, wx2, wy2, wz2, d2, 5 + 2 * i)
        for i in range(2)
    ]
    thin[...] = 0.5 * split_dot(jnp.concatenate(halves, axis=0), pair_sum_matrix(Z2, LANES))
    row = iota((8, LANES), 0)
    source = jnp.zeros((8, LANES), F32)
    for i in range(2):
        for j in range(2):
            at = 16 * i + 4 + 2 * j
            both = thin[at : at + 1, :] + thin[at + 1 : at + 2, :]
            source = jnp.where(row == 2 * i + j, jnp.broadcast_to(both, (8, LANES)), source)
    source = source + c3_ref[...]
    double = jnp.where(row < 4, source, pltpu.roll(source, 4, 0))
    for i in range(count_x * count_y // 2):
        send3_ref[8 * i : 8 * i + 8, :] = double
    v_far[...] = v1_ref[4:20]


def down1(count_x, count_y, *operands):
    frame1, frame2 = (X1, Y1, Z1), (X2, Y2, Z2)
    return call(
        functools.partial(down1_kernel, count_x, count_y),
        [struct(16, Y1, Z1), struct(7, 8, Z0), struct(7, 8, Z0), struct(8, Z0)]
        + [struct(4 * count_x * count_y, LANES)],
        [vmem(*frame1)] * 3 + [vmem(*frame2)] * 3 + [vmem(8, Z1 // LANES, Y1, LANES), vmem(32, LANES)],
        8,
    )(*operands)


def iterate_edge_kernel(count_x, own_ref, own2_ref, low_ref, high_ref, top_ref, bottom_ref):
    place = lax.axis_index("gx")
    first = jnp.where(place > 0, 1.0, 0.0).astype(F32)
    last = jnp.where(place < count_x - 1, 1.0, 0.0).astype(F32)
    row = iota((8, Z0), 0) < 4

    def slab(i, half):
        if i < 3:
            return low_ref[2 * i + half] * first
        if i < 19:
            return own_ref[i - 3, 8 * half : 8 * half + 8, :]
        return high_ref[2 * (i - 19) + half] * last

    for j in range(X0 // 2):
        top_ref[j] = jnp.where(row, pltpu.roll(slab(2 * j, 1), 4, 0), slab(2 * j + 1, 1))
        bottom_ref[j] = jnp.where(row, slab(2 * j, 0), pltpu.roll(slab(2 * j + 1, 0), 4, 0))
    for ref in (top_ref, bottom_ref):
        ref[11] = low_ref[6] * first
        ref[12] = own2_ref[...]
        ref[13] = high_ref[6] * last


def iterate_edges(count_x, *operands):
    return call(
        functools.partial(iterate_edge_kernel, count_x), [struct(14, 8, Z0), struct(14, 8, Z0)], [], 8
    )(*operands)


def coarse_kernel(
    count_x, count_y, all_ref, v3,
    c3, wx3, wy3, wz3, d3, q3, b3, w3, thin3,
    c4, wx4, wy4, wz4, d4, q4, g4, v4, w4, thin4,
):
    n3, n4 = 2 * count_x, count_x

    c3[...] = jnp.zeros(c3.shape, F32)
    b3[...] = jnp.zeros(b3.shape, F32)
    v3[...] = jnp.zeros(v3.shape, F32)
    w3[...] = jnp.zeros(w3.shape, F32)
    lane = iota((count_y, LANES), 1) < 64
    for i in range(n3):
        base = (i // 2) * count_y * 4 + 2 * (i % 2)
        for j in range(2):
            part = all_ref[pl.ds(base + j, count_y, stride=4), :]
            b3[1 + i, pl.ds(j, count_y, stride=2), :] = jnp.where(lane, part, 0.0)
            c3[1 + i, pl.ds(j, count_y, stride=2), :] = jnp.where(lane, pltpu.roll(part, 64, 1), 0.0)
    in_y = jnp.logical_and(iota((Y3, LANES), 0) < 2 * count_y, iota((Y3, LANES), 1) < 64).astype(F32)
    make_faces(c3, wx3, wy3, wz3, d3, q3, 1, n3 + 1, lambda i: 1.0, in_y, 8, whole_y=1)

    def begin3(i):
        return [(v3, i, q3[i] * b3[i])]

    loop(1, n3 + 1, begin3, 8)

    def sweep3(i):
        here, total = neighbours(v3, wx3, wy3, wz3, i)
        return [(w3, i, 0.2 * here + q3[i] * (b3[i] + total))]

    loop(1, n3 + 1, sweep3, 8)

    def restrict3(j):
        i = 2 * j + 1
        both = defect(w3, b3, wx3, wy3, wz3, d3, i) + defect(w3, b3, wx3, wy3, wz3, d3, i + 1)
        return [(thin3, j, both)]

    loop(0, n4, restrict3, 4)
    valid = iota((Y4, LANES), 0) < count_y
    rows = jnp.concatenate(
        [thin3[i, pl.ds(0, Y4, stride=2), :] + thin3[i, pl.ds(1, Y4, stride=2), :] for i in range(n4)], axis=0
    )
    pick = pair_sum_matrix(LANES, LANES)
    g4[...] = (0.5 * split_dot(rows, pick)).reshape(n4, Y4, LANES)
    for i in range(n4):
        thin3[i] = c3[2 * i + 1] + c3[2 * i + 2]
    rows = jnp.concatenate(
        [thin3[i, pl.ds(0, Y4, stride=2), :] + thin3[i, pl.ds(1, Y4, stride=2), :] for i in range(n4)], axis=0
    )
    c4[...] = jnp.zeros(c4.shape, F32)
    c4[1 : n4 + 1] = (0.125 * split_dot(rows, pick)).reshape(n4, Y4, LANES)
    in_y = jnp.logical_and(valid, iota((Y4, LANES), 1) < 32).astype(F32)
    make_faces(c4, wx4, wy4, wz4, d4, q4, 1, n4 + 1, lambda i: 1.0, in_y, n4, whole_y=1)
    v4[...] = jnp.zeros(v4.shape, F32)
    w4[...] = jnp.zeros(w4.shape, F32)
    for i in range(n4):
        g4[i] = q4[1 + i] * g4[i]
        v4[1 + i] = g4[i]

    def bottom(source, target):
        def body(i):
            here, total = neighbours(source, wx4, wy4, wz4, 1 + i)
            return [(target, 1 + i, (0.2 * here + g4[i]) + q4[1 + i] * total)]

        loop(0, n4, body, n4)

    def two(step):
        bottom(v4, w4)
        bottom(w4, v4)
        return []

    loop(0, (BOTTOM - 2) // 2, two)
    bottom(v4, w4)

    wide = split_dot(w4[1 : n4 + 1].reshape(n4 * Y4, LANES), copy_matrix(LANES, LANES)).reshape(n4, Y4, LANES)
    for i in range(n4):
        thin4[pl.ds(0, Y4, stride=2), :] = wide[i]
        thin4[pl.ds(1, Y4, stride=2), :] = wide[i]
        extra = thin4[...]
        v3[1 + 2 * i] = w3[1 + 2 * i] + extra
        v3[2 + 2 * i] = w3[2 + 2 * i] + extra

    loop(1, n3 + 1, sweep3, 8)

    def sweep3_again(i):
        here, total = neighbours(w3, wx3, wy3, wz3, i)
        return [(v3, i, 0.2 * here + q3[i] * (b3[i] + total))]

    loop(1, n3 + 1, sweep3_again, 8)


def coarse(count_x, count_y, everything):
    frame3, frame4 = (2 * count_x + 2, Y3, LANES), (count_x + 2, Y4, LANES)
    return call(
        functools.partial(coarse_kernel, count_x, count_y),
        struct(*frame3),
        [vmem(*frame3)] * 8 + [vmem(count_x, Y3, LANES)]
        + [vmem(*frame4)] * 6 + [vmem(count_x, Y4, LANES)] + [vmem(*frame4)] * 2 + [vmem(Y3, LANES)],
        8,
        flops=20000000,
        bytes_accessed=10000000,
    )(everything)


def up_kernel(
    count_x, count_y,
    v3, wx2, wy2, wz2, q2, own2, low_ref, high_ref, below_ref, above_ref, v_own, v1_ref,
    g1_mid, g1_below, g1_above, c1_ref, c_ref, g_ref, low0, high0, below0, above0,
    solution_ref, residual_ref,
    v2, w2, b2, v1, b1, c1, wx1, wy1, wz1, d1, q1, w1, spread1,
    c0, wx0, wy0, wz0, d0, q0, b0, v0, w0, spread0,
):
    place_x, place_y = lax.axis_index("gx"), lax.axis_index("gy")
    n3 = 2 * count_x
    sides = ends("gx", count_x) + ends("gy", count_y)
    first, last, low_y, high_y = sides

    fill_c1(c1, c1_ref, low0, high0, below0, above0, *sides)
    fill_g1(w1, g1_mid, g1_below, g1_above, low_y, high_y)
    in_y = inside((Y1, Z1), 0, place_y * 8 - OY1, 8 * count_y).astype(F32)
    make_faces(
        c1, wx1, wy1, wz1, d1, q1, 5, X1 - 5, lambda i: flag(place_x * 8 - OX1 + i, 8 * count_x), in_y, 2
    )

    def begin1(i):
        return [(b1, i, q1[i] * w1[i])]

    loop(5, X1 - 5, begin1, 2)
    window0(low0, high0, below0, above0, c_ref, g_ref, *sides)(c0, w0)
    in_y = inside((Y0, Z0), 0, place_y * 16 - OY0, 16 * count_y).astype(F32)
    make_faces(
        c0, wx0, wy0, wz0, d0, q0, 1, X0 - 1, lambda i: flag(place_x * 16 - OX0 + i, 16 * count_x), in_y, 1
    )

    def begin0(i):
        return [(b0, i, q0[i] * w0[i])]

    loop(1, X0 - 1, begin0, 2)

    slabs = []
    for j in range(6):
        at = 2 * place_x - 2 + j
        slabs.append(v3[1 + jnp.clip(at, 0, n3 - 1)] * flag(at, n3))
    wide = split_dot(jnp.concatenate(slabs, axis=0), copy_matrix(LANES, LANES))
    target, origin = iota((Y2, Y3), 0), iota((Y2, Y3), 1)
    rows = jnp.logical_and(origin == 2 * place_y - 2 + target // 2, target < 12).astype(F32).astype(BF16)
    half = iota((8, Z2), 0) < 4
    for j in range(6):
        extra = split_dot_left(rows, wide[Y3 * j : Y3 * j + Y3])
        for k in range(2):
            i = 2 * j + k
            at = slice(LANES * (i % 4), LANES * (i % 4) + LANES)
            mid = own2[:, at] if i // 4 == 1 else low_ref[6, :, at] * first if i < 4 else high_ref[6, :, at] * last
            below = below_ref[11 + i // 4, :, at] * low_y
            above = above_ref[11 + i // 4, :, at] * high_y
            v2[i, 0:8] = jnp.where(half, below, pltpu.roll(mid, 4, 0)) + extra[0:8]
            v2[i, 8:16] = jnp.where(half, above, 0.0) + extra[8:16]
            b2[i, 0:8] = jnp.where(half, pltpu.roll(below, 4, 0), mid)
            b2[i, 8:16] = jnp.where(half, pltpu.roll(above, 4, 0), 0.0)
    for i in range(1, X2 - 1):
        b2[i] = q2[i] * b2[i]
    sweep(v2, w2, b2, wx2, wy2, wz2, q2, 1, X2 - 1, 10)
    sweep(w2, v2, b2, wx2, wy2, wz2, q2, 2, X2 - 2, 8)

    wide = split_dot(v2[2:10].reshape(8 * Y2, Z2), copy_matrix(Z2, Z1)).reshape(8, Y2, Z1)
    spread1[...] = jnp.zeros(spread1.shape, F32)
    for j in range(8):
        extra = double_rows(spread1, wide[j, 2:10], 4)
        for k in range(2):
            i = 4 + 2 * j + k
            v1[i] = v1_ref[i - 4] + extra
    sweep(v1, w1, b1, wx1, wy1, wz1, q1, 5, X1 - 5, 3)
    sweep(w1, v1, b1, wx1, wy1, wz1, q1, 6, X1 - 6, 3)

    wide = split_dot(v1[6:18].reshape(12 * Y1, Z1), copy_matrix(Z1, Z0)).reshape(12, Y1, Z0)
    half = iota((8, Z0), 0) < 4
    for j in range(12):
        extra = double_rows(spread0, wide[j, 6:18], 0)
        for k in range(2):
            i = 2 * j - 1 + k
            if i < 0 or i >= X0:
                continue
            if i < 3:
                own = [low_ref[2 * i + side] * first for side in range(2)]
            elif i < 19:
                own = [v_own[i - 3, 8 * side : 8 * side + 8, :] for side in range(2)]
            else:
                own = [high_ref[2 * (i - 19) + side] * last for side in range(2)]
            below, above = below_ref[i // 2] * low_y, above_ref[i // 2] * high_y
            if i % 2:
                below = pltpu.roll(below, 4, 0)
            else:
                above = pltpu.roll(above, 4, 0)
            head, tail = pltpu.roll(own[0], 4, 0), pltpu.roll(own[1], 4, 0)
            v0[i, 0:8] = jnp.where(half, below, head) + extra[0:8]
            v0[i, 8:16] = jnp.where(half, head, tail) + extra[8:16]
            v0[i, 16:24] = jnp.where(half, tail, above) + extra[16:24]
    sweep(v0, w0, b0, wx0, wy0, wz0, q0, 1, X0 - 1, 2)
    sweep(w0, v0, b0, wx0, wy0, wz0, q0, 2, X0 - 2, 2)

    def finish(i):
        here, total = neighbours(v0, wx0, wy0, wz0, i + OX0)
        left = pltpu.roll(total - d0[i + OX0] * here, Y0 - OY0, 0)[0:16]
        return [(solution_ref, i, pltpu.roll(here, Y0 - OY0, 0)[0:16]), (residual_ref, i, g_ref[i] + left)]

    loop(0, 16, finish, 2)


def up(count_x, count_y, *operands):
    frame0, frame1, frame2 = (X0, Y0, Z0), (X1, Y1, Z1), (X2, Y2, Z2)
    return call(
        functools.partial(up_kernel, count_x, count_y),
        [struct(16, 16, Z0), struct(16, 16, Z0)],
        [vmem(*frame2)] * 3 + [vmem(*frame1)] * 9 + [vmem(Z1 // LANES, Y1, LANES)]
        + [vmem(*frame0)] * 9 + [vmem(Z0 // LANES, Y0, LANES)],
        24,
    )(*operands)


def to_next(cells, axis):
    count = lax.axis_size(axis)
    return lax.ppermute(cells, axis, [(i, (i + 1) % count) for i in range(count)])


def to_previous(cells, axis):
    count = lax.axis_size(axis)
    return lax.ppermute(cells, axis, [((i + 1) % count, i) for i in range(count)])


def shards(right_side, coefficient):
    count_x, count_y = lax.axis_size("gx"), lax.axis_size("gy")
    place_x = lax.axis_index("gx")

    def with_sides(low, cells, high):
        low = jnp.where(place_x > 0, low, 0.0)
        high = jnp.where(place_x < count_x - 1, high, 0.0)
        return jnp.concatenate([low, cells, high], axis=0)

    to_right, to_left, c1 = begin(coefficient, right_side)
    low, high = to_next(to_right, "gx"), to_previous(to_left, "gx")
    top, bottom = edges_y(count_x, coefficient, right_side, c1, low, high)
    below, above = to_next(top, "gy"), to_previous(bottom, "gy")
    g1, v_own = down0(count_x, count_y, coefficient, right_side, low, high, below, above)

    g1_low, g1_high = to_next(g1[2:8], "gx"), to_previous(g1[0:6], "gx")
    levels = prepare(count_x, count_y, c1, low, high, below, above)
    wx2, wy2, wz2, q2 = levels[5], levels[6], levels[7], levels[9]
    g1_mid = with_sides(g1_low, g1, g1_high)
    g1_below, g1_above = to_next(g1_mid, "gy"), to_previous(g1_mid, "gy")
    v1, to_right, to_left, own2, send3 = down1(count_x, count_y, v_own, g1_mid, g1_below, g1_above, *levels)

    low2, high2 = to_next(to_right, "gx"), to_previous(to_left, "gx")
    everything = lax.all_to_all(send3, ("gx", "gy"), split_axis=0, concat_axis=0, tiled=True)
    top, bottom = iterate_edges(count_x, v_own, own2, low2, high2)
    below2, above2 = to_next(top, "gy"), to_previous(bottom, "gy")
    v3 = coarse(count_x, count_y, everything)
    return tuple(
        up(
            count_x, count_y, v3, wx2, wy2, wz2, q2, own2, low2, high2, below2, above2, v_own, v1,
            g1_mid, g1_below, g1_above, c1, coefficient, right_side, low, high, below, above,
        )
    )


def solution(mesh):
    specs = (P("gx", "gy", None), P("gx", "gy", None))
    return jax.shard_map(shards, mesh=mesh, in_specs=specs, out_specs=specs, check_vma=False)
```

time: 123 us -> 91 us (0.74)
  Pallas kernels: 56 us -> 30 us
  starting transfers between devices: 39.2 us -> 30.6 us
  waiting for transfers between devices: 17.6 us -> 25 us
  local copies, waits for them, and re-layouts: 7.52 us -> 4.22 us
    pallas_call x1, Pallas kernels: 29.5 us -> 11.4 us  [up(): call(functools.partial(up_kernel, count_x, count_y), [struct(16, 16, Z0),...]
    ppermute x10 -> x6, waiting for transfers between devices: 5.28 us -> 14 us  [to_next(): lax.ppermute(cells, axis, [(i, (i + 1) % count) for i in range(count)])]
    ppermute x10 -> x6, starting transfers between devices: 22.2 us -> 13.9 us  [to_previous(): lax.ppermute(cells, axis, [((i + 1) % count, i) for i in range(count)])]
    pallas_call x1, Pallas kernels: 5.85 us -> 1.53 us  [prepare(): call(functools.partial(prepare_kernel, count_x, count_y), [struct(*frame1...]
    pallas_call x1, Pallas kernels: 8.22 us -> 5.07 us  [down0(): call(functools.partial(down0_kernel, count_x, count_y), [struct(8, 8, Z1)...]
    ppermute x10 -> x6, waiting for transfers between devices: 5.86 us -> 3.93 us  [to_previous(): lax.ppermute(cells, axis, [((i + 1) % count, i) for i in range(count)])]
    slice x2 -> x0, local copies, waits for them, and re-layouts: 1.84 us -> none  [the longest x1 0.96 us: shards(): coefficient[0:3]]
    unnamed x44 -> x34, local copies, waits for them, and re-layouts: 4.8 us -> 4.21 us
  transfers between devices with their start and end apart: 21 -> 13, of which waited for: 7 -> 6; matrix products, arithmetic and copies ran while one was open for 1% -> 0% of each run, Pallas kernels for 15% -> 10%
where the time goes in v2:
time: 91 us; the launch traced here: 90.6 us
  starting transfers between devices  30.6 us (34%)
  Pallas kernels  30 us (33%)
  waiting for transfers between devices  25 us (27%)
  local copies, waits for them, and re-layouts  4.22 us (5%)
    ppermute x6, waiting for transfers between devices, to_next(): lax.ppermute(cells, axis, [(i, (i + 1) % count) for i in range(count)])  14 us
    ppermute x6, starting transfers between devices, to_previous(): lax.ppermute(cells, axis, [((i + 1) % count, i) for i in range(count)])  13.9 us
    pallas_call x1, Pallas kernels, up(): call(functools.partial(up_kernel, count_x, count_y), [struct(16, 16, Z0),...  11.4 us
    all_to_all x1, starting transfers between devices, shards(): lax.all_to_all(send3, ('gx', 'gy'), split_axis=0, concat_axis=0, tiled=True)  8.62 us
    ppermute x6, starting transfers between devices, to_next(): lax.ppermute(cells, axis, [(i, (i + 1) % count) for i in range(count)])  8.04 us
    all_to_all x1, waiting for transfers between devices, shards(): lax.all_to_all(send3, ('gx', 'gy'), split_axis=0, concat_axis=0, tiled=True)  7.04 us
    pallas_call x1, Pallas kernels, coarse(): call(functools.partial(coarse_kernel, count_x, count_y), struct(*frame3),...  5.43 us
    pallas_call x1, Pallas kernels, down0(): call(functools.partial(down0_kernel, count_x, count_y), [struct(8, 8, Z1)...  5.07 us
  transfers between devices with their start and end apart: 13, of which 6 were waited for; matrix products, arithmetic and copies ran while one was open for 0% of the time, Pallas kernels for 10%

profile of v2, /device:TPU:1, one launch (start us, length us, event | category | flops | bytes accessed | tf_op | source)
XLA Modules:
  0.0 90.6 jit_solution(18308933430451310143)
XLA Ops:
  0.6 0.0 copy-start
  0.6 0.0 copy-start.1
  0.6 2.3 %shard_map.41 = (f32[7,16,512]{2,1,0:T(8,128)}, f32[7,16,512]{2,1,0:T(8,128)}, f32[8,8,256]{2,1,0:T(8,128)}) custom-call(f32[16,16,512]{2,1,0:T(8,128)} %c_ref.7, f32[16,16,512]{2,1,0:T(8,128)} %g_ref.7), custom_call_target="tpu_custom_call" | custom-call | flops 1000000 | bytes 1000000 | tf_op jit(solution)/shard_map/pallas_call | solution.py:216
  3.0 2.0 %collective-permute-start = (f32[7,16,512]{2,1,0:T(8,128)}, f32[7,16,512]{2,1,0:T(8,128)S(1)}, u32[]{:S(2)}, u32[]{:S(2)}) collective-permute-start(f32[7,16,512]{2,1,0:T(8,128)} %get-tuple-element.27), channel_id=1, source_target_pairs={{0,8},{8,16},{16,24},{24,32},{32,40},{40,48},{48,56},{56,64},{64,7... | collective-permute-start | bytes 688136 | tf_op jit(solution)/shard_map/ppermute | solution.py:718
  5.0 3.7 %collective-permute-start.1 = (f32[7,16,512]{2,1,0:T(8,128)}, f32[7,16,512]{2,1,0:T(8,128)S(1)}, u32[]{:S(2)}, u32[]{:S(2)}) collective-permute-start(f32[7,16,512]{2,1,0:T(8,128)} %get-tuple-element.28), channel_id=1, source_target_pairs={{8,0},{16,8},{24,16},{32,24},{40,32},{48,40},{56,48},{64,56},{72,6... | collective-permute-start | bytes 688136 | tf_op jit(solution)/shard_map/ppermute | solution.py:723
  8.7 5.5 %collective-permute-done.low_ref.low0 = f32[7,16,512]{2,1,0:T(8,128)S(1)} collective-permute-done((f32[7,16,512]{2,1,0:T(8,128)}, f32[7,16,512]{2,1,0:T(8,128)S(1)}, u32[]{:S(2)}, u32[]{:S(2)}) %collective-permute-start) | collective-permute-done | bytes 229408 | tf_op jit(solution)/shard_map/ppermute | solution.py:718
  14.2 0.0 collective-permute-done.1.high_ref.high0
  14.2 0.0 copy-done
  14.2 0.0 copy-done.1
  14.2 0.8 copy-done.4
  15.1 0.1 shard_map.42
  15.2 2.8 %collective-permute-start.2 = (f32[34,8,512]{2,1,0:T(8,128)S(1)}, f32[34,8,512]{2,1,0:T(8,128)S(1)}, u32[]{:S(2)}, u32[]{:S(2)}) collective-permute-start(f32[34,8,512]{2,1,0:T(8,128)S(1)} %get-tuple-element.30), channel_id=1, source_target_pairs={{0,1},{1,2},{2,3},{3,4},{4,5},{5,6},{6,7},{7,0},{8,9},{9,10},{10,1... | collective-permute-start | bytes 1671176 | tf_op jit(solution)/shard_map/ppermute | solution.py:718
  18.0 0.0 collective-permute-start.3
  18.0 6.5 %collective-permute-done.2.below_ref.below0 = f32[34,8,512]{2,1,0:T(8,128)S(1)} collective-permute-done((f32[34,8,512]{2,1,0:T(8,128)S(1)}, f32[34,8,512]{2,1,0:T(8,128)S(1)}, u32[]{:S(2)}, u32[]{:S(2)}) %collective-permute-start.2) | collective-permute-done | bytes 557088 | tf_op jit(solution)/shard_map/ppermute | solution.py:718
  24.5 2.5 %collective-permute-done.3.above_ref.above0 = f32[34,8,512]{2,1,0:T(8,128)S(1)} collective-permute-done((f32[34,8,512]{2,1,0:T(8,128)S(1)}, f32[34,8,512]{2,1,0:T(8,128)S(1)}, u32[]{:S(2)}, u32[]{:S(2)}) %collective-permute-start.3) | collective-permute-done | bytes 557088 | tf_op jit(solution)/shard_map/ppermute | solution.py:723
  27.0 5.1 %shard_map.43 = (f32[8,8,256]{2,1,0:T(8,128)S(1)}, f32[16,16,512]{2,1,0:T(8,128)S(1)}) custom-call(f32[16,16,512]{2,1,0:T(8,128)S(1)} %copy-done, f32[16,16,512]{2,1,0:T(8,128)S(1)} %copy-done.1, f32[7,16,512]{2,1,0:T(8,128)S(1)} %collective-permute-done.low_ref.low0, f32[7,16,512]{2,1,0:T(8,128)S(1)} %collective-permute-done.1.high_ref.high0, ...), custom_call_target="tpu_custom_call" | custom-call | flops 1000000 | bytes 1000000 | tf_op jit(solution)/shard_map/pallas_call | solution.py:330
  32.1 0.1 collective-permute-start.4
  32.2 4.8 %collective-permute-start.5 = (f32[6,8,256]{2,1,0:T(8,128)S(1)}, f32[6,8,256]{2,1,0:T(8,128)S(1)}, u32[]{:S(2)}, u32[]{:S(2)}) collective-permute-start(f32[6,8,256]{2,1,0:T(8,128)S(1)} %get-tuple-element.53), channel_id=1, source_target_pairs={{8,0},{16,8},{24,16},{32,24},{40,32},{48,40},{56,48},{64,56},{72,6... | collective-permute-start | bytes 147464 | tf_op jit(solution)/shard_map/ppermute | solution.py:723
  37.0 2.1 %collective-permute-done.4 = f32[6,8,256]{2,1,0:T(8,128)S(1)} collective-permute-done((f32[6,8,256]{2,1,0:T(8,128)S(1)}, f32[6,8,256]{2,1,0:T(8,128)S(1)}, u32[]{:S(2)}, u32[]{:S(2)}) %collective-permute-start.4) | collective-permute-done | bytes 49184 | tf_op jit(solution)/shard_map/ppermute | solution.py:718
  39.1 0.0 collective-permute-done.5
  39.1 0.6 collective-permute-start.7
  39.7 1.2 %collective-permute-start.6 = (f32[20,8,256]{2,1,0:T(8,128)S(1)}, f32[20,8,256]{2,1,0:T(8,128)S(1)}, u32[]{:S(2)}, u32[]{:S(2)}) collective-permute-start(f32[20,8,256]{2,1,0:T(8,128)S(1)} %pad_maximum_fusion.mid_ref.g1_mid), channel_id=1, source_target_pairs={{0,1},{1,2},{2,3},{3,4},{4,5},{5,6},{6,7},{7,0},{8,9},{9,10},{10,1... | collective-permute-start | bytes 491528 | tf_op jit(solution)/shard_map/ppermute | solution.py:718
  40.9 1.5 %shard_map.44 = (f32[24,24,256]{2,1,0:T(8,128)S(1)}, f32[24,24,256]{2,1,0:T(8,128)S(1)}, f32[24,24,256]{2,1,0:T(8,128)S(1)}, f32[24,24,256]{2,1,0:T(8,128)S(1)},...) custom-call(f32[8,8,256]{2,1,0:T(8,128)S(1)} %copy-done.5, ...), custom_call_target="tpu_custom_call" | custom-call | flops 1000000 | bytes 1000000 | tf_op jit(solution)/shard_map/pallas_call | solution.py:384
  42.4 0.0 copy-start.10
  42.5 1.4 %collective-permute-done.7.above_ref.g1_above = f32[20,8,256]{2,1,0:T(8,128)S(1)} collective-permute-done((f32[20,8,256]{2,1,0:T(8,128)S(1)}, f32[20,8,256]{2,1,0:T(8,128)S(1)}, u32[]{:S(2)}, u32[]{:S(2)}) %collective-permute-start.7) | collective-permute-done | bytes 163872 | tf_op jit(solution)/shard_map/ppermute | solution.py:723
  43.9 0.0 collective-permute-done.6.below_ref.g1_below
  43.9 2.3 %shard_map.45 = (f32[16,24,256]{2,1,0:T(8,128)S(1)}, f32[7,8,512]{2,1,0:T(8,128)}, f32[7,8,512]{2,1,0:T(8,128)}, f32[8,512]{1,0:T(8,128)S(1)}, f32[512,128]{1,0:T(8,128)S(1)}) custom-call(f32[16,16,512]{2,1,0:T(8,128)S(1)} %get-tuple-element.32.v_own_ref.own_ref.v_own, f32[20,8,256]{2,1,0:T(8,128)S(1)} %pad_maximum_fusion.mid_ref.g1_mid, ...), custom_call_target="tpu_custom_call" | custom-call | flops 1000000 | bytes 1000000 | tf_op jit(solution)/shard_map/pallas_call | solution.py:460
  46.2 0.0 copy-done.14
  46.3 0.0 copy-done.2
  46.3 0.0 copy-start.6
  46.3 0.7 copy-done.6
  47.0 0.7 copy-done.16
  47.7 0.0 collective-permute-start.8
  47.7 4.8 %collective-permute-start.9 = (f32[7,8,512]{2,1,0:T(8,128)}, f32[7,8,512]{2,1,0:T(8,128)}, u32[]{:S(2)}, u32[]{:S(2)}) collective-permute-start(f32[7,8,512]{2,1,0:T(8,128)} %get-tuple-element.48), channel_id=1, source_target_pairs={{8,0},{16,8},{24,16},{32,24},{40,32},{48,40},{56,48},{64,56},{72,6... | collective-permute-start | bytes 344072 | tf_op jit(solution)/shard_map/ppermute | solution.py:723
  52.5 8.6 %all-to-all-start = ((f32[128,4,128]{2,1,0:T(4,128)}), f32[128,4,128]{2,1,0:T(4,128)}, u32[]{:S(2)}, u32[]{:S(2)}) async-start(f32[128,4,128]{2,1,0:T(4,128)} %bitcast.2), calls=%async_computation | async-start | bytes 524288 | tf_op jit(solution)/shard_map/all_to_all | solution.py:749
  61.1 0.0 collective-permute-done.8.low_ref
  61.1 0.0 collective-permute-done.9.high_ref
  61.1 1.8 %shard_map.47 = (f32[14,8,512]{2,1,0:T(8,128)}, f32[14,8,512]{2,1,0:T(8,128)}) custom-call(f32[16,16,512]{2,1,0:T(8,128)S(1)} %get-tuple-element.32.v_own_ref.own_ref.v_own, f32[8,512]{1,0:T(8,128)S(1)} %get-tuple-element.46.own2_ref.own2, f32[7,8,512]{2,1,0:T(8,128)} %collective-permute-done.8.low_ref, f32[7,8,512]{2,1,0:T(8,128)} %collective-permute-done.9.high_ref), custom_call_target="tpu_custom_call" | custom-call | flops 1000000 | bytes 1000000 | tf_op jit(solution)/shard_map/pallas_call | solution.py:492
  63.0 1.9 %collective-permute-start.10 = (f32[14,8,512]{2,1,0:T(8,128)}, f32[14,8,512]{2,1,0:T(8,128)}, u32[]{:S(2)}, u32[]{:S(2)}) collective-permute-start(f32[14,8,512]{2,1,0:T(8,128)} %get-tuple-element.49), channel_id=1, source_target_pairs={{0,1},{1,2},{2,3},{3,4},{4,5},{5,6},{6,7},{7,0},{8,9},{9,10},{10,1... | collective-permute-start | bytes 688136 | tf_op jit(solution)/shard_map/ppermute | solution.py:718
  64.8 0.0 collective-permute-start.11
  64.8 7.0 %all-to-all-done = f32[128,4,128]{2,1,0:T(4,128)} async-done(((f32[128,4,128]{2,1,0:T(4,128)}), f32[128,4,128]{2,1,0:T(4,128)}, u32[]{:S(2)}, u32[]{:S(2)}) %all-to-all-start) | async-done | bytes 262176 | tf_op jit(solution)/shard_map/all_to_all | solution.py:749
  71.9 5.4 %shard_map.46.v3 = f32[34,16,128]{2,1,0:T(8,128)S(1)} custom-call(f32[512,128]{1,0:T(8,128)} %bitcast.1.all_ref), custom_call_target="tpu_custom_call" | custom-call | flops 20000000 | bytes 10000000 | tf_op jit(solution)/shard_map/pallas_call | solution.py:590
  77.3 0.0 collective-permute-done.10.below_ref
  77.3 0.0 collective-permute-done.11.above_ref
  77.4 0.0 copy-start.7
  77.4 1.0 %copy-done.7 = f32[16,24,256]{2,1,0:T(8,128)S(1)} copy-done((f32[16,24,256]{2,1,0:T(8,128)S(1)}, f32[16,24,256]{2,1,0:T(8,128)}, u32[]{:S(2)}) %copy-start.7) | copy-done | bytes 393240
  78.4 0.9 copy-done.15
  79.3 11.4 %shard_map.48 = (f32[16,16,512]{2,1,0:T(8,128)}, f32[16,16,512]{2,1,0:T(8,128)}) custom-call(f32[34,16,128]{2,1,0:T(8,128)S(1)} %shard_map.46.v3, f32[12,16,128]{2,1,0:T(8,128)S(1)} %copy-done.9, f32[12,16,128]{2,1,0:T(8,128)S(1)} %copy-done.11, f32[12,16,128]{2,1,0:T(8,128)S(1)} %copy-done.13, f32[12,16,128]{2,1,0:T(8,128)S(1)} %copy-done.15, ...), custom_call_target="tpu_custom_call" | custom-call | flops 1000000 | bytes 1000000 | tf_op jit(solution)/shard_map/pallas_call | solution.py:707
  (24 shorter events, 0.1 us)
Async XLA Ops:
  0.6 13.6 %copy-start = (f32[16,16,512]{2,1,0:T(8,128)S(1)}, f32[16,16,512]{2,1,0:T(8,128)}, u32[]{:S(2)}) copy-start(f32[16,16,512]{2,1,0:T(8,128)} %c_ref.7) | copy-start | bytes 1572868
  0.6 13.6 %copy-start.1 = (f32[16,16,512]{2,1,0:T(8,128)S(1)}, f32[16,16,512]{2,1,0:T(8,128)}, u32[]{:S(2)}) copy-start(f32[16,16,512]{2,1,0:T(8,128)} %g_ref.7) | copy-start | bytes 1572868
  3.0 11.2 %collective-permute-start = (f32[7,16,512]{2,1,0:T(8,128)}, f32[7,16,512]{2,1,0:T(8,128)S(1)}, u32[]{:S(2)}, u32[]{:S(2)}) collective-permute-start(f32[7,16,512]{2,1,0:T(8,128)} %get-tuple-element.27), channel_id=1, source_target_pairs={{0,8},{8,16},{16,24},{24,32},{32,40},{40,48},{48,56},{56,64},{64,7... | collective-permute-start | bytes 688136 | tf_op jit(solution)/shard_map/ppermute | solution.py:718
  5.0 9.2 %collective-permute-start.1 = (f32[7,16,512]{2,1,0:T(8,128)}, f32[7,16,512]{2,1,0:T(8,128)S(1)}, u32[]{:S(2)}, u32[]{:S(2)}) collective-permute-start(f32[7,16,512]{2,1,0:T(8,128)} %get-tuple-element.28), channel_id=1, source_target_pairs={{8,0},{16,8},{24,16},{32,24},{40,32},{48,40},{56,48},{64,56},{72,6... | collective-permute-start | bytes 688136 | tf_op jit(solution)/shard_map/ppermute | solution.py:723
  14.2 0.8 copy-start.4
  15.2 9.3 %collective-permute-start.2 = (f32[34,8,512]{2,1,0:T(8,128)S(1)}, f32[34,8,512]{2,1,0:T(8,128)S(1)}, u32[]{:S(2)}, u32[]{:S(2)}) collective-permute-start(f32[34,8,512]{2,1,0:T(8,128)S(1)} %get-tuple-element.30), channel_id=1, source_target_pairs={{0,1},{1,2},{2,3},{3,4},{4,5},{5,6},{6,7},{7,0},{8,9},{9,10},{10,1... | collective-permute-start | bytes 1671176 | tf_op jit(solution)/shard_map/ppermute | solution.py:718
  18.0 9.0 %collective-permute-start.3 = (f32[34,8,512]{2,1,0:T(8,128)S(1)}, f32[34,8,512]{2,1,0:T(8,128)S(1)}, u32[]{:S(2)}, u32[]{:S(2)}) collective-permute-start(f32[34,8,512]{2,1,0:T(8,128)S(1)} %get-tuple-element.31), channel_id=1, source_target_pairs={{1,0},{2,1},{3,2},{4,3},{5,4},{6,5},{7,6},{0,7},{9,8},{10,9},{11,1... | collective-permute-start | bytes 1671176 | tf_op jit(solution)/shard_map/ppermute | solution.py:723
  32.1 7.0 %collective-permute-start.4 = (f32[6,8,256]{2,1,0:T(8,128)S(1)}, f32[6,8,256]{2,1,0:T(8,128)S(1)}, u32[]{:S(2)}, u32[]{:S(2)}) collective-permute-start(f32[6,8,256]{2,1,0:T(8,128)S(1)} %get-tuple-element.52), channel_id=1, source_target_pairs={{0,8},{8,16},{16,24},{24,32},{32,40},{40,48},{48,56},{56,64},{64,7... | collective-permute-start | bytes 147464 | tf_op jit(solution)/shard_map/ppermute | solution.py:718
  32.2 6.9 %collective-permute-start.5 = (f32[6,8,256]{2,1,0:T(8,128)S(1)}, f32[6,8,256]{2,1,0:T(8,128)S(1)}, u32[]{:S(2)}, u32[]{:S(2)}) collective-permute-start(f32[6,8,256]{2,1,0:T(8,128)S(1)} %get-tuple-element.53), channel_id=1, source_target_pairs={{8,0},{16,8},{24,16},{32,24},{40,32},{48,40},{56,48},{64,56},{72,6... | collective-permute-start | bytes 147464 | tf_op jit(solution)/shard_map/ppermute | solution.py:723
  39.1 1.8 %copy-start.5 = (f32[8,8,256]{2,1,0:T(8,128)S(1)}, f32[8,8,256]{2,1,0:T(8,128)}, u32[]{:S(2)}) copy-start(f32[8,8,256]{2,1,0:T(8,128)} %get-tuple-element.29.c1_ref) | copy-start | bytes 196612
  39.1 4.8 %collective-permute-start.7 = (f32[20,8,256]{2,1,0:T(8,128)S(1)}, f32[20,8,256]{2,1,0:T(8,128)S(1)}, u32[]{:S(2)}, u32[]{:S(2)}) collective-permute-start(f32[20,8,256]{2,1,0:T(8,128)S(1)} %pad_maximum_fusion.mid_ref.g1_mid), channel_id=1, source_target_pairs={{1,0},{2,1},{3,2},{4,3},{5,4},{6,5},{7,6},{0,7},{9,8},{10,9},{11,1... | collective-permute-start | bytes 491528 | tf_op jit(solution)/shard_map/ppermute | solution.py:723
  39.7 4.2 %collective-permute-start.6 = (f32[20,8,256]{2,1,0:T(8,128)S(1)}, f32[20,8,256]{2,1,0:T(8,128)S(1)}, u32[]{:S(2)}, u32[]{:S(2)}) collective-permute-start(f32[20,8,256]{2,1,0:T(8,128)S(1)} %pad_maximum_fusion.mid_ref.g1_mid), channel_id=1, source_target_pairs={{0,1},{1,2},{2,3},{3,4},{4,5},{5,6},{6,7},{7,0},{8,9},{9,10},{10,1... | collective-permute-start | bytes 491528 | tf_op jit(solution)/shard_map/ppermute | solution.py:718
  42.4 3.8 %copy-start.8 = (f32[12,16,128]{2,1,0:T(8,128)}, f32[12,16,128]{2,1,0:T(8,128)S(1)}, u32[]{:S(2)}) copy-start(f32[12,16,128]{2,1,0:T(8,128)S(1)} %get-tuple-element.39.wx2) | copy-start | bytes 294916
  42.4 3.8 %copy-start.10 = (f32[12,16,128]{2,1,0:T(8,128)}, f32[12,16,128]{2,1,0:T(8,128)S(1)}, u32[]{:S(2)}) copy-start(f32[12,16,128]{2,1,0:T(8,128)S(1)} %get-tuple-element.40.wy2) | copy-start | bytes 294916
  42.4 3.8 %copy-start.12 = (f32[12,16,128]{2,1,0:T(8,128)}, f32[12,16,128]{2,1,0:T(8,128)S(1)}, u32[]{:S(2)}) copy-start(f32[12,16,128]{2,1,0:T(8,128)S(1)} %get-tuple-element.41.wz2) | copy-start | bytes 294916
  42.5 3.8 %copy-start.14 = (f32[12,16,128]{2,1,0:T(8,128)}, f32[12,16,128]{2,1,0:T(8,128)S(1)}, u32[]{:S(2)}) copy-start(f32[12,16,128]{2,1,0:T(8,128)S(1)} %get-tuple-element.43.q2) | copy-start | bytes 294916
  43.9 2.4 %copy-start.2 = (f32[20,8,256]{2,1,0:T(8,128)}, f32[20,8,256]{2,1,0:T(8,128)S(1)}, u32[]{:S(2)}) copy-start(f32[20,8,256]{2,1,0:T(8,128)S(1)} %collective-permute-done.6.below_ref.g1_below) | copy-start | bytes 491524
  46.3 0.7 copy-start.6
  47.0 0.7 copy-start.16
  47.7 13.4 %collective-permute-start.8 = (f32[7,8,512]{2,1,0:T(8,128)}, f32[7,8,512]{2,1,0:T(8,128)}, u32[]{:S(2)}, u32[]{:S(2)}) collective-permute-start(f32[7,8,512]{2,1,0:T(8,128)} %get-tuple-element.47), channel_id=1, source_target_pairs={{0,8},{8,16},{16,24},{24,32},{32,40},{40,48},{48,56},{56,64},{64,7... | collective-permute-start | bytes 344072 | tf_op jit(solution)/shard_map/ppermute | solution.py:718
  47.7 13.4 %collective-permute-start.9 = (f32[7,8,512]{2,1,0:T(8,128)}, f32[7,8,512]{2,1,0:T(8,128)}, u32[]{:S(2)}, u32[]{:S(2)}) collective-permute-start(f32[7,8,512]{2,1,0:T(8,128)} %get-tuple-element.48), channel_id=1, source_target_pairs={{8,0},{16,8},{24,16},{32,24},{40,32},{48,40},{56,48},{64,56},{72,6... | collective-permute-start | bytes 344072 | tf_op jit(solution)/shard_map/ppermute | solution.py:723
  52.5 19.4 %all-to-all-start = ((f32[128,4,128]{2,1,0:T(4,128)}), f32[128,4,128]{2,1,0:T(4,128)}, u32[]{:S(2)}, u32[]{:S(2)}) async-start(f32[128,4,128]{2,1,0:T(4,128)} %bitcast.2), calls=%async_computation | async-start | bytes 524288 | tf_op jit(solution)/shard_map/all_to_all | solution.py:749
  63.0 14.4 %collective-permute-start.10 = (f32[14,8,512]{2,1,0:T(8,128)}, f32[14,8,512]{2,1,0:T(8,128)}, u32[]{:S(2)}, u32[]{:S(2)}) collective-permute-start(f32[14,8,512]{2,1,0:T(8,128)} %get-tuple-element.49), channel_id=1, source_target_pairs={{0,1},{1,2},{2,3},{3,4},{4,5},{5,6},{6,7},{7,0},{8,9},{9,10},{10,1... | collective-permute-start | bytes 688136 | tf_op jit(solution)/shard_map/ppermute | solution.py:718
  64.8 12.5 %collective-permute-start.11 = (f32[14,8,512]{2,1,0:T(8,128)}, f32[14,8,512]{2,1,0:T(8,128)}, u32[]{:S(2)}, u32[]{:S(2)}) collective-permute-start(f32[14,8,512]{2,1,0:T(8,128)} %get-tuple-element.50), channel_id=1, source_target_pairs={{1,0},{2,1},{3,2},{4,3},{5,4},{6,5},{7,6},{0,7},{9,8},{10,9},{11,1... | collective-permute-start | bytes 688136 | tf_op jit(solution)/shard_map/ppermute | solution.py:723
  71.9 5.5 %copy-start.3 = (f32[20,8,256]{2,1,0:T(8,128)S(1)}, f32[20,8,256]{2,1,0:T(8,128)}, u32[]{:S(2)}) copy-start(f32[20,8,256]{2,1,0:T(8,128)} %copy-done.2) | copy-start | bytes 491524
  71.9 5.5 %copy-start.9 = (f32[12,16,128]{2,1,0:T(8,128)S(1)}, f32[12,16,128]{2,1,0:T(8,128)}, u32[]{:S(2)}) copy-start(f32[12,16,128]{2,1,0:T(8,128)} %copy-done.8) | copy-start | bytes 294916
  71.9 5.5 %copy-start.11 = (f32[12,16,128]{2,1,0:T(8,128)S(1)}, f32[12,16,128]{2,1,0:T(8,128)}, u32[]{:S(2)}) copy-start(f32[12,16,128]{2,1,0:T(8,128)} %copy-done.10) | copy-start | bytes 294916
  71.9 5.5 %copy-start.13 = (f32[12,16,128]{2,1,0:T(8,128)S(1)}, f32[12,16,128]{2,1,0:T(8,128)}, u32[]{:S(2)}) copy-start(f32[12,16,128]{2,1,0:T(8,128)} %copy-done.12) | copy-start | bytes 294916
  77.4 1.0 %copy-start.7 = (f32[16,24,256]{2,1,0:T(8,128)S(1)}, f32[16,24,256]{2,1,0:T(8,128)}, u32[]{:S(2)}) copy-start(f32[16,24,256]{2,1,0:T(8,128)} %copy-done.6) | copy-start | bytes 1179652
  78.4 0.9 copy-start.15

commit v3 on v2

--- a/solution.py
+++ b/solution.py
@@ -17,6 +17,7 @@
 X1, Y1, Z1, OX1, OY1 = 24, 24, 256, 8, 8
 X2, Y2, Z2, OX2, OY2 = 12, 16, 128, 4, 4
 Y3, Y4, LANES = 16, 8, 128
+C_TILES, CG_TILES = 11, 16
 
 
 def iota(shape, dim):
@@ -24,11 +25,36 @@
 
 
 def up_of(cells, dim):
-    return pltpu.roll(cells, cells.shape[dim] - 1, dim)
+    if dim == 0 or cells.shape[1] == LANES:
+        return pltpu.roll(cells, cells.shape[dim] - 1, dim)
+    return jnp.concatenate([cells[:, LANES:], pltpu.roll(cells[:, :LANES], LANES - 1, 1)], axis=1)
 
 
 def down_of(cells, dim):
-    return pltpu.roll(cells, 1, dim)
+    if dim == 0 or cells.shape[1] == LANES:
+        return pltpu.roll(cells, 1, dim)
+    return jnp.concatenate([pltpu.roll(cells[:, -LANES:], 1, 1), cells[:, :-LANES]], axis=1)
+
+
+def cell_of(position, count):
+    pieces = count // LANES
+    return pieces * (position % LANES) + position // LANES
+
+
+def deal_matrix(count):
+    hit = iota((count, count), 0) == cell_of(iota((count, count), 1), count)
+    return hit.astype(F32).astype(BF16)
+
+
+def collect_matrix(count):
+    hit = cell_of(iota((count, count), 0), count) == iota((count, count), 1)
+    return hit.astype(F32).astype(BF16)
+
+
+def pair_sums(cells):
+    pieces = [lanes(cells, k) for k in range(cells.shape[1] // LANES)]
+    sums = [even + odd for even, odd in zip(pieces[::2], pieces[1::2])]
+    return jnp.concatenate(sums, axis=1) if len(sums) > 1 else sums[0]
 
 
 def split_dot(cells, pick):
@@ -54,6 +80,11 @@
     return hit.astype(F32).astype(BF16)
 
 
+def pair_deal_matrix(fine, coarse):
+    hit = iota((fine, coarse), 0) // 2 == cell_of(iota((fine, coarse), 1), coarse)
+    return hit.astype(F32).astype(BF16)
+
+
 def copy_matrix(coarse, fine):
     hit = iota((coarse, fine), 0) == iota((coarse, fine), 1) // 2
     return hit.astype(F32).astype(BF16)
@@ -86,6 +117,13 @@
         lax.fori_loop(0, count, step, 0)
     if (last - first) % width:
         run(first + count * width, (last - first) % width)
+
+
+def inverse(total):
+    total = jnp.maximum(total, 1e-30)
+    guess = pl.reciprocal(total, approx=True)
+    guess = guess * (2.0 - total * guess)
+    return guess * (2.0 - total * guess)
 
 
 def make_faces(c, wx, wy, wz, d, q, first, last, in_x, in_y, width, whole_y=0):
@@ -113,7 +151,7 @@
             (wy, i, side),
             (wz, i, jnp.where(end_z, 0.0, 0.5 * (here + z_up))),
             (d, i, total),
-            (q, i, (in_y * (OMEGA * in_x(i))) / jnp.maximum(total, 1e-30)),
+            (q, i, (in_y * (OMEGA * in_x(i))) * inverse(total)),
         ]
 
     loop(first, last, body, width)
@@ -189,6 +227,26 @@
     return pltpu.VMEM(shape, F32)
 
 
+WHOLE = pl.BlockSpec(memory_space=pltpu.VMEM)
+FAR = pl.BlockSpec(memory_space=pl.ANY)
+FAR_COUNT = 26
+
+
+def start_copies(sources, targets, sems, first):
+    copies = [
+        pltpu.make_async_copy(source, target, sems.at[first + k])
+        for k, (source, target) in enumerate(zip(sources, targets))
+    ]
+    for copy in copies:
+        copy.start()
+    return copies
+
+
+def wait_copies(copies):
+    for copy in copies:
+        copy.wait()
+
+
 def place_of(i):
     row, cell = 8 * ((i // 2) % 2), Z1 * (i % 2)
     return 5 + i // 4, slice(row, row + 8), slice(cell, cell + Z1)
@@ -204,7 +262,7 @@
         next_ref[3 + i] = g_ref[14 + i]
         previous_ref[3 + i] = g_ref[i]
     rows = jnp.concatenate([halve_rows(pairs, i, 0, 8) for i in range(8)], axis=0)
-    small = 0.125 * split_dot(rows, pair_sum_matrix(Z0, Z1))
+    small = 0.125 * split_dot(rows, pair_deal_matrix(Z0, Z1))
     for i in range(8):
         block = small[8 * i : 8 * i + 8]
         c1_ref[i] = block
@@ -214,44 +272,64 @@
 
 def begin(coefficient, right_side):
     return call(
-        begin_kernel, [struct(7, 16, Z0), struct(7, 16, Z0), struct(8, 8, Z1)], [vmem(8, Z0 // LANES, 16, LANES)], 60
+        begin_kernel, [struct(7, 16, Z0), struct(7, 16, Z0), struct(8, 8, Z1)], [vmem(8, Z0 // LANES, 16, LANES)], 8
     )(coefficient, right_side)
 
 
-def edge_kernel(count_x, c_ref, g_ref, c1_ref, low_ref, high_ref, top_ref, bottom_ref):
+def deal_kernel(c_ref, g_ref, c_out, g_out):
+    pick = deal_matrix(Z0)
+    for ref, out in ((c_ref, c_out), (g_ref, g_out)):
+        out[...] = split_dot(ref[...].reshape(256, Z0), pick).reshape(16, 16, Z0)
+
+
+def deal(coefficient, right_side):
+    return call(deal_kernel, [struct(16, 16, Z0), struct(16, 16, Z0)], [], 8)(coefficient, right_side)
+
+
+def edge_kernel(count_x, c_ref, g_ref, c1_ref, low_raw, high_raw, top_ref, bottom_ref, low_ref, high_ref):
+    pick = deal_matrix(Z0)
+    for raw, out in ((low_raw, low_ref), (high_raw, high_ref)):
+        out[0:5] = split_dot(raw[0:5].reshape(80, Z0), pick).reshape(5, 16, Z0)
+        out[5:7] = raw[5:7]
     place = lax.axis_index("gx")
     first = jnp.where(place > 0, 1.0, 0.0).astype(F32)
     last = jnp.where(place < count_x - 1, 1.0, 0.0).astype(F32)
     row = iota((8, Z0), 0)
 
-    def put(i, c, g):
-        return [
-            (top_ref, i, jnp.where(row < 4, pltpu.roll(c[8:16], 4, 0), g[8:16])),
-            (bottom_ref, i, jnp.where(row < 4, g[0:8], pltpu.roll(c[0:8], 4, 0))),
-        ]
-
-    def put_now(*what):
-        for ref, at, value in put(*what):
-            ref[at] = value
-
-    nothing = jnp.zeros((16, Z0), F32)
-    for i in range(3):
-        put_now(i, low_ref[i] * first, low_ref[i + 2] * first if i > 0 else nothing)
-        put_now(19 + i, high_ref[i] * last, high_ref[i + 3] * last if i < 2 else nothing)
-
-    def body(i):
-        return put(i + 3, c_ref[i], g_ref[i])
-
-    loop(0, 16, body, 2)
+    def c_part(i, half):
+        rows = slice(8 * half, 8 * half + 8)
+        if i < 3:
+            return low_ref[i, rows, :] * first
+        return c_ref[i - 3, rows, :] if i < 19 else high_ref[i - 19, rows, :] * last
+
+    def g_part(i, half):
+        rows = slice(8 * half, 8 * half + 8)
+        if i < 3:
+            return low_ref[i + 2, rows, :] * first
+        return g_ref[i - 3, rows, :] if i < 19 else high_ref[i - 16, rows, :] * last
+
+    for j in range(X0 // 2):
+        top_ref[j] = jnp.where(row < 4, pltpu.roll(c_part(2 * j, 1), 4, 0), c_part(2 * j + 1, 1))
+        bottom_ref[j] = jnp.where(row < 4, c_part(2 * j, 0), pltpu.roll(c_part(2 * j + 1, 0), 4, 0))
+    for j in range(5):
+        top, bottom = g_part(1 + 4 * j, 1), g_part(1 + 4 * j, 0)
+        top = pltpu.roll(top, 2, 0)
+        for k in range(1, 4):
+            part = g_part(1 + 4 * j + k, 1)
+            part = pltpu.roll(part, (2 * k + 2) % 8, 0) if k < 3 else part
+            top = jnp.where(row // 2 == k, part, top)
+            bottom = jnp.where(row // 2 == k, pltpu.roll(g_part(1 + 4 * j + k, 0), 2 * k, 0), bottom)
+        top_ref[C_TILES + j] = top
+        bottom_ref[C_TILES + j] = bottom
     for i in range(24):
         part = low_ref[place_of(i)] * first if i < 8 else c1_ref[i - 8] if i < 16 else high_ref[place_of(i - 16)] * last
         for ref in (top_ref, bottom_ref):
-            ref[X0 + i // 2, :, Z1 * (i % 2) : Z1 * (i % 2) + Z1] = part
+            ref[CG_TILES + i // 2, :, Z1 * (i % 2) : Z1 * (i % 2) + Z1] = part
 
 
 def edges_y(count_x, *operands):
     return call(
-        functools.partial(edge_kernel, count_x), [struct(X0 + 12, 8, Z0), struct(X0 + 12, 8, Z0)], [], 8
+        functools.partial(edge_kernel, count_x), [struct(CG_TILES + 12, 8, Z0)] * 2 + [struct(7, 16, Z0)] * 2, [], 8
     )(*operands)
 
 
@@ -263,30 +341,36 @@
 
 def window0(low_ref, high_ref, below_ref, above_ref, c_ref, g_ref, first, last, low_y, high_y):
     row = iota((8, Z0), 0) < 4
-    nothing = jnp.zeros((16, Z0), F32)
 
     def put(own, below, above):
         head, tail = pltpu.roll(own[0:8], 4, 0), pltpu.roll(own[8:16], 4, 0)
         parts = [jnp.where(row, below, head), jnp.where(row, head, tail), jnp.where(row, tail, above)]
         return jnp.concatenate(parts, axis=0)
 
+    def turn(cells, rows):
+        return pltpu.roll(cells, rows % 8, 0) if rows % 8 else cells
+
     def c_slab(i, own):
-        return put(own, below_ref[i] * low_y, above_ref[i] * high_y)
+        odd = i % 2
+        below = turn(below_ref[i // 2], 4 * odd) * low_y
+        return put(own, below, turn(above_ref[i // 2], 4 - 4 * odd) * high_y)
 
     def g_slab(i, own):
-        return put(own, pltpu.roll(below_ref[i], 4, 0) * low_y, pltpu.roll(above_ref[i], 4, 0) * high_y)
+        tile, k = C_TILES + (i - 1) // 4, (i - 1) % 4
+        below = turn(below_ref[tile], 2 - 2 * k) * low_y
+        return put(own, below, turn(above_ref[tile], 4 - 2 * k) * high_y)
 
     def fill(c, g):
         for i in range(3):
             c[i] = c_slab(i, low_ref[i] * first)
             c[19 + i] = c_slab(19 + i, high_ref[i] * last)
-            g[i] = g_slab(i, low_ref[i + 2] * first if i > 0 else nothing)
-            g[19 + i] = g_slab(19 + i, high_ref[i + 3] * last if i < 2 else nothing)
-
-        def body(i):
-            return [(c, i + 3, c_slab(i + 3, c_ref[i])), (g, i + 3, g_slab(i + 3, g_ref[i]))]
-
-        loop(0, 16, body)
+        for i in range(3, 19):
+            c[i] = c_slab(i, c_ref[i - 3])
+        for i in (1, 2):
+            g[i] = g_slab(i, low_ref[i + 2] * first)
+            g[18 + i] = g_slab(18 + i, high_ref[i + 2] * last)
+        for i in range(3, 19):
+            g[i] = g_slab(i, g_ref[i - 3])
 
     return fill
 
@@ -301,14 +385,14 @@
     window0(low_ref, high_ref, below_ref, above_ref, c_ref, g_ref, *sides)(c, g)
     in_y = inside((Y0, Z0), 0, place_y * 16 - OY0, 16 * count_y).astype(F32)
     make_faces(
-        c, wx, wy, wz, d, q, 1, X0 - 1, lambda i: flag(place_x * 16 - OX0 + i, 16 * count_x), in_y, 1
+        c, wx, wy, wz, d, q, 1, X0 - 1, lambda i: flag(place_x * 16 - OX0 + i, 16 * count_x), in_y, 2
     )
 
     def begin(i):
         return [(b, i, q[i] * g[i])]
 
     loop(1, X0 - 1, begin, 2)
-    sweep(b, v, b, wx, wy, wz, q, 2, X0 - 2, 2)
+    sweep(b, v, b, wx, wy, wz, q, 2, X0 - 2, 3)
 
     def own_of(i):
         return [(v_own_ref, i, pltpu.roll(v[i + 3], Y0 - OY0, 0)[0:16])]
@@ -322,7 +406,7 @@
 
     loop(0, 8, restrict)
     rows = jnp.concatenate([halve_rows(pairs, i, 4, 8) for i in range(8)], axis=0)
-    g1_ref[...] = (0.5 * split_dot(rows, pair_sum_matrix(Z0, Z1))).reshape(8, 8, Z1)
+    g1_ref[...] = (0.5 * pair_sums(rows)).reshape(8, 8, Z1)
 
 
 def down0(count_x, count_y, *operands):
@@ -337,7 +421,7 @@
 
 def fill_c1(c1, c1_ref, low_ref, high_ref, below_ref, above_ref, first, last, low_y, high_y):
     for i in range(24):
-        at = X0 + i // 2, slice(0, 8), slice(Z1 * (i % 2), Z1 * (i % 2) + Z1)
+        at = CG_TILES + i // 2, slice(0, 8), slice(Z1 * (i % 2), Z1 * (i % 2) + Z1)
         part = low_ref[place_of(i)] * first if i < 8 else c1_ref[i - 8] if i < 16 else high_ref[place_of(i - 16)] * last
         c1[i, 0:8, :] = below_ref[at] * low_y
         c1[i, 8:16, :] = part
@@ -362,7 +446,7 @@
     for i in range(12):
         rows.append(halve_rows(pairs, i, 0, 12))
         rows.append(blank)
-    c2[...] = (0.125 * split_dot(jnp.concatenate(rows, axis=0), pair_sum_matrix(Z1, Z2))).reshape(X2, Y2, Z2)
+    c2[...] = (0.125 * pair_sums(jnp.concatenate(rows, axis=0))).reshape(X2, Y2, Z2)
     in_y = inside((Y2, Z2), 0, place_y * 4 - OY2, 4 * count_y).astype(F32)
     make_faces(
         c2, wx2, wy2, wz2, d2, q2, 1, X2 - 1, lambda i: flag(place_x * 4 - OX2 + i, 4 * count_x), in_y, 10
@@ -419,7 +503,7 @@
 
     loop(0, 8, restrict, 2)
     rows = jnp.concatenate([halve_rows(pairs, i, 4, 8) for i in range(8)], axis=0)
-    small = 0.5 * split_dot(rows, pair_sum_matrix(Z1, Z2))
+    small = 0.5 * pair_sums(rows)
     g2[...] = jnp.zeros((X2, Y2, Z2), F32)
     for i in range(8):
         g2[2 + i, 2:10, :] = small[8 * i : 8 * i + 8]
@@ -494,7 +578,42 @@
     )(*operands)
 
 
-def coarse_kernel(
+def weights0_kernel(
+    count_x, count_y, c_ref, g_ref, low0, high0, below0, above0, *rest,
+):
+    stored, (c, g, wx, wy, wz, d, q, b, sems) = rest[:6], rest[6:]
+    place_x, place_y = lax.axis_index("gx"), lax.axis_index("gy")
+    sides = ends("gx", count_x) + ends("gy", count_y)
+    window0(low0, high0, below0, above0, c_ref, g_ref, *sides)(c, g)
+    in_y = inside((Y0, Z0), 0, place_y * 16 - OY0, 16 * count_y).astype(F32)
+    make_faces(
+        c, wx, wy, wz, d, q, 1, X0 - 1, lambda i: flag(place_x * 16 - OX0 + i, 16 * count_x), in_y, 2
+    )
+    copies = start_copies((wx, wy, wz, d, q), stored[:5], sems, 0)
+
+    def begin(i):
+        return [(b, i, q[i] * g[i])]
+
+    loop(1, X0 - 1, begin, 2)
+    copies += start_copies((b,), stored[5:], sems, 5)
+    wait_copies(copies)
+
+
+def weights0(count_x, count_y, *operands):
+    frame0 = (X0, Y0, Z0)
+    return call(
+        functools.partial(weights0_kernel, count_x, count_y),
+        [struct(*frame0)] * 6,
+        [vmem(*frame0)] * 8 + [pltpu.SemaphoreType.DMA((6,))],
+        60,
+        in_specs=[WHOLE] * 6,
+        out_specs=[FAR] * 6,
+        flops=20000000,
+        bytes_accessed=20000000,
+    )(*operands)
+
+
+def solve_coarse(
     count_x, count_y, all_ref, v3,
     c3, wx3, wy3, wz3, d3, q3, b3, w3, thin3,
     c4, wx4, wy4, wz4, d4, q4, g4, v4, w4, thin4,
@@ -524,7 +643,7 @@
         here, total = neighbours(v3, wx3, wy3, wz3, i)
         return [(w3, i, 0.2 * here + q3[i] * (b3[i] + total))]
 
-    loop(1, n3 + 1, sweep3, 8)
+    loop(1, n3 + 1, sweep3, 16)
 
     def restrict3(j):
         i = 2 * j + 1
@@ -582,30 +701,26 @@
         here, total = neighbours(w3, wx3, wy3, wz3, i)
         return [(v3, i, 0.2 * here + q3[i] * (b3[i] + total))]
 
-    loop(1, n3 + 1, sweep3_again, 8)
-
-
-def coarse(count_x, count_y, everything):
-    frame3, frame4 = (2 * count_x + 2, Y3, LANES), (count_x + 2, Y4, LANES)
-    return call(
-        functools.partial(coarse_kernel, count_x, count_y),
-        struct(*frame3),
-        [vmem(*frame3)] * 8 + [vmem(count_x, Y3, LANES)]
-        + [vmem(*frame4)] * 6 + [vmem(count_x, Y4, LANES)] + [vmem(*frame4)] * 2 + [vmem(Y3, LANES)],
-        8,
-        flops=20000000,
-        bytes_accessed=10000000,
-    )(everything)
+    loop(1, n3 + 1, sweep3_again, 16)
 
 
 def up_kernel(
     count_x, count_y,
-    v3, wx2, wy2, wz2, q2, own2, low_ref, high_ref, below_ref, above_ref, v_own, v1_ref,
-    g1_mid, g1_below, g1_above, c1_ref, c_ref, g_ref, low0, high0, below0, above0,
-    solution_ref, residual_ref,
-    v2, w2, b2, v1, b1, c1, wx1, wy1, wz1, d1, q1, w1, spread1,
-    c0, wx0, wy0, wz0, d0, q0, b0, v0, w0, spread0,
+    all_ref, *rest,
 ):
+    far, rest = rest[:FAR_COUNT], rest[FAR_COUNT:]
+    solution_far, residual_far = rest[:2]
+    near, rest = rest[2 : 2 + FAR_COUNT], rest[2 + FAR_COUNT :]
+    grids, rest = rest[:20], rest[20:]
+    v2, w2, b2, v1, b1, c1, wx1, wy1, wz1, d1, q1, w1, spread1 = rest[:13]
+    v0, w0, spread0, solution_ref, residual_ref, sems = rest[13:]
+    (wx2, wy2, wz2, q2, own2, low_ref, high_ref, below_ref, above_ref,
+     g1_mid, g1_below, g1_above, c1_ref, low0, high0, below0, above0, v1_ref, v_own,
+     wx0, wy0, wz0, q0, b0, d0, g_ref) = near
+    copies = start_copies(far, near, sems, 0)
+    v3 = grids[0]
+    solve_coarse(count_x, count_y, all_ref, *grids)
+    wait_copies(copies[:19])
     place_x, place_y = lax.axis_index("gx"), lax.axis_index("gy")
     n3 = 2 * count_x
     sides = ends("gx", count_x) + ends("gy", count_y)
@@ -622,16 +737,6 @@
         return [(b1, i, q1[i] * w1[i])]
 
     loop(5, X1 - 5, begin1, 2)
-    window0(low0, high0, below0, above0, c_ref, g_ref, *sides)(c0, w0)
-    in_y = inside((Y0, Z0), 0, place_y * 16 - OY0, 16 * count_y).astype(F32)
-    make_faces(
-        c0, wx0, wy0, wz0, d0, q0, 1, X0 - 1, lambda i: flag(place_x * 16 - OX0 + i, 16 * count_x), in_y, 1
-    )
-
-    def begin0(i):
-        return [(b0, i, q0[i] * w0[i])]
-
-    loop(1, X0 - 1, begin0, 2)
 
     slabs = []
     for j in range(6):
@@ -658,20 +763,21 @@
     sweep(v2, w2, b2, wx2, wy2, wz2, q2, 1, X2 - 1, 10)
     sweep(w2, v2, b2, wx2, wy2, wz2, q2, 2, X2 - 2, 8)
 
-    wide = split_dot(v2[2:10].reshape(8 * Y2, Z2), copy_matrix(Z2, Z1)).reshape(8, Y2, Z1)
     spread1[...] = jnp.zeros(spread1.shape, F32)
     for j in range(8):
-        extra = double_rows(spread1, wide[j, 2:10], 4)
+        extra = double_rows(spread1, v2[2 + j, 2:10], 4)
+        extra = jnp.concatenate([extra, extra], axis=1)
         for k in range(2):
             i = 4 + 2 * j + k
             v1[i] = v1_ref[i - 4] + extra
-    sweep(v1, w1, b1, wx1, wy1, wz1, q1, 5, X1 - 5, 3)
-    sweep(w1, v1, b1, wx1, wy1, wz1, q1, 6, X1 - 6, 3)
-
-    wide = split_dot(v1[6:18].reshape(12 * Y1, Z1), copy_matrix(Z1, Z0)).reshape(12, Y1, Z0)
+    sweep(v1, w1, b1, wx1, wy1, wz1, q1, 5, X1 - 5, 7)
+    sweep(w1, v1, b1, wx1, wy1, wz1, q1, 6, X1 - 6, 6)
+
     half = iota((8, Z0), 0) < 4
+    wait_copies(copies[19:])
     for j in range(12):
-        extra = double_rows(spread0, wide[j, 6:18], 0)
+        extra = double_rows(spread0, v1[6 + j, 6:18], 0)
+        extra = jnp.concatenate([lanes(extra, k // 2) for k in range(Z0 // LANES)], axis=1)
         for k in range(2):
             i = 2 * j - 1 + k
             if i < 0 or i >= X0:
@@ -694,23 +800,40 @@
     sweep(v0, w0, b0, wx0, wy0, wz0, q0, 1, X0 - 1, 2)
     sweep(w0, v0, b0, wx0, wy0, wz0, q0, 2, X0 - 2, 2)
 
+    pick = collect_matrix(Z0)
+    rows = jnp.concatenate([pltpu.roll(v0[i + OX0], Y0 - OY0, 0)[0:16] for i in range(16)], axis=0)
+    solution_ref[...] = split_dot(rows, pick).reshape(16, 16, Z0)
+    copies = start_copies((solution_ref,), (solution_far,), sems, FAR_COUNT)
+
     def finish(i):
         here, total = neighbours(v0, wx0, wy0, wz0, i + OX0)
-        left = pltpu.roll(total - d0[i + OX0] * here, Y0 - OY0, 0)[0:16]
-        return [(solution_ref, i, pltpu.roll(here, Y0 - OY0, 0)[0:16]), (residual_ref, i, g_ref[i] + left)]
+        return [(residual_ref, i, pltpu.roll(total - d0[i + OX0] * here, Y0 - OY0, 0)[0:16])]
 
     loop(0, 16, finish, 2)
-
-
-def up(count_x, count_y, *operands):
+    for part in range(2):
+        here = pl.ds(8 * part, 8)
+        rows = residual_ref[here].reshape(128, Z0)
+        residual_ref[here] = g_ref[here] + split_dot(rows, pick).reshape(8, 16, Z0)
+        copies += start_copies((residual_ref.at[here],), (residual_far.at[here],), sems, FAR_COUNT + 1 + part)
+    wait_copies(copies)
+
+
+def up(count_x, count_y, everything, *operands):
     frame0, frame1, frame2 = (X0, Y0, Z0), (X1, Y1, Z1), (X2, Y2, Z2)
+    frame3, frame4 = (2 * count_x + 2, Y3, LANES), (count_x + 2, Y4, LANES)
     return call(
         functools.partial(up_kernel, count_x, count_y),
         [struct(16, 16, Z0), struct(16, 16, Z0)],
-        [vmem(*frame2)] * 3 + [vmem(*frame1)] * 9 + [vmem(Z1 // LANES, Y1, LANES)]
-        + [vmem(*frame0)] * 9 + [vmem(Z0 // LANES, Y0, LANES)],
-        24,
-    )(*operands)
+        [vmem(*operand.shape) for operand in operands]
+        + [vmem(*frame3)] * 9 + [vmem(count_x, Y3, LANES)]
+        + [vmem(*frame4)] * 6 + [vmem(count_x, Y4, LANES)] + [vmem(*frame4)] * 2 + [vmem(Y3, LANES)]
+        + [vmem(*frame2)] * 3 + [vmem(*frame1)] * 9 + [vmem(1, Y1, LANES)]
+        + [vmem(*frame0)] * 2 + [vmem(Z1 // LANES, Y0, LANES)] + [vmem(16, 16, Z0)] * 2
+        + [pltpu.SemaphoreType.DMA((FAR_COUNT + 3,))],
+        60,
+        in_specs=[WHOLE] + [FAR] * FAR_COUNT,
+        out_specs=[FAR] * 2,
+    )(everything, *operands)
 
 
 def to_next(cells, axis):
@@ -734,9 +857,10 @@
 
     to_right, to_left, c1 = begin(coefficient, right_side)
     low, high = to_next(to_right, "gx"), to_previous(to_left, "gx")
-    top, bottom = edges_y(count_x, coefficient, right_side, c1, low, high)
+    c_own, g_own = deal(coefficient, right_side)
+    top, bottom, low, high = edges_y(count_x, c_own, g_own, c1, low, high)
     below, above = to_next(top, "gy"), to_previous(bottom, "gy")
-    g1, v_own = down0(count_x, count_y, coefficient, right_side, low, high, below, above)
+    g1, v_own = down0(count_x, count_y, c_own, g_own, low, high, below, above)
 
     g1_low, g1_high = to_next(g1[2:8], "gx"), to_previous(g1[0:6], "gx")
     levels = prepare(count_x, count_y, c1, low, high, below, above)
@@ -749,11 +873,14 @@
     everything = lax.all_to_all(send3, ("gx", "gy"), split_axis=0, concat_axis=0, tiled=True)
     top, bottom = iterate_edges(count_x, v_own, own2, low2, high2)
     below2, above2 = to_next(top, "gy"), to_previous(bottom, "gy")
-    v3 = coarse(count_x, count_y, everything)
+    c_own, send3 = lax.optimization_barrier((c_own, send3))
+    weights = weights0(count_x, count_y, c_own, g_own, low, high, below, above)
+    wx0, wy0, wz0, d0, q0, b0 = weights
     return tuple(
         up(
-            count_x, count_y, v3, wx2, wy2, wz2, q2, own2, low2, high2, below2, above2, v_own, v1,
-            g1_mid, g1_below, g1_above, c1, coefficient, right_side, low, high, below, above,
+            count_x, count_y, everything, wx2, wy2, wz2, q2, own2, low2, high2, below2, above2,
+            g1_mid, g1_below, g1_above, c1, low, high, below, above, v1, v_own,
+            wx0, wy0, wz0, q0, b0, d0, right_side,
         )
     )
 

time: 91 us -> 79.8 us (0.88)
  waiting for transfers between devices: 25 us -> 19.2 us
  Pallas kernels: 30 us -> 25.8 us
    all_to_all x1, waiting for transfers between devices: 7.04 us -> 3.32 us  [shards(): lax.all_to_all(send3, ('gx', 'gy'), split_axis=0, concat_axis=0, tiled=True)]
    ppermute x6, waiting for transfers between devices: 14 us -> 11.7 us  [to_next(): lax.ppermute(cells, axis, [(i, (i + 1) % count) for i in range(count)])]
    pallas_call x1, Pallas kernels: 5.07 us -> 2.81 us  [down0(): call(functools.partial(down0_kernel, count_x, count_y), [struct(8, 8, Z1)...]
    pallas_call x1, Pallas kernels: 2.34 us -> 0.29 us  [begin(): call(begin_kernel, [struct(7, 16, Z0), struct(7, 16, Z0), struct(8, 8, Z1...]
    pallas_call x2 -> x3, Pallas kernels: 5.56 us -> 7.38 us  [the longest x1 5.61 us: weights0(): call(functools.partial(weights0_kernel, count_x, count_y), [struct(*frame...]
    pallas_call x1, Pallas kernels: 1.8 us -> 0.05 us  [iterate_edges(): call(functools.partial(iterate_edge_kernel, count_x), [struct(14, 8, Z0),...]
    all_to_all x1, starting transfers between devices: 8.62 us -> 7.59 us  [shards(): lax.all_to_all(send3, ('gx', 'gy'), split_axis=0, concat_axis=0, tiled=True)]
    unnamed x34 -> x48, local copies, waits for them, and re-layouts: 4.21 us -> 3.78 us
where the time goes in v3:
time: 79.8 us; the launch traced here: 79.5 us
  starting transfers between devices  29.8 us (37%)
  Pallas kernels  25.8 us (32%)
  waiting for transfers between devices  19.2 us (24%)
  local copies, waits for them, and re-layouts  3.79 us (5%)
  between operations  0.97 us (1%)
    ppermute x6, starting transfers between devices, to_previous(): lax.ppermute(cells, axis, [((i + 1) % count, i) for i in range(count)])  14 us
    pallas_call x1, Pallas kernels, up(): call(functools.partial(up_kernel, count_x, count_y), [struct(16, 16, Z0),...  11.9 us
    ppermute x6, waiting for transfers between devices, to_next(): lax.ppermute(cells, axis, [(i, (i + 1) % count) for i in range(count)])  11.7 us
    ppermute x6, starting transfers between devices, to_next(): lax.ppermute(cells, axis, [(i, (i + 1) % count) for i in range(count)])  8.18 us
    all_to_all x1, starting transfers between devices, shards(): lax.all_to_all(send3, ('gx', 'gy'), split_axis=0, concat_axis=0, tiled=True)  7.59 us
    pallas_call x1, Pallas kernels, weights0(): call(functools.partial(weights0_kernel, count_x, count_y), [struct(*frame...  5.61 us
    ppermute x6, waiting for transfers between devices, to_previous(): lax.ppermute(cells, axis, [((i + 1) % count, i) for i in range(count)])  4.15 us
    unnamed x48, local copies, waits for them, and re-layouts  3.78 us
  transfers between devices with their start and end apart: 13, of which 6 were waited for; matrix products, arithmetic and copies ran while one was open for 0% of the time, Pallas kernels for 10%

profile of v3, /device:TPU:1, one launch (start us, length us, event | category | flops | bytes accessed | tf_op | source)
XLA Modules:
  0.0 79.5 jit_solution(4146776603284421839)
XLA Ops:
  0.6 0.0 copy-start.5
  0.6 1.0 %copy-done.5 = f32[16,16,512]{2,1,0:T(8,128)S(1)} copy-done((f32[16,16,512]{2,1,0:T(8,128)S(1)}, f32[16,16,512]{2,1,0:T(8,128)}, u32[]{:S(2)}) %copy-start.5) | copy-done | bytes 524312
  1.7 1.0 %copy-done.8 = f32[16,16,512]{2,1,0:T(8,128)S(1)} copy-done((f32[16,16,512]{2,1,0:T(8,128)S(1)}, f32[16,16,512]{2,1,0:T(8,128)}, u32[]{:S(2)}) %copy-start.8) | copy-done | bytes 524312
  2.7 0.3 shard_map.42
  3.0 2.1 %collective-permute-start = (f32[7,16,512]{2,1,0:T(8,128)S(1)}, f32[7,16,512]{2,1,0:T(8,128)S(1)}, u32[]{:S(2)}, u32[]{:S(2)}) collective-permute-start(f32[7,16,512]{2,1,0:T(8,128)S(1)} %get-tuple-element.41), channel_id=1, source_target_pairs={{0,8},{8,16},{16,24},{24,32},{32,40},{40,48},{48,56},{56,64},{64,7... | collective-permute-start | bytes 688136 | tf_op jit(solution)/shard_map/ppermute | solution.py:841
  5.1 3.8 %collective-permute-start.1 = (f32[7,16,512]{2,1,0:T(8,128)S(1)}, f32[7,16,512]{2,1,0:T(8,128)S(1)}, u32[]{:S(2)}, u32[]{:S(2)}) collective-permute-start(f32[7,16,512]{2,1,0:T(8,128)S(1)} %get-tuple-element.42), channel_id=1, source_target_pairs={{8,0},{16,8},{24,16},{32,24},{40,32},{48,40},{56,48},{64,56},{72,6... | collective-permute-start | bytes 688136 | tf_op jit(solution)/shard_map/ppermute | solution.py:846
  8.9 1.0 %shard_map.41 = (f32[16,16,512]{2,1,0:T(8,128)S(1)}, f32[16,16,512]{2,1,0:T(8,128)S(1)}) custom-call(f32[16,16,512]{2,1,0:T(8,128)S(1)} %copy-done.8, f32[16,16,512]{2,1,0:T(8,128)S(1)} %copy-done.5), custom_call_target="tpu_custom_call" | custom-call | flops 1000000 | bytes 1000000 | tf_op jit(solution)/shard_map/pallas_call | solution.py:286
  10.0 0.0 copy-start.2
  10.0 0.0 copy-start.3
  10.0 4.1 %collective-permute-done.low_raw = f32[7,16,512]{2,1,0:T(8,128)S(1)} collective-permute-done((f32[7,16,512]{2,1,0:T(8,128)S(1)}, f32[7,16,512]{2,1,0:T(8,128)S(1)}, u32[]{:S(2)}, u32[]{:S(2)}) %collective-permute-start) | collective-permute-done | bytes 229408 | tf_op jit(solution)/shard_map/ppermute | solution.py:841
  14.1 0.0 collective-permute-done.1.high_raw
  14.1 0.7 shard_map.43
  14.9 2.8 %collective-permute-start.2 = (f32[28,8,512]{2,1,0:T(8,128)S(1)}, f32[28,8,512]{2,1,0:T(8,128)S(1)}, u32[]{:S(2)}, u32[]{:S(2)}) collective-permute-start(f32[28,8,512]{2,1,0:T(8,128)S(1)} %get-tuple-element.45), channel_id=1, source_target_pairs={{0,1},{1,2},{2,3},{3,4},{4,5},{5,6},{6,7},{7,0},{8,9},{9,10},{10,1... | collective-permute-start | bytes 1376264 | tf_op jit(solution)/shard_map/ppermute | solution.py:841
  17.7 0.0 collective-permute-start.3
  17.7 5.4 %collective-permute-done.2.below_ref.below0.rest_15_ = f32[28,8,512]{2,1,0:T(8,128)S(1)} collective-permute-done((f32[28,8,512]{2,1,0:T(8,128)S(1)}, f32[28,8,512]{2,1,0:T(8,128)S(1)}, u32[]{:S(2)}, u32[]{:S(2)}) %collective-permute-start.2) | collective-permute-done | bytes 458784 | tf_op jit(solution)/shard_map/ppermute | solution.py:841
  23.1 2.5 %collective-permute-done.3.above_ref.above0.rest_16_ = f32[28,8,512]{2,1,0:T(8,128)S(1)} collective-permute-done((f32[28,8,512]{2,1,0:T(8,128)S(1)}, f32[28,8,512]{2,1,0:T(8,128)S(1)}, u32[]{:S(2)}, u32[]{:S(2)}) %collective-permute-start.3) | collective-permute-done | bytes 458784 | tf_op jit(solution)/shard_map/ppermute | solution.py:846
  25.6 2.8 %shard_map.44 = (f32[8,8,256]{2,1,0:T(8,128)S(1)}, f32[16,16,512]{2,1,0:T(8,128)S(1)}) custom-call(f32[16,16,512]{2,1,0:T(8,128)S(1)} %get-tuple-element.67.c_ref, f32[16,16,512]{2,1,0:T(8,128)S(1)} %get-tuple-element.39.g_ref, f32[7,16,512]{2,1,0:T(8,128)S(1)} %get-tuple-element.43.low_ref.low0.rest_13_, ...), custom_call_target="tpu_custom_call" | custom-call | flops 1000000 | bytes 1000000 | tf_op jit(solution)/shard_map/pallas_call | solution.py:414
  28.5 0.1 collective-permute-start.4
  28.6 4.9 %collective-permute-start.5 = (f32[6,8,256]{2,1,0:T(8,128)S(1)}, f32[6,8,256]{2,1,0:T(8,128)S(1)}, u32[]{:S(2)}, u32[]{:S(2)}) collective-permute-start(f32[6,8,256]{2,1,0:T(8,128)S(1)} %get-tuple-element.75), channel_id=1, source_target_pairs={{8,0},{16,8},{24,16},{32,24},{40,32},{48,40},{56,48},{64,56},{72,6... | collective-permute-start | bytes 147464 | tf_op jit(solution)/shard_map/ppermute | solution.py:846
  33.5 2.1 %collective-permute-done.4 = f32[6,8,256]{2,1,0:T(8,128)S(1)} collective-permute-done((f32[6,8,256]{2,1,0:T(8,128)S(1)}, f32[6,8,256]{2,1,0:T(8,128)S(1)}, u32[]{:S(2)}, u32[]{:S(2)}) %collective-permute-start.4) | collective-permute-done | bytes 49184 | tf_op jit(solution)/shard_map/ppermute | solution.py:841
  35.6 0.0 collective-permute-done.5
  35.7 0.5 collective-permute-start.7
  36.2 1.3 %collective-permute-start.6 = (f32[20,8,256]{2,1,0:T(8,128)S(1)}, f32[20,8,256]{2,1,0:T(8,128)S(1)}, u32[]{:S(2)}, u32[]{:S(2)}) collective-permute-start(f32[20,8,256]{2,1,0:T(8,128)S(1)} %pad_maximum_fusion.mid_ref.rest_9_), channel_id=1, source_target_pairs={{0,1},{1,2},{2,3},{3,4},{4,5},{5,6},{6,7},{7,0},{8,9},{9,10},{10,1... | collective-permute-start | bytes 491528 | tf_op jit(solution)/shard_map/ppermute | solution.py:841
  37.5 0.0 copy-done.7
  37.5 1.3 %shard_map.45 = (f32[24,24,256]{2,1,0:T(8,128)S(1)}, f32[24,24,256]{2,1,0:T(8,128)S(1)}, f32[24,24,256]{2,1,0:T(8,128)S(1)}, f32[24,24,256]{2,1,0:T(8,128)S(1)},...) custom-call(f32[8,8,256]{2,1,0:T(8,128)S(1)} %get-tuple-element.40.c, ...), custom_call_target="tpu_custom_call" | custom-call | flops 1000000 | bytes 1000000 | tf_op jit(solution)/shard_map/pallas_call | solution.py:468
  38.7 0.0 copy-start.16
  38.8 0.0 copy-start.17
  38.8 0.0 copy-start.18
  38.8 0.0 copy-start.19
  38.8 1.7 %collective-permute-done.7.above_ref.rest_11_ = f32[20,8,256]{2,1,0:T(8,128)S(1)} collective-permute-done((f32[20,8,256]{2,1,0:T(8,128)S(1)}, f32[20,8,256]{2,1,0:T(8,128)S(1)}, u32[]{:S(2)}, u32[]{:S(2)}) %collective-permute-start.7) | collective-permute-done | bytes 163872 | tf_op jit(solution)/shard_map/ppermute | solution.py:846
  40.5 0.0 collective-permute-done.6.below_ref.rest_10_
  40.5 2.1 %shard_map.46 = (f32[16,24,256]{2,1,0:T(8,128)S(1)}, f32[7,8,512]{2,1,0:T(8,128)S(1)}, f32[7,8,512]{2,1,0:T(8,128)S(1)}, f32[8,512]{1,0:T(8,128)S(1)}, f32[512,128]{1,0:T(8,128)}) custom-call(f32[16,16,512]{2,1,0:T(8,128)S(1)} %get-tuple-element.47.v_own_ref.own_ref.rest_18_, f32[20,8,256]{2,1,0:T(8,128)S(1)} %pad_maximum_fusion.mid_ref.rest_9_, ...), custom_call_target="tpu_custom_call" | custom-call | flops 1000000 | bytes 1000000 | tf_op jit(solution)/shard_map/pallas_call | solution.py:544
  42.6 0.8 copy-done.15
  43.4 0.0 collective-permute-start.8
  43.4 4.8 %collective-permute-start.9 = (f32[7,8,512]{2,1,0:T(8,128)S(1)}, f32[7,8,512]{2,1,0:T(8,128)S(1)}, u32[]{:S(2)}, u32[]{:S(2)}) collective-permute-start(f32[7,8,512]{2,1,0:T(8,128)S(1)} %get-tuple-element.63), channel_id=1, source_target_pairs={{8,0},{16,8},{24,16},{32,24},{40,32},{48,40},{56,48},{64,56},{72,6... | collective-permute-start | bytes 344072 | tf_op jit(solution)/shard_map/ppermute | solution.py:846
  48.2 7.6 %all-to-all-start = ((f32[128,4,128]{2,1,0:T(4,128)}), f32[128,4,128]{2,1,0:T(4,128)S(1)}, u32[]{:S(2)}, u32[]{:S(2)}) async-start(f32[128,4,128]{2,1,0:T(4,128)} %bitcast), calls=%async_computation | async-start | bytes 524288 | tf_op jit(solution)/shard_map/all_to_all | solution.py:873
  55.8 0.0 collective-permute-done.8.low_ref.rest_5_
  55.8 0.0 collective-permute-done.9.high_ref.rest_6_
  55.9 1.9 %collective-permute-start.10 = (f32[14,8,512]{2,1,0:T(8,128)S(1)}, f32[14,8,512]{2,1,0:T(8,128)S(1)}, u32[]{:S(2)}, u32[]{:S(2)}) collective-permute-start(f32[14,8,512]{2,1,0:T(8,128)S(1)} %get-tuple-element.64), channel_id=1, source_target_pairs={{0,1},{1,2},{2,3},{3,4},{4,5},{5,6},{6,7},{7,0},{8,9},{9,10},{10,1... | collective-permute-start | bytes 688136 | tf_op jit(solution)/shard_map/ppermute | solution.py:841
  57.8 0.0 collective-permute-start.11
  57.8 5.6 %shard_map.48 = (f32[22,24,512]{2,1,0:T(8,128)}, f32[22,24,512]{2,1,0:T(8,128)}, f32[22,24,512]{2,1,0:T(8,128)}, f32[22,24,512]{2,1,0:T(8,128)}, f32[22,24,512]{2,1,0:T(8,128)}, /*index=5*/f32[22,24,512]{2,1,0:T(8,128)}) custom-call(f32[16,16,512]{2,1,0:T(8,128)} %copy-done.2, f32[16,16,512]{2,1,0:T(8,128)} %copy-done.3, f32[7,16,512]{2,1,0:T(8,128)} %copy-done.6, ...), custom_call_target="tpu_custom_call" | custom-call | flops 20000000 | bytes 20000000 | tf_op jit(solution)/shard_map/pallas_call | solution.py:604
  63.5 3.3 %all-to-all-done = f32[128,4,128]{2,1,0:T(4,128)S(1)} async-done(((f32[128,4,128]{2,1,0:T(4,128)}), f32[128,4,128]{2,1,0:T(4,128)S(1)}, u32[]{:S(2)}, u32[]{:S(2)}) %all-to-all-start) | async-done | bytes 262176 | tf_op jit(solution)/shard_map/all_to_all | solution.py:873
  66.8 0.0 collective-permute-done.10.rest_7_
  66.8 0.0 collective-permute-done.11.rest_8_
  66.8 0.7 copy-done.21
  67.5 0.1 copy-done.22
  67.6 0.1 copy-done.23
  67.7 11.9 %shard_map.49 = (f32[16,16,512]{2,1,0:T(8,128)}, f32[16,16,512]{2,1,0:T(8,128)}) custom-call(f32[512,128]{1,0:T(8,128)} %bitcast.2, f32[12,16,128]{2,1,0:T(8,128)} %copy-done.16, f32[12,16,128]{2,1,0:T(8,128)} %copy-done.17, f32[12,16,128]{2,1,0:T(8,128)} %copy-done.18, f32[12,16,128]{2,1,0:T(8,128)} %copy-done.19, f32[8,512]{1,0:T(8,128)} %copy-done.20, ...), custom_call_target="tpu_custom_call" | custom-call | flops 1000000 | bytes 1000000 | tf_op jit(solution)/shard_map/pallas_call | solution.py:824
  (39 shorter events, 0.2 us)
Async XLA Ops:
  0.6 1.0 %copy-start.5 = (f32[16,16,512]{2,1,0:T(8,128)S(1)}, f32[16,16,512]{2,1,0:T(8,128)}, u32[]{:S(2)}) copy-start(f32[16,16,512]{2,1,0:T(8,128)} %rest_25_.1) | copy-start | bytes 1572868
  1.7 1.0 %copy-start.8 = (f32[16,16,512]{2,1,0:T(8,128)S(1)}, f32[16,16,512]{2,1,0:T(8,128)}, u32[]{:S(2)}) copy-start(f32[16,16,512]{2,1,0:T(8,128)} %c_ref.3) | copy-start | bytes 1572868
  3.0 34.4 %copy-start.12 = (f32[8,8,256]{2,1,0:T(8,128)}, f32[8,8,256]{2,1,0:T(8,128)S(1)}, u32[]{:S(2)}) copy-start(f32[8,8,256]{2,1,0:T(8,128)S(1)} %get-tuple-element.40.c1_ref.rest_12_) | copy-start | bytes 196612
  3.0 11.1 %collective-permute-start = (f32[7,16,512]{2,1,0:T(8,128)S(1)}, f32[7,16,512]{2,1,0:T(8,128)S(1)}, u32[]{:S(2)}, u32[]{:S(2)}) collective-permute-start(f32[7,16,512]{2,1,0:T(8,128)S(1)} %get-tuple-element.41), channel_id=1, source_target_pairs={{0,8},{8,16},{16,24},{24,32},{32,40},{40,48},{48,56},{56,64},{64,7... | collective-permute-start | bytes 688136 | tf_op jit(solution)/shard_map/ppermute | solution.py:841
  5.1 9.0 %collective-permute-start.1 = (f32[7,16,512]{2,1,0:T(8,128)S(1)}, f32[7,16,512]{2,1,0:T(8,128)S(1)}, u32[]{:S(2)}, u32[]{:S(2)}) collective-permute-start(f32[7,16,512]{2,1,0:T(8,128)S(1)} %get-tuple-element.42), channel_id=1, source_target_pairs={{8,0},{16,8},{24,16},{32,24},{40,32},{48,40},{56,48},{64,56},{72,6... | collective-permute-start | bytes 688136 | tf_op jit(solution)/shard_map/ppermute | solution.py:846
  10.0 18.5 %copy-start.2 = (f32[16,16,512]{2,1,0:T(8,128)}, f32[16,16,512]{2,1,0:T(8,128)S(1)}, u32[]{:S(2)}) copy-start(f32[16,16,512]{2,1,0:T(8,128)S(1)} %get-tuple-element.67.c_ref) | copy-start | bytes 1572868
  10.0 18.5 %copy-start.3 = (f32[16,16,512]{2,1,0:T(8,128)}, f32[16,16,512]{2,1,0:T(8,128)S(1)}, u32[]{:S(2)}) copy-start(f32[16,16,512]{2,1,0:T(8,128)S(1)} %get-tuple-element.39.g_ref) | copy-start | bytes 1572868
  14.9 22.6 %copy-start.6 = (f32[7,16,512]{2,1,0:T(8,128)}, f32[7,16,512]{2,1,0:T(8,128)S(1)}, u32[]{:S(2)}) copy-start(f32[7,16,512]{2,1,0:T(8,128)S(1)} %get-tuple-element.43.low_ref.low0.rest_13_) | copy-start | bytes 688132
  14.9 22.6 %copy-start.7 = (f32[7,16,512]{2,1,0:T(8,128)}, f32[7,16,512]{2,1,0:T(8,128)S(1)}, u32[]{:S(2)}) copy-start(f32[7,16,512]{2,1,0:T(8,128)S(1)} %get-tuple-element.44.high_ref.high0.rest_14_) | copy-start | bytes 688132
  14.9 8.2 %collective-permute-start.2 = (f32[28,8,512]{2,1,0:T(8,128)S(1)}, f32[28,8,512]{2,1,0:T(8,128)S(1)}, u32[]{:S(2)}, u32[]{:S(2)}) collective-permute-start(f32[28,8,512]{2,1,0:T(8,128)S(1)} %get-tuple-element.45), channel_id=1, source_target_pairs={{0,1},{1,2},{2,3},{3,4},{4,5},{5,6},{6,7},{7,0},{8,9},{9,10},{10,1... | collective-permute-start | bytes 1376264 | tf_op jit(solution)/shard_map/ppermute | solution.py:841
  17.7 7.9 %collective-permute-start.3 = (f32[28,8,512]{2,1,0:T(8,128)S(1)}, f32[28,8,512]{2,1,0:T(8,128)S(1)}, u32[]{:S(2)}, u32[]{:S(2)}) collective-permute-start(f32[28,8,512]{2,1,0:T(8,128)S(1)} %get-tuple-element.46), channel_id=1, source_target_pairs={{1,0},{2,1},{3,2},{4,3},{5,4},{6,5},{7,6},{0,7},{9,8},{10,9},{11,1... | collective-permute-start | bytes 1376264 | tf_op jit(solution)/shard_map/ppermute | solution.py:846
  23.1 14.3 %copy-start = (f32[28,8,512]{2,1,0:T(8,128)}, f32[28,8,512]{2,1,0:T(8,128)S(1)}, u32[]{:S(2)}) copy-start(f32[28,8,512]{2,1,0:T(8,128)S(1)} %collective-permute-done.2.below_ref.below0.rest_15_) | copy-start | bytes 1376260
  25.6 11.8 %copy-start.1 = (f32[28,8,512]{2,1,0:T(8,128)}, f32[28,8,512]{2,1,0:T(8,128)S(1)}, u32[]{:S(2)}) copy-start(f32[28,8,512]{2,1,0:T(8,128)S(1)} %collective-permute-done.3.above_ref.above0.rest_16_) | copy-start | bytes 1376260
  28.5 27.4 %copy-start.4 = (f32[16,16,512]{2,1,0:T(8,128)}, f32[16,16,512]{2,1,0:T(8,128)S(1)}, u32[]{:S(2)}) copy-start(f32[16,16,512]{2,1,0:T(8,128)S(1)} %get-tuple-element.47.v_own_ref.own_ref.rest_18_) | copy-start | bytes 1572868
  28.5 7.1 %collective-permute-start.4 = (f32[6,8,256]{2,1,0:T(8,128)S(1)}, f32[6,8,256]{2,1,0:T(8,128)S(1)}, u32[]{:S(2)}, u32[]{:S(2)}) collective-permute-start(f32[6,8,256]{2,1,0:T(8,128)S(1)} %get-tuple-element.74), channel_id=1, source_target_pairs={{0,8},{8,16},{16,24},{24,32},{32,40},{40,48},{48,56},{56,64},{64,7... | collective-permute-start | bytes 147464 | tf_op jit(solution)/shard_map/ppermute | solution.py:841
  28.6 7.1 %collective-permute-start.5 = (f32[6,8,256]{2,1,0:T(8,128)S(1)}, f32[6,8,256]{2,1,0:T(8,128)S(1)}, u32[]{:S(2)}, u32[]{:S(2)}) collective-permute-start(f32[6,8,256]{2,1,0:T(8,128)S(1)} %get-tuple-element.75), channel_id=1, source_target_pairs={{8,0},{16,8},{24,16},{32,24},{40,32},{48,40},{56,48},{64,56},{72,6... | collective-permute-start | bytes 147464 | tf_op jit(solution)/shard_map/ppermute | solution.py:846
  35.7 6.9 %copy-start.9 = (f32[20,8,256]{2,1,0:T(8,128)}, f32[20,8,256]{2,1,0:T(8,128)S(1)}, u32[]{:S(2)}) copy-start(f32[20,8,256]{2,1,0:T(8,128)S(1)} %pad_maximum_fusion.mid_ref.rest_9_) | copy-start | bytes 491524
  35.7 4.8 %collective-permute-start.7 = (f32[20,8,256]{2,1,0:T(8,128)S(1)}, f32[20,8,256]{2,1,0:T(8,128)S(1)}, u32[]{:S(2)}, u32[]{:S(2)}) collective-permute-start(f32[20,8,256]{2,1,0:T(8,128)S(1)} %pad_maximum_fusion.mid_ref.rest_9_), channel_id=1, source_target_pairs={{1,0},{2,1},{3,2},{4,3},{5,4},{6,5},{7,6},{0,7},{9,8},{10,9},{11,1... | collective-permute-start | bytes 491528 | tf_op jit(solution)/shard_map/ppermute | solution.py:846
  36.2 4.3 %collective-permute-start.6 = (f32[20,8,256]{2,1,0:T(8,128)S(1)}, f32[20,8,256]{2,1,0:T(8,128)S(1)}, u32[]{:S(2)}, u32[]{:S(2)}) collective-permute-start(f32[20,8,256]{2,1,0:T(8,128)S(1)} %pad_maximum_fusion.mid_ref.rest_9_), channel_id=1, source_target_pairs={{0,1},{1,2},{2,3},{3,4},{4,5},{5,6},{6,7},{7,0},{8,9},{9,10},{10,1... | collective-permute-start | bytes 491528 | tf_op jit(solution)/shard_map/ppermute | solution.py:841
  38.7 3.9 %copy-start.16 = (f32[12,16,128]{2,1,0:T(8,128)}, f32[12,16,128]{2,1,0:T(8,128)S(1)}, u32[]{:S(2)}) copy-start(f32[12,16,128]{2,1,0:T(8,128)S(1)} %get-tuple-element.54.wx2.rest_0_) | copy-start | bytes 294916
  38.8 3.8 %copy-start.17 = (f32[12,16,128]{2,1,0:T(8,128)}, f32[12,16,128]{2,1,0:T(8,128)S(1)}, u32[]{:S(2)}) copy-start(f32[12,16,128]{2,1,0:T(8,128)S(1)} %get-tuple-element.55.wy2.rest_1_) | copy-start | bytes 294916
  38.8 3.8 %copy-start.18 = (f32[12,16,128]{2,1,0:T(8,128)}, f32[12,16,128]{2,1,0:T(8,128)S(1)}, u32[]{:S(2)}) copy-start(f32[12,16,128]{2,1,0:T(8,128)S(1)} %get-tuple-element.56.wz2.rest_2_) | copy-start | bytes 294916
  38.8 3.8 %copy-start.19 = (f32[12,16,128]{2,1,0:T(8,128)}, f32[12,16,128]{2,1,0:T(8,128)S(1)}, u32[]{:S(2)}) copy-start(f32[12,16,128]{2,1,0:T(8,128)S(1)} %get-tuple-element.58.q2.rest_3_) | copy-start | bytes 294916
  40.5 2.2 %copy-start.10 = (f32[20,8,256]{2,1,0:T(8,128)}, f32[20,8,256]{2,1,0:T(8,128)S(1)}, u32[]{:S(2)}) copy-start(f32[20,8,256]{2,1,0:T(8,128)S(1)} %collective-permute-done.7.above_ref.rest_11_) | copy-start | bytes 491524
  40.5 2.2 %copy-start.11 = (f32[20,8,256]{2,1,0:T(8,128)}, f32[20,8,256]{2,1,0:T(8,128)S(1)}, u32[]{:S(2)}) copy-start(f32[20,8,256]{2,1,0:T(8,128)S(1)} %collective-permute-done.6.below_ref.rest_10_) | copy-start | bytes 491524
  42.6 0.8 copy-start.15
  43.4 20.0 %copy-start.20 = (f32[8,512]{1,0:T(8,128)}, f32[8,512]{1,0:T(8,128)S(1)}, u32[]{:S(2)}) copy-start(f32[8,512]{1,0:T(8,128)S(1)} %get-tuple-element.61.own2_ref.rest_4_) | copy-start | bytes 49156
  43.4 12.4 %collective-permute-start.8 = (f32[7,8,512]{2,1,0:T(8,128)S(1)}, f32[7,8,512]{2,1,0:T(8,128)S(1)}, u32[]{:S(2)}, u32[]{:S(2)}) collective-permute-start(f32[7,8,512]{2,1,0:T(8,128)S(1)} %get-tuple-element.62), channel_id=1, source_target_pairs={{0,8},{8,16},{16,24},{24,32},{32,40},{40,48},{48,56},{56,64},{64,7... | collective-permute-start | bytes 344072 | tf_op jit(solution)/shard_map/ppermute | solution.py:841
  43.4 12.4 %collective-permute-start.9 = (f32[7,8,512]{2,1,0:T(8,128)S(1)}, f32[7,8,512]{2,1,0:T(8,128)S(1)}, u32[]{:S(2)}, u32[]{:S(2)}) collective-permute-start(f32[7,8,512]{2,1,0:T(8,128)S(1)} %get-tuple-element.63), channel_id=1, source_target_pairs={{8,0},{16,8},{24,16},{32,24},{40,32},{48,40},{56,48},{64,56},{72,6... | collective-permute-start | bytes 344072 | tf_op jit(solution)/shard_map/ppermute | solution.py:846
  48.2 18.6 %all-to-all-start = ((f32[128,4,128]{2,1,0:T(4,128)}), f32[128,4,128]{2,1,0:T(4,128)S(1)}, u32[]{:S(2)}, u32[]{:S(2)}) async-start(f32[128,4,128]{2,1,0:T(4,128)} %bitcast), calls=%async_computation | async-start | bytes 524288 | tf_op jit(solution)/shard_map/all_to_all | solution.py:873
  55.8 7.6 %copy-start.13 = (f32[7,8,512]{2,1,0:T(8,128)}, f32[7,8,512]{2,1,0:T(8,128)S(1)}, u32[]{:S(2)}) copy-start(f32[7,8,512]{2,1,0:T(8,128)S(1)} %collective-permute-done.8.low_ref.rest_5_) | copy-start | bytes 344068
  55.8 7.6 %copy-start.14 = (f32[7,8,512]{2,1,0:T(8,128)}, f32[7,8,512]{2,1,0:T(8,128)S(1)}, u32[]{:S(2)}) copy-start(f32[7,8,512]{2,1,0:T(8,128)S(1)} %collective-permute-done.9.high_ref.rest_6_) | copy-start | bytes 344068
  55.9 10.9 %collective-permute-start.10 = (f32[14,8,512]{2,1,0:T(8,128)S(1)}, f32[14,8,512]{2,1,0:T(8,128)S(1)}, u32[]{:S(2)}, u32[]{:S(2)}) collective-permute-start(f32[14,8,512]{2,1,0:T(8,128)S(1)} %get-tuple-element.64), channel_id=1, source_target_pairs={{0,1},{1,2},{2,3},{3,4},{4,5},{5,6},{6,7},{7,0},{8,9},{9,10},{10,1... | collective-permute-start | bytes 688136 | tf_op jit(solution)/shard_map/ppermute | solution.py:841
  57.8 9.0 %collective-permute-start.11 = (f32[14,8,512]{2,1,0:T(8,128)S(1)}, f32[14,8,512]{2,1,0:T(8,128)S(1)}, u32[]{:S(2)}, u32[]{:S(2)}) collective-permute-start(f32[14,8,512]{2,1,0:T(8,128)S(1)} %get-tuple-element.65), channel_id=1, source_target_pairs={{1,0},{2,1},{3,2},{4,3},{5,4},{6,5},{7,6},{0,7},{9,8},{10,9},{11,1... | collective-permute-start | bytes 688136 | tf_op jit(solution)/shard_map/ppermute | solution.py:846
  66.8 0.7 copy-start.21
  66.8 0.8 %copy-start.22 = (f32[14,8,512]{2,1,0:T(8,128)}, f32[14,8,512]{2,1,0:T(8,128)S(1)}, u32[]{:S(2)}) copy-start(f32[14,8,512]{2,1,0:T(8,128)S(1)} %collective-permute-done.10.rest_7_) | copy-start | bytes 688132
  66.8 0.9 %copy-start.23 = (f32[14,8,512]{2,1,0:T(8,128)}, f32[14,8,512]{2,1,0:T(8,128)S(1)}, u32[]{:S(2)}) copy-start(f32[14,8,512]{2,1,0:T(8,128)S(1)} %collective-permute-done.11.rest_8_) | copy-start | bytes 688132

commit v4 on v3

--- a/solution.py
+++ b/solution.py
@@ -126,10 +126,11 @@
     return guess * (2.0 - total * guess)
 
 
-def make_faces(c, wx, wy, wz, d, q, first, last, in_x, in_y, width, whole_y=0):
+def make_faces(c, wx, wy, wz, d, q, first, last, in_x, in_y, width, whole_y=0, period=0):
     rows, cells = c.shape[1], c.shape[2]
-    end_z = iota((rows, cells), 1) == cells - 1
-    start_z = iota((rows, cells), 1) == 0
+    period = period or cells
+    end_z = iota((rows, cells), 1) % period == period - 1
+    start_z = iota((rows, cells), 1) % period == 0
     row = iota((rows, cells), 0)
     wx[first - 1] = 0.5 * (c[first - 1] + c[first])
 
@@ -196,11 +197,14 @@
     return jnp.concatenate(parts, axis=1)
 
 
-def double_rows(scratch, cells, start):
-    for k in range(scratch.shape[0]):
+def double_rows(scratch, j, cells, start):
+    for k in range(scratch.shape[1]):
         for odd in range(2):
-            scratch[k, pl.ds(start + odd, cells.shape[0], stride=2), :] = lanes(cells, k)
-    return jnp.concatenate([scratch[k] for k in range(scratch.shape[0])], axis=1)
+            scratch[j, k, pl.ds(start + odd, cells.shape[0], stride=2), :] = lanes(cells, k)
+
+
+def doubled(scratch, j):
+    return [scratch[j, k] for k in range(scratch.shape[1])]
 
 
 def call(kernel, out_shape, scratch, limit, in_specs=None, out_specs=None, flops=1000000, bytes_accessed=1000000):
@@ -276,18 +280,22 @@
     )(coefficient, right_side)
 
 
-def deal_kernel(c_ref, g_ref, c_out, g_out):
+def deal_kernel(c_ref, g_ref, c_out, g_out, pick_out):
     pick = deal_matrix(Z0)
+    pick_out[...] = pick
     for ref, out in ((c_ref, c_out), (g_ref, g_out)):
         out[...] = split_dot(ref[...].reshape(256, Z0), pick).reshape(16, 16, Z0)
 
 
 def deal(coefficient, right_side):
-    return call(deal_kernel, [struct(16, 16, Z0), struct(16, 16, Z0)], [], 8)(coefficient, right_side)
-
-
-def edge_kernel(count_x, c_ref, g_ref, c1_ref, low_raw, high_raw, top_ref, bottom_ref, low_ref, high_ref):
-    pick = deal_matrix(Z0)
+    pick = jax.ShapeDtypeStruct((Z0, Z0), BF16)
+    return call(deal_kernel, [struct(16, 16, Z0), struct(16, 16, Z0), pick], [], 8)(coefficient, right_side)
+
+
+def edge_kernel(
+    count_x, pick_ref, c_ref, g_ref, c1_ref, low_raw, high_raw, top_ref, bottom_ref, low_ref, high_ref
+):
+    pick = pick_ref[...]
     for raw, out in ((low_raw, low_ref), (high_raw, high_ref)):
         out[0:5] = split_dot(raw[0:5].reshape(80, Z0), pick).reshape(5, 16, Z0)
         out[5:7] = raw[5:7]
@@ -480,9 +488,9 @@
 
 
 def down1_kernel(
-    count_x, count_y, v_own_ref, mid_ref, below_ref, above_ref,
+    count_x, count_y, mid_ref, below_ref, above_ref,
     wx1, wy1, wz1, d1, q1, wx2, wy2, wz2, d2, q2, c3_ref,
-    v_far, next_ref, previous_ref, send2_ref, send3_ref, v1_ref, b1_ref, g1, g2, b2, v2, pairs, thin,
+    v_far, send2_ref, send3_ref, v1_ref, b1_ref, g1, g2, b2, v2, pairs, thin,
 ):
     place_y = lax.axis_index("gy")
     low_y = jnp.where(place_y > 0, 1.0, 0.0).astype(F32)
@@ -514,12 +522,6 @@
     for i in range(4):
         both = jnp.where(row, pltpu.roll(v2[4 + i, 0:8, :], 4, 0), g2[4 + i, 0:8, :])
         send2_ref[:, LANES * i : LANES * i + LANES] = both
-        next_ref[6, :, LANES * i : LANES * i + LANES] = both
-        previous_ref[6, :, LANES * i : LANES * i + LANES] = both
-    for i in range(3):
-        for half in range(2):
-            next_ref[2 * i + half] = v_own_ref[13 + i, 8 * half : 8 * half + 8, :]
-            previous_ref[2 * i + half] = v_own_ref[i, 8 * half : 8 * half + 8, :]
     halves = [
         defect(v2, g2, wx2, wy2, wz2, d2, 4 + 2 * i) + defect(v2, g2, wx2, wy2, wz2, d2, 5 + 2 * i)
         for i in range(2)
@@ -543,11 +545,24 @@
     frame1, frame2 = (X1, Y1, Z1), (X2, Y2, Z2)
     return call(
         functools.partial(down1_kernel, count_x, count_y),
-        [struct(16, Y1, Z1), struct(7, 8, Z0), struct(7, 8, Z0), struct(8, Z0)]
+        [struct(16, Y1, Z1), struct(8, Z0)]
         + [struct(4 * count_x * count_y, LANES)],
         [vmem(*frame1)] * 3 + [vmem(*frame2)] * 3 + [vmem(8, Z1 // LANES, Y1, LANES), vmem(32, LANES)],
         8,
     )(*operands)
+
+
+def iterate_side_kernel(own_ref, own2_ref, next_ref, previous_ref):
+    for i in range(3):
+        for half in range(2):
+            next_ref[2 * i + half] = own_ref[13 + i, 8 * half : 8 * half + 8, :]
+            previous_ref[2 * i + half] = own_ref[i, 8 * half : 8 * half + 8, :]
+    next_ref[6] = own2_ref[...]
+    previous_ref[6] = own2_ref[...]
+
+
+def iterate_sides(*operands):
+    return call(iterate_side_kernel, [struct(7, 8, Z0), struct(7, 8, Z0)], [], 8)(*operands)
 
 
 def iterate_edge_kernel(count_x, own_ref, own2_ref, low_ref, high_ref, top_ref, bottom_ref):
@@ -613,95 +628,108 @@
     )(*operands)
 
 
+def join_halves(frame, count):
+    first = iota(frame.shape[1:], 1) < 64
+    frame[0] = jnp.where(first, 0.0, pltpu.roll(frame[count], 64, 1))
+    frame[count + 1] = jnp.where(first, pltpu.roll(frame[1], 64, 1), 0.0)
+
+
+def halves_matrix(of_fine):
+    fine, coarse = iota((LANES, LANES), of_fine), iota((LANES, LANES), 1 - of_fine)
+    hit = jnp.logical_and(fine // 64 == coarse // 64, (fine % 64) // 2 == coarse % 64)
+    return hit.astype(F32).astype(BF16)
+
+
 def solve_coarse(
     count_x, count_y, all_ref, v3,
     c3, wx3, wy3, wz3, d3, q3, b3, w3, thin3,
-    c4, wx4, wy4, wz4, d4, q4, g4, v4, w4, thin4,
+    c4, wx4, wy4, wz4, d4, q4, g4, v4, thin4,
 ):
-    n3, n4 = 2 * count_x, count_x
-
-    c3[...] = jnp.zeros(c3.shape, F32)
-    b3[...] = jnp.zeros(b3.shape, F32)
-    v3[...] = jnp.zeros(v3.shape, F32)
-    w3[...] = jnp.zeros(w3.shape, F32)
-    lane = iota((count_y, LANES), 1) < 64
-    for i in range(n3):
-        base = (i // 2) * count_y * 4 + 2 * (i % 2)
+    h3, h4 = count_x, count_x // 2
+
+    if 2 * count_y < Y3:
+        c3[...] = jnp.zeros(c3.shape, F32)
+        b3[...] = jnp.zeros(b3.shape, F32)
+    first = iota((count_y, LANES), 1) < 64
+    for i in range(h3):
         for j in range(2):
-            part = all_ref[pl.ds(base + j, count_y, stride=4), :]
-            b3[1 + i, pl.ds(j, count_y, stride=2), :] = jnp.where(lane, part, 0.0)
-            c3[1 + i, pl.ds(j, count_y, stride=2), :] = jnp.where(lane, pltpu.roll(part, 64, 1), 0.0)
-    in_y = jnp.logical_and(iota((Y3, LANES), 0) < 2 * count_y, iota((Y3, LANES), 1) < 64).astype(F32)
-    make_faces(c3, wx3, wy3, wz3, d3, q3, 1, n3 + 1, lambda i: 1.0, in_y, 8, whole_y=1)
+            parts = []
+            for x in (i, i + h3):
+                base = (x // 2) * count_y * 4 + 2 * (x % 2)
+                parts.append(all_ref[pl.ds(base + j, count_y, stride=4), :])
+            rows = pl.ds(j, count_y, stride=2)
+            b3[1 + i, rows, :] = jnp.where(first, parts[0], pltpu.roll(parts[1], 64, 1))
+            c3[1 + i, rows, :] = jnp.where(first, pltpu.roll(parts[0], 64, 1), parts[1])
+    join_halves(c3, h3)
+    in_y = (iota((Y3, LANES), 0) < 2 * count_y).astype(F32)
+    make_faces(c3, wx3, wy3, wz3, d3, q3, 1, h3 + 1, lambda i: 1.0, in_y, min(8, h3), whole_y=1, period=64)
 
     def begin3(i):
         return [(v3, i, q3[i] * b3[i])]
 
-    loop(1, n3 + 1, begin3, 8)
+    loop(1, h3 + 1, begin3, h3)
+    join_halves(v3, h3)
 
     def sweep3(i):
         here, total = neighbours(v3, wx3, wy3, wz3, i)
         return [(w3, i, 0.2 * here + q3[i] * (b3[i] + total))]
 
-    loop(1, n3 + 1, sweep3, 16)
+    loop(1, h3 + 1, sweep3, h3)
+    join_halves(w3, h3)
 
     def restrict3(j):
         i = 2 * j + 1
         both = defect(w3, b3, wx3, wy3, wz3, d3, i) + defect(w3, b3, wx3, wy3, wz3, d3, i + 1)
-        return [(thin3, j, both)]
-
-    loop(0, n4, restrict3, 4)
-    valid = iota((Y4, LANES), 0) < count_y
+        return [(thin3, j, both), (thin3, h4 + j, c3[i] + c3[i + 1])]
+
+    loop(0, h4, restrict3, min(4, h4))
     rows = jnp.concatenate(
-        [thin3[i, pl.ds(0, Y4, stride=2), :] + thin3[i, pl.ds(1, Y4, stride=2), :] for i in range(n4)], axis=0
+        [thin3[i, pl.ds(0, Y4, stride=2), :] + thin3[i, pl.ds(1, Y4, stride=2), :] for i in range(2 * h4)], axis=0
     )
-    pick = pair_sum_matrix(LANES, LANES)
-    g4[...] = (0.5 * split_dot(rows, pick)).reshape(n4, Y4, LANES)
-    for i in range(n4):
-        thin3[i] = c3[2 * i + 1] + c3[2 * i + 2]
-    rows = jnp.concatenate(
-        [thin3[i, pl.ds(0, Y4, stride=2), :] + thin3[i, pl.ds(1, Y4, stride=2), :] for i in range(n4)], axis=0
-    )
-    c4[...] = jnp.zeros(c4.shape, F32)
-    c4[1 : n4 + 1] = (0.125 * split_dot(rows, pick)).reshape(n4, Y4, LANES)
-    in_y = jnp.logical_and(valid, iota((Y4, LANES), 1) < 32).astype(F32)
-    make_faces(c4, wx4, wy4, wz4, d4, q4, 1, n4 + 1, lambda i: 1.0, in_y, n4, whole_y=1)
-    v4[...] = jnp.zeros(v4.shape, F32)
-    w4[...] = jnp.zeros(w4.shape, F32)
-    for i in range(n4):
-        g4[i] = q4[1 + i] * g4[i]
-        v4[1 + i] = g4[i]
-
-    def bottom(source, target):
-        def body(i):
-            here, total = neighbours(source, wx4, wy4, wz4, 1 + i)
-            return [(target, 1 + i, (0.2 * here + g4[i]) + q4[1 + i] * total)]
-
-        loop(0, n4, body, n4)
-
-    def two(step):
-        bottom(v4, w4)
-        bottom(w4, v4)
-        return []
-
-    loop(0, (BOTTOM - 2) // 2, two)
-    bottom(v4, w4)
-
-    wide = split_dot(w4[1 : n4 + 1].reshape(n4 * Y4, LANES), copy_matrix(LANES, LANES)).reshape(n4, Y4, LANES)
-    for i in range(n4):
-        thin4[pl.ds(0, Y4, stride=2), :] = wide[i]
-        thin4[pl.ds(1, Y4, stride=2), :] = wide[i]
-        extra = thin4[...]
+    both = split_dot(rows, halves_matrix(0)).reshape(2 * h4, Y4, LANES)
+    g4[...] = 0.5 * both[:h4]
+    c4[1 : h4 + 1] = 0.125 * both[h4:]
+    join_halves(c4, h4)
+    in_y = jnp.logical_and(iota((Y4, LANES), 0) < count_y, iota((Y4, LANES), 1) % 64 < 32).astype(F32)
+    make_faces(c4, wx4, wy4, wz4, d4, q4, 1, h4 + 1, lambda i: 1.0, in_y, h4, whole_y=1, period=64)
+
+    along_x = [wx4[i] for i in range(h4 + 1)]
+    along_y, along_z = [wy4[1 + i] for i in range(h4)], [wz4[1 + i] for i in range(h4)]
+    scale = [q4[1 + i] for i in range(h4)]
+    start = [scale[i] * g4[i] for i in range(h4)]
+    first = iota((Y4, LANES), 1) < 64
+
+    def bottom(step, v):
+        before = jnp.where(first, 0.0, pltpu.roll(v[-1], 64, 1))
+        after = jnp.where(first, pltpu.roll(v[0], 64, 1), 0.0)
+        padded = (before, *v, after)
+        out = []
+        for i, here in enumerate(v):
+            total = along_x[i + 1] * padded[i + 2] + along_x[i] * padded[i]
+            total += along_y[i] * up_of(here, 0) + down_of(along_y[i] * here, 0)
+            total += along_z[i] * up_of(here, 1) + down_of(along_z[i] * here, 1)
+            out.append((0.2 * here + start[i]) + scale[i] * total)
+        return tuple(out)
+
+    final = lax.fori_loop(0, BOTTOM - 1, bottom, tuple(start))
+
+    wide = split_dot(jnp.concatenate(final, axis=0), halves_matrix(1)).reshape(h4, Y4, LANES)
+    for i in range(h4):
+        thin4[i, pl.ds(0, Y4, stride=2), :] = wide[i]
+        thin4[i, pl.ds(1, Y4, stride=2), :] = wide[i]
+    for i in range(h4):
+        extra = thin4[i]
         v3[1 + 2 * i] = w3[1 + 2 * i] + extra
         v3[2 + 2 * i] = w3[2 + 2 * i] + extra
-
-    loop(1, n3 + 1, sweep3, 8)
+    join_halves(v3, h3)
+    loop(1, h3 + 1, sweep3, h3)
+    join_halves(w3, h3)
 
     def sweep3_again(i):
         here, total = neighbours(w3, wx3, wy3, wz3, i)
         return [(v3, i, 0.2 * here + q3[i] * (b3[i] + total))]
 
-    loop(1, n3 + 1, sweep3_again, 16)
+    loop(1, h3 + 1, sweep3_again, h3)
 
 
 def up_kernel(
@@ -711,7 +739,7 @@
     far, rest = rest[:FAR_COUNT], rest[FAR_COUNT:]
     solution_far, residual_far = rest[:2]
     near, rest = rest[2 : 2 + FAR_COUNT], rest[2 + FAR_COUNT :]
-    grids, rest = rest[:20], rest[20:]
+    grids, rest = rest[:19], rest[19:]
     v2, w2, b2, v1, b1, c1, wx1, wy1, wz1, d1, q1, w1, spread1 = rest[:13]
     v0, w0, spread0, solution_ref, residual_ref, sems = rest[13:]
     (wx2, wy2, wz2, q2, own2, low_ref, high_ref, below_ref, above_ref,
@@ -722,7 +750,7 @@
     solve_coarse(count_x, count_y, all_ref, *grids)
     wait_copies(copies[:19])
     place_x, place_y = lax.axis_index("gx"), lax.axis_index("gy")
-    n3 = 2 * count_x
+    n3, h3 = 2 * count_x, count_x
     sides = ends("gx", count_x) + ends("gy", count_y)
     first, last, low_y, high_y = sides
 
@@ -741,13 +769,16 @@
     slabs = []
     for j in range(6):
         at = 2 * place_x - 2 + j
-        slabs.append(v3[1 + jnp.clip(at, 0, n3 - 1)] * flag(at, n3))
+        cells = v3[1 + jnp.clip(at - jnp.where(at < h3, 0, h3), 0, h3 - 1)]
+        slabs.append(cells * flag(at, h3) + pltpu.roll(cells, 64, 1) * flag(at - h3, h3))
     wide = split_dot(jnp.concatenate(slabs, axis=0), copy_matrix(LANES, LANES))
     target, origin = iota((Y2, Y3), 0), iota((Y2, Y3), 1)
     rows = jnp.logical_and(origin == 2 * place_y - 2 + target // 2, target < 12).astype(F32).astype(BF16)
     half = iota((8, Z2), 0) < 4
+    wide = jnp.concatenate([wide[Y3 * j : Y3 * j + Y3] for j in range(6)], axis=1)
+    wide = split_dot_left(rows, wide)
     for j in range(6):
-        extra = split_dot_left(rows, wide[Y3 * j : Y3 * j + Y3])
+        extra = lanes(wide, j)
         for k in range(2):
             i = 2 * j + k
             at = slice(LANES * (i % 4), LANES * (i % 4) + LANES)
@@ -765,8 +796,10 @@
 
     spread1[...] = jnp.zeros(spread1.shape, F32)
     for j in range(8):
-        extra = double_rows(spread1, v2[2 + j, 2:10], 4)
-        extra = jnp.concatenate([extra, extra], axis=1)
+        double_rows(spread1, j, v2[2 + j, 2:10], 4)
+    for j in range(8):
+        extra = doubled(spread1, j)
+        extra = jnp.concatenate([extra[0], extra[0]], axis=1)
         for k in range(2):
             i = 4 + 2 * j + k
             v1[i] = v1_ref[i - 4] + extra
@@ -776,8 +809,10 @@
     half = iota((8, Z0), 0) < 4
     wait_copies(copies[19:])
     for j in range(12):
-        extra = double_rows(spread0, v1[6 + j, 6:18], 0)
-        extra = jnp.concatenate([lanes(extra, k // 2) for k in range(Z0 // LANES)], axis=1)
+        double_rows(spread0, j, v1[6 + j, 6:18], 0)
+    for j in range(12):
+        extra = doubled(spread0, j)
+        extra = jnp.concatenate([extra[k // 2] for k in range(Z0 // LANES)], axis=1)
         for k in range(2):
             i = 2 * j - 1 + k
             if i < 0 or i >= X0:
@@ -820,15 +855,15 @@
 
 def up(count_x, count_y, everything, *operands):
     frame0, frame1, frame2 = (X0, Y0, Z0), (X1, Y1, Z1), (X2, Y2, Z2)
-    frame3, frame4 = (2 * count_x + 2, Y3, LANES), (count_x + 2, Y4, LANES)
+    frame3, frame4 = (count_x + 2, Y3, LANES), (count_x // 2 + 2, Y4, LANES)
     return call(
         functools.partial(up_kernel, count_x, count_y),
         [struct(16, 16, Z0), struct(16, 16, Z0)],
         [vmem(*operand.shape) for operand in operands]
         + [vmem(*frame3)] * 9 + [vmem(count_x, Y3, LANES)]
-        + [vmem(*frame4)] * 6 + [vmem(count_x, Y4, LANES)] + [vmem(*frame4)] * 2 + [vmem(Y3, LANES)]
-        + [vmem(*frame2)] * 3 + [vmem(*frame1)] * 9 + [vmem(1, Y1, LANES)]
-        + [vmem(*frame0)] * 2 + [vmem(Z1 // LANES, Y0, LANES)] + [vmem(16, 16, Z0)] * 2
+        + [vmem(*frame4)] * 6 + [vmem(count_x // 2, Y4, LANES), vmem(*frame4), vmem(count_x // 2, Y3, LANES)]
+        + [vmem(*frame2)] * 3 + [vmem(*frame1)] * 9 + [vmem(8, 1, Y1, LANES)]
+        + [vmem(*frame0)] * 2 + [vmem(12, Z1 // LANES, Y0, LANES)] + [vmem(16, 16, Z0)] * 2
         + [pltpu.SemaphoreType.DMA((FAR_COUNT + 3,))],
         60,
         in_specs=[WHOLE] + [FAR] * FAR_COUNT,
@@ -857,8 +892,8 @@
 
     to_right, to_left, c1 = begin(coefficient, right_side)
     low, high = to_next(to_right, "gx"), to_previous(to_left, "gx")
-    c_own, g_own = deal(coefficient, right_side)
-    top, bottom, low, high = edges_y(count_x, c_own, g_own, c1, low, high)
+    c_own, g_own, pick = deal(coefficient, right_side)
+    top, bottom, low, high = edges_y(count_x, pick, c_own, g_own, c1, low, high)
     below, above = to_next(top, "gy"), to_previous(bottom, "gy")
     g1, v_own = down0(count_x, count_y, c_own, g_own, low, high, below, above)
 
@@ -867,10 +902,11 @@
     wx2, wy2, wz2, q2 = levels[5], levels[6], levels[7], levels[9]
     g1_mid = with_sides(g1_low, g1, g1_high)
     g1_below, g1_above = to_next(g1_mid, "gy"), to_previous(g1_mid, "gy")
-    v1, to_right, to_left, own2, send3 = down1(count_x, count_y, v_own, g1_mid, g1_below, g1_above, *levels)
-
+    v1, own2, send3 = down1(count_x, count_y, g1_mid, g1_below, g1_above, *levels)
+
+    everything = lax.all_to_all(send3, ("gx", "gy"), split_axis=0, concat_axis=0, tiled=True)
+    to_right, to_left = iterate_sides(v_own, own2)
     low2, high2 = to_next(to_right, "gx"), to_previous(to_left, "gx")
-    everything = lax.all_to_all(send3, ("gx", "gy"), split_axis=0, concat_axis=0, tiled=True)
     top, bottom = iterate_edges(count_x, v_own, own2, low2, high2)
     below2, above2 = to_next(top, "gy"), to_previous(bottom, "gy")
     c_own, send3 = lax.optimization_barrier((c_own, send3))

time: 79.8 us -> 77.7 us (0.974)
  Pallas kernels: 25.8 us -> 24.4 us
    pallas_call x1, Pallas kernels: 11.9 us -> 10.5 us  [up(): call(functools.partial(up_kernel, count_x, count_y), [struct(16, 16, Z0),...]
where the time goes in v4:
time: 77.7 us; the launch traced here: 77.4 us
  starting transfers between devices  29.8 us (38%)
  Pallas kernels  24.4 us (31%)
  waiting for transfers between devices  19.1 us (25%)
  local copies, waits for them, and re-layouts  3.02 us (4%)
  between operations  1 us (1%)
    ppermute x6, starting transfers between devices, to_previous(): lax.ppermute(cells, axis, [((i + 1) % count, i) for i in range(count)])  14 us
    ppermute x6, waiting for transfers between devices, to_next(): lax.ppermute(cells, axis, [(i, (i + 1) % count) for i in range(count)])  11.7 us
    pallas_call x1, Pallas kernels, up(): call(functools.partial(up_kernel, count_x, count_y), [struct(16, 16, Z0),...  10.5 us
    ppermute x6, starting transfers between devices, to_next(): lax.ppermute(cells, axis, [(i, (i + 1) % count) for i in range(count)])  8.25 us
    all_to_all x1, starting transfers between devices, shards(): lax.all_to_all(send3, ('gx', 'gy'), split_axis=0, concat_axis=0, tiled=True)  7.59 us
    pallas_call x1, Pallas kernels, weights0(): call(functools.partial(weights0_kernel, count_x, count_y), [struct(*frame...  5.6 us
    ppermute x6, waiting for transfers between devices, to_previous(): lax.ppermute(cells, axis, [((i + 1) % count, i) for i in range(count)])  4.15 us
    all_to_all x1, waiting for transfers between devices, shards(): lax.all_to_all(send3, ('gx', 'gy'), split_axis=0, concat_axis=0, tiled=True)  3.31 us
  transfers between devices with their start and end apart: 13, of which 6 were waited for; matrix products, arithmetic and copies ran while one was open for 0% of the time, Pallas kernels for 10%

profile of v4, /device:TPU:1, one launch (start us, length us, event | category | flops | bytes accessed | tf_op | source)
XLA Modules:
  0.0 77.4 jit_solution(14497928387572738789)
XLA Ops:
  0.6 0.0 copy-start.2
  0.6 1.0 %copy-done.2 = f32[16,16,512]{2,1,0:T(8,128)S(1)} copy-done((f32[16,16,512]{2,1,0:T(8,128)S(1)}, f32[16,16,512]{2,1,0:T(8,128)}, u32[]{:S(2)}) %copy-start.2) | copy-done | bytes 524312
  1.7 1.0 %copy-done.8 = f32[16,16,512]{2,1,0:T(8,128)S(1)} copy-done((f32[16,16,512]{2,1,0:T(8,128)S(1)}, f32[16,16,512]{2,1,0:T(8,128)}, u32[]{:S(2)}) %copy-start.8) | copy-done | bytes 524312
  2.7 0.3 shard_map.42
  3.0 2.1 %collective-permute-start = (f32[7,16,512]{2,1,0:T(8,128)S(1)}, f32[7,16,512]{2,1,0:T(8,128)S(1)}, u32[]{:S(2)}, u32[]{:S(2)}) collective-permute-start(f32[7,16,512]{2,1,0:T(8,128)S(1)} %get-tuple-element.43), channel_id=1, source_target_pairs={{0,8},{8,16},{16,24},{24,32},{32,40},{40,48},{48,56},{56,64},{64,7... | collective-permute-start | bytes 688136 | tf_op jit(solution)/shard_map/ppermute | solution.py:876
  5.1 3.8 %collective-permute-start.1 = (f32[7,16,512]{2,1,0:T(8,128)S(1)}, f32[7,16,512]{2,1,0:T(8,128)S(1)}, u32[]{:S(2)}, u32[]{:S(2)}) collective-permute-start(f32[7,16,512]{2,1,0:T(8,128)S(1)} %get-tuple-element.44), channel_id=1, source_target_pairs={{8,0},{16,8},{24,16},{32,24},{40,32},{48,40},{56,48},{64,56},{72,6... | collective-permute-start | bytes 688136 | tf_op jit(solution)/shard_map/ppermute | solution.py:881
  8.9 1.1 %shard_map.41 = (f32[16,16,512]{2,1,0:T(8,128)S(1)}, f32[16,16,512]{2,1,0:T(8,128)S(1)}, bf16[512,512]{1,0:T(8,128)(2,1)S(1)}) custom-call(f32[16,16,512]{2,1,0:T(8,128)S(1)} %copy-done.8, f32[16,16,512]{2,1,0:T(8,128)S(1)} %copy-done.2), custom_call_target="tpu_custom_call" | custom-call | flops 1000000 | bytes 1000000 | tf_op jit(solution)/shard_map/pallas_call | solution.py:292
  10.0 0.0 copy-start.3
  10.0 0.0 copy-start.4
  10.0 4.1 %collective-permute-done.low_raw = f32[7,16,512]{2,1,0:T(8,128)S(1)} collective-permute-done((f32[7,16,512]{2,1,0:T(8,128)S(1)}, f32[7,16,512]{2,1,0:T(8,128)S(1)}, u32[]{:S(2)}, u32[]{:S(2)}) %collective-permute-start) | collective-permute-done | bytes 229408 | tf_op jit(solution)/shard_map/ppermute | solution.py:876
  14.1 0.0 collective-permute-done.1.high_raw
  14.1 0.7 shard_map.43
  14.8 2.8 %collective-permute-start.2 = (f32[28,8,512]{2,1,0:T(8,128)S(1)}, f32[28,8,512]{2,1,0:T(8,128)S(1)}, u32[]{:S(2)}, u32[]{:S(2)}) collective-permute-start(f32[28,8,512]{2,1,0:T(8,128)S(1)} %get-tuple-element.47), channel_id=1, source_target_pairs={{0,1},{1,2},{2,3},{3,4},{4,5},{5,6},{6,7},{7,0},{8,9},{9,10},{10,1... | collective-permute-start | bytes 1376264 | tf_op jit(solution)/shard_map/ppermute | solution.py:876
  17.7 0.0 collective-permute-start.3
  17.7 5.4 %collective-permute-done.2.below_ref.below0.rest_15_ = f32[28,8,512]{2,1,0:T(8,128)S(1)} collective-permute-done((f32[28,8,512]{2,1,0:T(8,128)S(1)}, f32[28,8,512]{2,1,0:T(8,128)S(1)}, u32[]{:S(2)}, u32[]{:S(2)}) %collective-permute-start.2) | collective-permute-done | bytes 458784 | tf_op jit(solution)/shard_map/ppermute | solution.py:876
  23.1 2.5 %collective-permute-done.3.above_ref.above0.rest_16_ = f32[28,8,512]{2,1,0:T(8,128)S(1)} collective-permute-done((f32[28,8,512]{2,1,0:T(8,128)S(1)}, f32[28,8,512]{2,1,0:T(8,128)S(1)}, u32[]{:S(2)}, u32[]{:S(2)}) %collective-permute-start.3) | collective-permute-done | bytes 458784 | tf_op jit(solution)/shard_map/ppermute | solution.py:881
  25.6 2.8 %shard_map.44 = (f32[8,8,256]{2,1,0:T(8,128)S(1)}, f32[16,16,512]{2,1,0:T(8,128)S(1)}) custom-call(f32[16,16,512]{2,1,0:T(8,128)S(1)} %get-tuple-element.69.c_ref, f32[16,16,512]{2,1,0:T(8,128)S(1)} %get-tuple-element.40.g_ref, f32[7,16,512]{2,1,0:T(8,128)S(1)} %get-tuple-element.45.low_ref.low0.rest_13_, ...), custom_call_target="tpu_custom_call" | custom-call | flops 1000000 | bytes 1000000 | tf_op jit(solution)/shard_map/pallas_call | solution.py:422
  28.4 0.1 collective-permute-start.4
  28.5 4.9 %collective-permute-start.5 = (f32[6,8,256]{2,1,0:T(8,128)S(1)}, f32[6,8,256]{2,1,0:T(8,128)S(1)}, u32[]{:S(2)}, u32[]{:S(2)}) collective-permute-start(f32[6,8,256]{2,1,0:T(8,128)S(1)} %get-tuple-element.77), channel_id=1, source_target_pairs={{8,0},{16,8},{24,16},{32,24},{40,32},{48,40},{56,48},{64,56},{72,6... | collective-permute-start | bytes 147464 | tf_op jit(solution)/shard_map/ppermute | solution.py:881
  33.4 2.1 %collective-permute-done.4 = f32[6,8,256]{2,1,0:T(8,128)S(1)} collective-permute-done((f32[6,8,256]{2,1,0:T(8,128)S(1)}, f32[6,8,256]{2,1,0:T(8,128)S(1)}, u32[]{:S(2)}, u32[]{:S(2)}) %collective-permute-start.4) | collective-permute-done | bytes 49184 | tf_op jit(solution)/shard_map/ppermute | solution.py:876
  35.6 0.0 collective-permute-done.5
  35.6 0.5 collective-permute-start.7
  36.1 1.3 %collective-permute-start.6 = (f32[20,8,256]{2,1,0:T(8,128)S(1)}, f32[20,8,256]{2,1,0:T(8,128)S(1)}, u32[]{:S(2)}, u32[]{:S(2)}) collective-permute-start(f32[20,8,256]{2,1,0:T(8,128)S(1)} %pad_maximum_fusion.mid_ref.rest_9_), channel_id=1, source_target_pairs={{0,1},{1,2},{2,3},{3,4},{4,5},{5,6},{6,7},{7,0},{8,9},{9,10},{10,1... | collective-permute-start | bytes 491528 | tf_op jit(solution)/shard_map/ppermute | solution.py:876
  37.4 0.0 copy-done.6
  37.4 0.0 copy-done
  37.4 1.3 %shard_map.45 = (f32[24,24,256]{2,1,0:T(8,128)S(1)}, f32[24,24,256]{2,1,0:T(8,128)S(1)}, f32[24,24,256]{2,1,0:T(8,128)S(1)}, f32[24,24,256]{2,1,0:T(8,128)S(1)},...) custom-call(f32[8,8,256]{2,1,0:T(8,128)S(1)} %get-tuple-element.42.c, ...), custom_call_target="tpu_custom_call" | custom-call | flops 1000000 | bytes 1000000 | tf_op jit(solution)/shard_map/pallas_call | solution.py:476
  38.7 1.7 %collective-permute-done.7.above_ref.rest_11_ = f32[20,8,256]{2,1,0:T(8,128)S(1)} collective-permute-done((f32[20,8,256]{2,1,0:T(8,128)S(1)}, f32[20,8,256]{2,1,0:T(8,128)S(1)}, u32[]{:S(2)}, u32[]{:S(2)}) %collective-permute-start.7) | collective-permute-done | bytes 163872 | tf_op jit(solution)/shard_map/ppermute | solution.py:881
  40.4 0.0 collective-permute-done.6.below_ref.rest_10_
  40.4 2.1 %shard_map.46 = (f32[16,24,256]{2,1,0:T(8,128)S(1)}, f32[8,512]{1,0:T(8,128)S(1)}, f32[512,128]{1,0:T(8,128)}) custom-call(f32[20,8,256]{2,1,0:T(8,128)S(1)} %pad_maximum_fusion.mid_ref.rest_9_, f32[20,8,256]{2,1,0:T(8,128)S(1)} %collective-permute-done.6.below_ref.rest_10_, f32[20,8,256]{2,1,0:T(8,128)S(1)} %collective-permute-done.7.above_ref.rest_11_, ...), custom_call_target="tpu_custom_call" | custom-call | flops 1000000 | bytes 1000000 | tf_op jit(solution)/shard_map/pallas_call | solution.py:546
  42.5 0.0 copy-done.18
  42.5 0.0 copy-done.19
  42.5 0.0 copy-done.10
  42.6 0.0 copy-done.11
  42.6 0.1 collective-permute-start.8
  42.7 4.8 %collective-permute-start.9 = (f32[7,8,512]{2,1,0:T(8,128)S(1)}, f32[7,8,512]{2,1,0:T(8,128)S(1)}, u32[]{:S(2)}, u32[]{:S(2)}) collective-permute-start(f32[7,8,512]{2,1,0:T(8,128)S(1)} %get-tuple-element.65), channel_id=1, source_target_pairs={{8,0},{16,8},{24,16},{32,24},{40,32},{48,40},{56,48},{64,56},{72,6... | collective-permute-start | bytes 344072 | tf_op jit(solution)/shard_map/ppermute | solution.py:881
  47.5 7.6 %all-to-all-start = ((f32[128,4,128]{2,1,0:T(4,128)}), f32[128,4,128]{2,1,0:T(4,128)S(1)}, u32[]{:S(2)}, u32[]{:S(2)}) async-start(f32[128,4,128]{2,1,0:T(4,128)} %bitcast), calls=%async_computation | async-start | bytes 524288 | tf_op jit(solution)/shard_map/all_to_all | solution.py:907
  55.1 0.0 collective-permute-done.8.low_ref.rest_5_
  55.1 0.0 collective-permute-done.9.high_ref.rest_6_
  55.2 1.9 %collective-permute-start.10 = (f32[14,8,512]{2,1,0:T(8,128)S(1)}, f32[14,8,512]{2,1,0:T(8,128)S(1)}, u32[]{:S(2)}, u32[]{:S(2)}) collective-permute-start(f32[14,8,512]{2,1,0:T(8,128)S(1)} %get-tuple-element.66), channel_id=1, source_target_pairs={{0,1},{1,2},{2,3},{3,4},{4,5},{5,6},{6,7},{7,0},{8,9},{9,10},{10,1... | collective-permute-start | bytes 688136 | tf_op jit(solution)/shard_map/ppermute | solution.py:876
  57.1 0.0 collective-permute-start.11
  57.1 5.6 %shard_map.49 = (f32[22,24,512]{2,1,0:T(8,128)}, f32[22,24,512]{2,1,0:T(8,128)}, f32[22,24,512]{2,1,0:T(8,128)}, f32[22,24,512]{2,1,0:T(8,128)}, f32[22,24,512]{2,1,0:T(8,128)}, /*index=5*/f32[22,24,512]{2,1,0:T(8,128)}) custom-call(f32[16,16,512]{2,1,0:T(8,128)} %copy-done.3, f32[16,16,512]{2,1,0:T(8,128)} %copy-done.4, f32[7,16,512]{2,1,0:T(8,128)} %copy-done.6, ...), custom_call_target="tpu_custom_call" | custom-call | flops 20000000 | bytes 20000000 | tf_op jit(solution)/shard_map/pallas_call | solution.py:619
  62.7 3.3 %all-to-all-done = f32[128,4,128]{2,1,0:T(4,128)S(1)} async-done(((f32[128,4,128]{2,1,0:T(4,128)}), f32[128,4,128]{2,1,0:T(4,128)S(1)}, u32[]{:S(2)}, u32[]{:S(2)}) %all-to-all-start) | async-done | bytes 262176 | tf_op jit(solution)/shard_map/all_to_all | solution.py:907
  66.0 0.0 collective-permute-done.10.rest_7_
  66.0 0.0 collective-permute-done.11.rest_8_
  66.1 0.7 copy-done.21
  66.8 0.1 copy-done.22
  66.8 0.1 copy-done.23
  66.9 10.5 %shard_map.50 = (f32[16,16,512]{2,1,0:T(8,128)}, f32[16,16,512]{2,1,0:T(8,128)}) custom-call(f32[512,128]{1,0:T(8,128)} %bitcast.2, f32[12,16,128]{2,1,0:T(8,128)} %copy-done.16, f32[12,16,128]{2,1,0:T(8,128)} %copy-done.17, f32[12,16,128]{2,1,0:T(8,128)} %copy-done.18, f32[12,16,128]{2,1,0:T(8,128)} %copy-done.19, f32[8,512]{1,0:T(8,128)} %copy-done.20, ...), custom_call_target="tpu_custom_call" | custom-call | flops 1000000 | bytes 1000000 | tf_op jit(solution)/shard_map/pallas_call | solution.py:859
  (40 shorter events, 0.2 us)
Async XLA Ops:
  0.6 1.0 %copy-start.2 = (f32[16,16,512]{2,1,0:T(8,128)S(1)}, f32[16,16,512]{2,1,0:T(8,128)}, u32[]{:S(2)}) copy-start(f32[16,16,512]{2,1,0:T(8,128)} %rest_25_.1) | copy-start | bytes 1572868
  1.7 1.0 %copy-start.8 = (f32[16,16,512]{2,1,0:T(8,128)S(1)}, f32[16,16,512]{2,1,0:T(8,128)}, u32[]{:S(2)}) copy-start(f32[16,16,512]{2,1,0:T(8,128)} %c_ref.3) | copy-start | bytes 1572868
  3.0 34.4 %copy-start.12 = (f32[8,8,256]{2,1,0:T(8,128)}, f32[8,8,256]{2,1,0:T(8,128)S(1)}, u32[]{:S(2)}) copy-start(f32[8,8,256]{2,1,0:T(8,128)S(1)} %get-tuple-element.42.c1_ref.rest_12_) | copy-start | bytes 196612
  3.0 11.1 %collective-permute-start = (f32[7,16,512]{2,1,0:T(8,128)S(1)}, f32[7,16,512]{2,1,0:T(8,128)S(1)}, u32[]{:S(2)}, u32[]{:S(2)}) collective-permute-start(f32[7,16,512]{2,1,0:T(8,128)S(1)} %get-tuple-element.43), channel_id=1, source_target_pairs={{0,8},{8,16},{16,24},{24,32},{32,40},{40,48},{48,56},{56,64},{64,7... | collective-permute-start | bytes 688136 | tf_op jit(solution)/shard_map/ppermute | solution.py:876
  5.1 9.0 %collective-permute-start.1 = (f32[7,16,512]{2,1,0:T(8,128)S(1)}, f32[7,16,512]{2,1,0:T(8,128)S(1)}, u32[]{:S(2)}, u32[]{:S(2)}) collective-permute-start(f32[7,16,512]{2,1,0:T(8,128)S(1)} %get-tuple-element.44), channel_id=1, source_target_pairs={{8,0},{16,8},{24,16},{32,24},{40,32},{48,40},{56,48},{64,56},{72,6... | collective-permute-start | bytes 688136 | tf_op jit(solution)/shard_map/ppermute | solution.py:881
  10.0 18.4 %copy-start.3 = (f32[16,16,512]{2,1,0:T(8,128)}, f32[16,16,512]{2,1,0:T(8,128)S(1)}, u32[]{:S(2)}) copy-start(f32[16,16,512]{2,1,0:T(8,128)S(1)} %get-tuple-element.69.c_ref) | copy-start | bytes 1572868
  10.0 18.4 %copy-start.4 = (f32[16,16,512]{2,1,0:T(8,128)}, f32[16,16,512]{2,1,0:T(8,128)S(1)}, u32[]{:S(2)}) copy-start(f32[16,16,512]{2,1,0:T(8,128)S(1)} %get-tuple-element.40.g_ref) | copy-start | bytes 1572868
  14.8 22.6 %copy-start.6 = (f32[7,16,512]{2,1,0:T(8,128)}, f32[7,16,512]{2,1,0:T(8,128)S(1)}, u32[]{:S(2)}) copy-start(f32[7,16,512]{2,1,0:T(8,128)S(1)} %get-tuple-element.45.low_ref.low0.rest_13_) | copy-start | bytes 688132
  14.8 22.6 %copy-start.7 = (f32[7,16,512]{2,1,0:T(8,128)}, f32[7,16,512]{2,1,0:T(8,128)S(1)}, u32[]{:S(2)}) copy-start(f32[7,16,512]{2,1,0:T(8,128)S(1)} %get-tuple-element.46.high_ref.high0.rest_14_) | copy-start | bytes 688132
  14.8 8.2 %collective-permute-start.2 = (f32[28,8,512]{2,1,0:T(8,128)S(1)}, f32[28,8,512]{2,1,0:T(8,128)S(1)}, u32[]{:S(2)}, u32[]{:S(2)}) collective-permute-start(f32[28,8,512]{2,1,0:T(8,128)S(1)} %get-tuple-element.47), channel_id=1, source_target_pairs={{0,1},{1,2},{2,3},{3,4},{4,5},{5,6},{6,7},{7,0},{8,9},{9,10},{10,1... | collective-permute-start | bytes 1376264 | tf_op jit(solution)/shard_map/ppermute | solution.py:876
  17.7 7.9 %collective-permute-start.3 = (f32[28,8,512]{2,1,0:T(8,128)S(1)}, f32[28,8,512]{2,1,0:T(8,128)S(1)}, u32[]{:S(2)}, u32[]{:S(2)}) collective-permute-start(f32[28,8,512]{2,1,0:T(8,128)S(1)} %get-tuple-element.48), channel_id=1, source_target_pairs={{1,0},{2,1},{3,2},{4,3},{5,4},{6,5},{7,6},{0,7},{9,8},{10,9},{11,1... | collective-permute-start | bytes 1376264 | tf_op jit(solution)/shard_map/ppermute | solution.py:881
  23.1 14.3 %copy-start = (f32[28,8,512]{2,1,0:T(8,128)}, f32[28,8,512]{2,1,0:T(8,128)S(1)}, u32[]{:S(2)}) copy-start(f32[28,8,512]{2,1,0:T(8,128)S(1)} %collective-permute-done.2.below_ref.below0.rest_15_) | copy-start | bytes 1376260
  25.6 11.8 %copy-start.1 = (f32[28,8,512]{2,1,0:T(8,128)}, f32[28,8,512]{2,1,0:T(8,128)S(1)}, u32[]{:S(2)}) copy-start(f32[28,8,512]{2,1,0:T(8,128)S(1)} %collective-permute-done.3.above_ref.above0.rest_16_) | copy-start | bytes 1376260
  28.4 26.7 %copy-start.5 = (f32[16,16,512]{2,1,0:T(8,128)}, f32[16,16,512]{2,1,0:T(8,128)S(1)}, u32[]{:S(2)}) copy-start(f32[16,16,512]{2,1,0:T(8,128)S(1)} %get-tuple-element.63.own_ref.rest_18_) | copy-start | bytes 1572868
  28.4 7.1 %collective-permute-start.4 = (f32[6,8,256]{2,1,0:T(8,128)S(1)}, f32[6,8,256]{2,1,0:T(8,128)S(1)}, u32[]{:S(2)}, u32[]{:S(2)}) collective-permute-start(f32[6,8,256]{2,1,0:T(8,128)S(1)} %get-tuple-element.76), channel_id=1, source_target_pairs={{0,8},{8,16},{16,24},{24,32},{32,40},{40,48},{48,56},{56,64},{64,7... | collective-permute-start | bytes 147464 | tf_op jit(solution)/shard_map/ppermute | solution.py:876
  28.5 7.1 %collective-permute-start.5 = (f32[6,8,256]{2,1,0:T(8,128)S(1)}, f32[6,8,256]{2,1,0:T(8,128)S(1)}, u32[]{:S(2)}, u32[]{:S(2)}) collective-permute-start(f32[6,8,256]{2,1,0:T(8,128)S(1)} %get-tuple-element.77), channel_id=1, source_target_pairs={{8,0},{16,8},{24,16},{32,24},{40,32},{48,40},{56,48},{64,56},{72,6... | collective-permute-start | bytes 147464 | tf_op jit(solution)/shard_map/ppermute | solution.py:881
  35.6 6.9 %copy-start.9 = (f32[20,8,256]{2,1,0:T(8,128)}, f32[20,8,256]{2,1,0:T(8,128)S(1)}, u32[]{:S(2)}) copy-start(f32[20,8,256]{2,1,0:T(8,128)S(1)} %pad_maximum_fusion.mid_ref.rest_9_) | copy-start | bytes 491524
  35.6 4.8 %collective-permute-start.7 = (f32[20,8,256]{2,1,0:T(8,128)S(1)}, f32[20,8,256]{2,1,0:T(8,128)S(1)}, u32[]{:S(2)}, u32[]{:S(2)}) collective-permute-start(f32[20,8,256]{2,1,0:T(8,128)S(1)} %pad_maximum_fusion.mid_ref.rest_9_), channel_id=1, source_target_pairs={{1,0},{2,1},{3,2},{4,3},{5,4},{6,5},{7,6},{0,7},{9,8},{10,9},{11,1... | collective-permute-start | bytes 491528 | tf_op jit(solution)/shard_map/ppermute | solution.py:881
  36.1 4.3 %collective-permute-start.6 = (f32[20,8,256]{2,1,0:T(8,128)S(1)}, f32[20,8,256]{2,1,0:T(8,128)S(1)}, u32[]{:S(2)}, u32[]{:S(2)}) collective-permute-start(f32[20,8,256]{2,1,0:T(8,128)S(1)} %pad_maximum_fusion.mid_ref.rest_9_), channel_id=1, source_target_pairs={{0,1},{1,2},{2,3},{3,4},{4,5},{5,6},{6,7},{7,0},{8,9},{9,10},{10,1... | collective-permute-start | bytes 491528 | tf_op jit(solution)/shard_map/ppermute | solution.py:876
  38.7 3.8 %copy-start.16 = (f32[12,16,128]{2,1,0:T(8,128)}, f32[12,16,128]{2,1,0:T(8,128)S(1)}, u32[]{:S(2)}) copy-start(f32[12,16,128]{2,1,0:T(8,128)S(1)} %get-tuple-element.55.wx2.rest_0_) | copy-start | bytes 294916
  38.7 3.8 %copy-start.17 = (f32[12,16,128]{2,1,0:T(8,128)}, f32[12,16,128]{2,1,0:T(8,128)S(1)}, u32[]{:S(2)}) copy-start(f32[12,16,128]{2,1,0:T(8,128)S(1)} %get-tuple-element.56.wy2.rest_1_) | copy-start | bytes 294916
  38.7 3.8 %copy-start.18 = (f32[12,16,128]{2,1,0:T(8,128)}, f32[12,16,128]{2,1,0:T(8,128)S(1)}, u32[]{:S(2)}) copy-start(f32[12,16,128]{2,1,0:T(8,128)S(1)} %get-tuple-element.57.wz2.rest_2_) | copy-start | bytes 294916
  38.7 3.8 %copy-start.19 = (f32[12,16,128]{2,1,0:T(8,128)}, f32[12,16,128]{2,1,0:T(8,128)S(1)}, u32[]{:S(2)}) copy-start(f32[12,16,128]{2,1,0:T(8,128)S(1)} %get-tuple-element.59.q2.rest_3_) | copy-start | bytes 294916
  40.4 2.2 %copy-start.10 = (f32[20,8,256]{2,1,0:T(8,128)}, f32[20,8,256]{2,1,0:T(8,128)S(1)}, u32[]{:S(2)}) copy-start(f32[20,8,256]{2,1,0:T(8,128)S(1)} %collective-permute-done.7.above_ref.rest_11_) | copy-start | bytes 491524
  40.4 2.2 %copy-start.11 = (f32[20,8,256]{2,1,0:T(8,128)}, f32[20,8,256]{2,1,0:T(8,128)S(1)}, u32[]{:S(2)}) copy-start(f32[20,8,256]{2,1,0:T(8,128)S(1)} %collective-permute-done.6.below_ref.rest_10_) | copy-start | bytes 491524
  42.6 20.1 %copy-start.15 = (f32[16,24,256]{2,1,0:T(8,128)}, f32[16,24,256]{2,1,0:T(8,128)S(1)}, u32[]{:S(2)}) copy-start(f32[16,24,256]{2,1,0:T(8,128)S(1)} %get-tuple-element.68.rest_17_) | copy-start | bytes 1179652
  42.6 20.1 %copy-start.20 = (f32[8,512]{1,0:T(8,128)}, f32[8,512]{1,0:T(8,128)S(1)}, u32[]{:S(2)}) copy-start(f32[8,512]{1,0:T(8,128)S(1)} %get-tuple-element.62.own2_ref.rest_4_) | copy-start | bytes 49156
  42.6 12.5 %collective-permute-start.8 = (f32[7,8,512]{2,1,0:T(8,128)S(1)}, f32[7,8,512]{2,1,0:T(8,128)S(1)}, u32[]{:S(2)}, u32[]{:S(2)}) collective-permute-start(f32[7,8,512]{2,1,0:T(8,128)S(1)} %get-tuple-element.64), channel_id=1, source_target_pairs={{0,8},{8,16},{16,24},{24,32},{32,40},{40,48},{48,56},{56,64},{64,7... | collective-permute-start | bytes 344072 | tf_op jit(solution)/shard_map/ppermute | solution.py:876
  42.7 12.4 %collective-permute-start.9 = (f32[7,8,512]{2,1,0:T(8,128)S(1)}, f32[7,8,512]{2,1,0:T(8,128)S(1)}, u32[]{:S(2)}, u32[]{:S(2)}) collective-permute-start(f32[7,8,512]{2,1,0:T(8,128)S(1)} %get-tuple-element.65), channel_id=1, source_target_pairs={{8,0},{16,8},{24,16},{32,24},{40,32},{48,40},{56,48},{64,56},{72,6... | collective-permute-start | bytes 344072 | tf_op jit(solution)/shard_map/ppermute | solution.py:881
  47.5 18.6 %all-to-all-start = ((f32[128,4,128]{2,1,0:T(4,128)}), f32[128,4,128]{2,1,0:T(4,128)S(1)}, u32[]{:S(2)}, u32[]{:S(2)}) async-start(f32[128,4,128]{2,1,0:T(4,128)} %bitcast), calls=%async_computation | async-start | bytes 524288 | tf_op jit(solution)/shard_map/all_to_all | solution.py:907
  55.1 7.6 %copy-start.13 = (f32[7,8,512]{2,1,0:T(8,128)}, f32[7,8,512]{2,1,0:T(8,128)S(1)}, u32[]{:S(2)}) copy-start(f32[7,8,512]{2,1,0:T(8,128)S(1)} %collective-permute-done.8.low_ref.rest_5_) | copy-start | bytes 344068
  55.1 7.6 %copy-start.14 = (f32[7,8,512]{2,1,0:T(8,128)}, f32[7,8,512]{2,1,0:T(8,128)S(1)}, u32[]{:S(2)}) copy-start(f32[7,8,512]{2,1,0:T(8,128)S(1)} %collective-permute-done.9.high_ref.rest_6_) | copy-start | bytes 344068
  55.2 10.9 %collective-permute-start.10 = (f32[14,8,512]{2,1,0:T(8,128)S(1)}, f32[14,8,512]{2,1,0:T(8,128)S(1)}, u32[]{:S(2)}, u32[]{:S(2)}) collective-permute-start(f32[14,8,512]{2,1,0:T(8,128)S(1)} %get-tuple-element.66), channel_id=1, source_target_pairs={{0,1},{1,2},{2,3},{3,4},{4,5},{5,6},{6,7},{7,0},{8,9},{9,10},{10,1... | collective-permute-start | bytes 688136 | tf_op jit(solution)/shard_map/ppermute | solution.py:876
  57.1 9.0 %collective-permute-start.11 = (f32[14,8,512]{2,1,0:T(8,128)S(1)}, f32[14,8,512]{2,1,0:T(8,128)S(1)}, u32[]{:S(2)}, u32[]{:S(2)}) collective-permute-start(f32[14,8,512]{2,1,0:T(8,128)S(1)} %get-tuple-element.67), channel_id=1, source_target_pairs={{1,0},{2,1},{3,2},{4,3},{5,4},{6,5},{7,6},{0,7},{9,8},{10,9},{11,1... | collective-permute-start | bytes 688136 | tf_op jit(solution)/shard_map/ppermute | solution.py:881
  66.0 0.7 copy-start.21
  66.0 0.8 %copy-start.22 = (f32[14,8,512]{2,1,0:T(8,128)}, f32[14,8,512]{2,1,0:T(8,128)S(1)}, u32[]{:S(2)}) copy-start(f32[14,8,512]{2,1,0:T(8,128)S(1)} %collective-permute-done.10.rest_7_) | copy-start | bytes 688132
  66.1 0.9 %copy-start.23 = (f32[14,8,512]{2,1,0:T(8,128)}, f32[14,8,512]{2,1,0:T(8,128)S(1)}, u32[]{:S(2)}) copy-start(f32[14,8,512]{2,1,0:T(8,128)S(1)} %collective-permute-done.11.rest_8_) | copy-start | bytes 688132

commit v5 on v4

--- a/solution.py
+++ b/solution.py
@@ -62,8 +62,9 @@
     rest = cells - high.astype(F32)
     mid = rest.astype(BF16)
     low = (rest - mid.astype(F32)).astype(BF16)
-    dot = functools.partial(jnp.dot, preferred_element_type=F32)
-    return dot(high, pick) + (dot(mid, pick) + dot(low, pick))
+    count = cells.shape[0]
+    all_pieces = jnp.dot(jnp.concatenate([high, mid, low], axis=0), pick, preferred_element_type=F32)
+    return all_pieces[:count] + (all_pieces[count : 2 * count] + all_pieces[2 * count :])
 
 
 def split_dot_left(pick, cells):
@@ -393,14 +394,14 @@
     window0(low_ref, high_ref, below_ref, above_ref, c_ref, g_ref, *sides)(c, g)
     in_y = inside((Y0, Z0), 0, place_y * 16 - OY0, 16 * count_y).astype(F32)
     make_faces(
-        c, wx, wy, wz, d, q, 1, X0 - 1, lambda i: flag(place_x * 16 - OX0 + i, 16 * count_x), in_y, 2
+        c, wx, wy, wz, d, q, 1, X0 - 1, lambda i: flag(place_x * 16 - OX0 + i, 16 * count_x), in_y, 4
     )
 
     def begin(i):
         return [(b, i, q[i] * g[i])]
 
     loop(1, X0 - 1, begin, 2)
-    sweep(b, v, b, wx, wy, wz, q, 2, X0 - 2, 3)
+    sweep(b, v, b, wx, wy, wz, q, 2, X0 - 2, 6)
 
     def own_of(i):
         return [(v_own_ref, i, pltpu.roll(v[i + 3], Y0 - OY0, 0)[0:16])]
@@ -412,7 +413,7 @@
         both = defect(v, g, wx, wy, wz, d, i) + defect(v, g, wx, wy, wz, d, i + 1)
         return [(pairs, (j, k), lanes(both, k)) for k in range(Z0 // LANES)]
 
-    loop(0, 8, restrict)
+    loop(0, 8, restrict, 2)
     rows = jnp.concatenate([halve_rows(pairs, i, 4, 8) for i in range(8)], axis=0)
     g1_ref[...] = (0.5 * pair_sums(rows)).reshape(8, 8, Z1)
 
@@ -445,7 +446,7 @@
     fill_c1(c1, c1_ref, low_ref, high_ref, below_ref, above_ref, *sides)
     in_y = inside((Y1, Z1), 0, place_y * 8 - OY1, 8 * count_y).astype(F32)
     make_faces(
-        c1, wx1, wy1, wz1, d1, q1, 2, X1 - 2, lambda i: flag(place_x * 8 - OX1 + i, 8 * count_x), in_y, 2
+        c1, wx1, wy1, wz1, d1, q1, 2, X1 - 2, lambda i: flag(place_x * 8 - OX1 + i, 8 * count_x), in_y, 5
     )
     for i in range(12):
         keep(pairs, i, c1[2 * i] + c1[2 * i + 1])
@@ -500,8 +501,8 @@
     def begin1(i):
         return [(b1_ref, i, q1[i] * g1[i])]
 
-    loop(2, X1 - 2, begin1, 4)
-    sweep(b1_ref, v1_ref, b1_ref, wx1, wy1, wz1, q1, 3, X1 - 3, 3)
+    loop(2, X1 - 2, begin1, 10)
+    sweep(b1_ref, v1_ref, b1_ref, wx1, wy1, wz1, q1, 3, X1 - 3, 6)
 
     def restrict(j):
         i = 2 * j + 4
@@ -509,7 +510,7 @@
         both = defect(v1_ref, g1, wx1, wy1, wz1, d1, i) + after
         return [(pairs, (j, k), lanes(both, k)) for k in range(Z1 // LANES)]
 
-    loop(0, 8, restrict, 2)
+    loop(0, 8, restrict, 4)
     rows = jnp.concatenate([halve_rows(pairs, i, 4, 8) for i in range(8)], axis=0)
     small = 0.5 * pair_sums(rows)
     g2[...] = jnp.zeros((X2, Y2, Z2), F32)
@@ -758,7 +759,7 @@
     fill_g1(w1, g1_mid, g1_below, g1_above, low_y, high_y)
     in_y = inside((Y1, Z1), 0, place_y * 8 - OY1, 8 * count_y).astype(F32)
     make_faces(
-        c1, wx1, wy1, wz1, d1, q1, 5, X1 - 5, lambda i: flag(place_x * 8 - OX1 + i, 8 * count_x), in_y, 2
+        c1, wx1, wy1, wz1, d1, q1, 5, X1 - 5, lambda i: flag(place_x * 8 - OX1 + i, 8 * count_x), in_y, 7
     )
 
     def begin1(i):
@@ -832,8 +833,8 @@
             v0[i, 0:8] = jnp.where(half, below, head) + extra[0:8]
             v0[i, 8:16] = jnp.where(half, head, tail) + extra[8:16]
             v0[i, 16:24] = jnp.where(half, tail, above) + extra[16:24]
-    sweep(v0, w0, b0, wx0, wy0, wz0, q0, 1, X0 - 1, 2)
-    sweep(w0, v0, b0, wx0, wy0, wz0, q0, 2, X0 - 2, 2)
+    sweep(v0, w0, b0, wx0, wy0, wz0, q0, 1, X0 - 1, 4)
+    sweep(w0, v0, b0, wx0, wy0, wz0, q0, 2, X0 - 2, 3)
 
     pick = collect_matrix(Z0)
     rows = jnp.concatenate([pltpu.roll(v0[i + OX0], Y0 - OY0, 0)[0:16] for i in range(16)], axis=0)
@@ -844,7 +845,7 @@
         here, total = neighbours(v0, wx0, wy0, wz0, i + OX0)
         return [(residual_ref, i, pltpu.roll(total - d0[i + OX0] * here, Y0 - OY0, 0)[0:16])]
 
-    loop(0, 16, finish, 2)
+    loop(0, 16, finish, 4)
     for part in range(2):
         here = pl.ds(8 * part, 8)
         rows = residual_ref[here].reshape(128, Z0)

time: 77.7 us -> 76 us (0.978)
  Pallas kernels: 24.4 us -> 22.2 us
    pallas_call x1, Pallas kernels: 10.5 us -> 9.62 us  [up(): call(functools.partial(up_kernel, count_x, count_y), [struct(16, 16, Z0),...]
where the time goes in v5:
time: 76 us; the launch traced here: 75.7 us
  starting transfers between devices  29.8 us (39%)
  Pallas kernels  22.2 us (29%)
  waiting for transfers between devices  19.6 us (26%)
  local copies, waits for them, and re-layouts  3.02 us (4%)
  between operations  1.02 us (1%)
    ppermute x6, starting transfers between devices, to_previous(): lax.ppermute(cells, axis, [((i + 1) % count, i) for i in range(count)])  14 us
    ppermute x6, waiting for transfers between devices, to_next(): lax.ppermute(cells, axis, [(i, (i + 1) % count) for i in range(count)])  11.7 us
    pallas_call x1, Pallas kernels, up(): call(functools.partial(up_kernel, count_x, count_y), [struct(16, 16, Z0),...  9.62 us
    ppermute x6, starting transfers between devices, to_next(): lax.ppermute(cells, axis, [(i, (i + 1) % count) for i in range(count)])  8.25 us
    all_to_all x1, starting transfers between devices, shards(): lax.all_to_all(send3, ('gx', 'gy'), split_axis=0, concat_axis=0, tiled=True)  7.59 us
    pallas_call x1, Pallas kernels, weights0(): call(functools.partial(weights0_kernel, count_x, count_y), [struct(*frame...  5.6 us
    ppermute x6, waiting for transfers between devices, to_previous(): lax.ppermute(cells, axis, [((i + 1) % count, i) for i in range(count)])  4.6 us
    all_to_all x1, waiting for transfers between devices, shards(): lax.all_to_all(send3, ('gx', 'gy'), split_axis=0, concat_axis=0, tiled=True)  3.31 us
  transfers between devices with their start and end apart: 13, of which 6 were waited for; matrix products, arithmetic and copies ran while one was open for 0% of the time, Pallas kernels for 10%

profile of v5, /device:TPU:1, one launch (start us, length us, event | category | flops | bytes accessed | tf_op | source)
XLA Modules:
  0.0 75.7 jit_solution(14823028033209186090)
XLA Ops:
  0.6 0.0 copy-start.2
  0.6 1.0 %copy-done.2 = f32[16,16,512]{2,1,0:T(8,128)S(1)} copy-done((f32[16,16,512]{2,1,0:T(8,128)S(1)}, f32[16,16,512]{2,1,0:T(8,128)}, u32[]{:S(2)}) %copy-start.2) | copy-done | bytes 524312
  1.7 1.0 %copy-done.8 = f32[16,16,512]{2,1,0:T(8,128)S(1)} copy-done((f32[16,16,512]{2,1,0:T(8,128)S(1)}, f32[16,16,512]{2,1,0:T(8,128)}, u32[]{:S(2)}) %copy-start.8) | copy-done | bytes 524312
  2.7 0.2 shard_map.42
  3.0 2.1 %collective-permute-start = (f32[7,16,512]{2,1,0:T(8,128)S(1)}, f32[7,16,512]{2,1,0:T(8,128)S(1)}, u32[]{:S(2)}, u32[]{:S(2)}) collective-permute-start(f32[7,16,512]{2,1,0:T(8,128)S(1)} %get-tuple-element.43), channel_id=1, source_target_pairs={{0,8},{8,16},{16,24},{24,32},{32,40},{40,48},{48,56},{56,64},{64,7... | collective-permute-start | bytes 688136 | tf_op jit(solution)/shard_map/ppermute | solution.py:877
  5.1 3.8 %collective-permute-start.1 = (f32[7,16,512]{2,1,0:T(8,128)S(1)}, f32[7,16,512]{2,1,0:T(8,128)S(1)}, u32[]{:S(2)}, u32[]{:S(2)}) collective-permute-start(f32[7,16,512]{2,1,0:T(8,128)S(1)} %get-tuple-element.44), channel_id=1, source_target_pairs={{8,0},{16,8},{24,16},{32,24},{40,32},{48,40},{56,48},{64,56},{72,6... | collective-permute-start | bytes 688136 | tf_op jit(solution)/shard_map/ppermute | solution.py:882
  8.9 1.0 %shard_map.41 = (f32[16,16,512]{2,1,0:T(8,128)S(1)}, f32[16,16,512]{2,1,0:T(8,128)S(1)}, bf16[512,512]{1,0:T(8,128)(2,1)S(1)}) custom-call(f32[16,16,512]{2,1,0:T(8,128)S(1)} %copy-done.8, f32[16,16,512]{2,1,0:T(8,128)S(1)} %copy-done.2), custom_call_target="tpu_custom_call" | custom-call | flops 1000000 | bytes 1000000 | tf_op jit(solution)/shard_map/pallas_call | solution.py:293
  9.9 0.0 copy-start.3
  9.9 0.0 copy-start.4
  10.0 4.1 %collective-permute-done.low_raw = f32[7,16,512]{2,1,0:T(8,128)S(1)} collective-permute-done((f32[7,16,512]{2,1,0:T(8,128)S(1)}, f32[7,16,512]{2,1,0:T(8,128)S(1)}, u32[]{:S(2)}, u32[]{:S(2)}) %collective-permute-start) | collective-permute-done | bytes 229408 | tf_op jit(solution)/shard_map/ppermute | solution.py:877
  14.1 0.0 collective-permute-done.1.high_raw
  14.1 0.4 shard_map.43
  14.5 0.0 copy-start.6
  14.5 0.0 copy-start.7
  14.5 2.8 %collective-permute-start.2 = (f32[28,8,512]{2,1,0:T(8,128)S(1)}, f32[28,8,512]{2,1,0:T(8,128)S(1)}, u32[]{:S(2)}, u32[]{:S(2)}) collective-permute-start(f32[28,8,512]{2,1,0:T(8,128)S(1)} %get-tuple-element.47), channel_id=1, source_target_pairs={{0,1},{1,2},{2,3},{3,4},{4,5},{5,6},{6,7},{7,0},{8,9},{9,10},{10,1... | collective-permute-start | bytes 1376264 | tf_op jit(solution)/shard_map/ppermute | solution.py:877
  17.3 0.0 collective-permute-start.3
  17.4 5.4 %collective-permute-done.2.below_ref.below0.rest_15_ = f32[28,8,512]{2,1,0:T(8,128)S(1)} collective-permute-done((f32[28,8,512]{2,1,0:T(8,128)S(1)}, f32[28,8,512]{2,1,0:T(8,128)S(1)}, u32[]{:S(2)}, u32[]{:S(2)}) %collective-permute-start.2) | collective-permute-done | bytes 458784 | tf_op jit(solution)/shard_map/ppermute | solution.py:877
  22.8 2.5 %collective-permute-done.3.above_ref.above0.rest_16_ = f32[28,8,512]{2,1,0:T(8,128)S(1)} collective-permute-done((f32[28,8,512]{2,1,0:T(8,128)S(1)}, f32[28,8,512]{2,1,0:T(8,128)S(1)}, u32[]{:S(2)}, u32[]{:S(2)}) %collective-permute-start.3) | collective-permute-done | bytes 458784 | tf_op jit(solution)/shard_map/ppermute | solution.py:882
  25.3 2.6 %shard_map.44 = (f32[8,8,256]{2,1,0:T(8,128)S(1)}, f32[16,16,512]{2,1,0:T(8,128)S(1)}) custom-call(f32[16,16,512]{2,1,0:T(8,128)S(1)} %get-tuple-element.69.c_ref, f32[16,16,512]{2,1,0:T(8,128)S(1)} %get-tuple-element.40.g_ref, f32[7,16,512]{2,1,0:T(8,128)S(1)} %get-tuple-element.45.low_ref.low0.rest_13_, ...), custom_call_target="tpu_custom_call" | custom-call | flops 1000000 | bytes 1000000 | tf_op jit(solution)/shard_map/pallas_call | solution.py:423
  27.9 0.1 collective-permute-start.4
  28.0 4.9 %collective-permute-start.5 = (f32[6,8,256]{2,1,0:T(8,128)S(1)}, f32[6,8,256]{2,1,0:T(8,128)S(1)}, u32[]{:S(2)}, u32[]{:S(2)}) collective-permute-start(f32[6,8,256]{2,1,0:T(8,128)S(1)} %get-tuple-element.77), channel_id=1, source_target_pairs={{8,0},{16,8},{24,16},{32,24},{40,32},{48,40},{56,48},{64,56},{72,6... | collective-permute-start | bytes 147464 | tf_op jit(solution)/shard_map/ppermute | solution.py:882
  32.9 2.1 %collective-permute-done.4 = f32[6,8,256]{2,1,0:T(8,128)S(1)} collective-permute-done((f32[6,8,256]{2,1,0:T(8,128)S(1)}, f32[6,8,256]{2,1,0:T(8,128)S(1)}, u32[]{:S(2)}, u32[]{:S(2)}) %collective-permute-start.4) | collective-permute-done | bytes 49184 | tf_op jit(solution)/shard_map/ppermute | solution.py:877
  35.1 0.0 collective-permute-done.5
  35.1 0.5 collective-permute-start.7
  35.6 1.3 %collective-permute-start.6 = (f32[20,8,256]{2,1,0:T(8,128)S(1)}, f32[20,8,256]{2,1,0:T(8,128)S(1)}, u32[]{:S(2)}, u32[]{:S(2)}) collective-permute-start(f32[20,8,256]{2,1,0:T(8,128)S(1)} %pad_maximum_fusion.mid_ref.rest_9_), channel_id=1, source_target_pairs={{0,1},{1,2},{2,3},{3,4},{4,5},{5,6},{6,7},{7,0},{8,9},{9,10},{10,1... | collective-permute-start | bytes 491528 | tf_op jit(solution)/shard_map/ppermute | solution.py:877
  36.9 0.0 copy-done.12
  36.9 0.0 copy-done.1
  36.9 0.8 %shard_map.45 = (f32[24,24,256]{2,1,0:T(8,128)S(1)}, f32[24,24,256]{2,1,0:T(8,128)S(1)}, f32[24,24,256]{2,1,0:T(8,128)S(1)}, f32[24,24,256]{2,1,0:T(8,128)S(1)},...) custom-call(f32[8,8,256]{2,1,0:T(8,128)S(1)} %get-tuple-element.42.c, ...), custom_call_target="tpu_custom_call" | custom-call | flops 1000000 | bytes 1000000 | tf_op jit(solution)/shard_map/pallas_call | solution.py:477
  37.8 2.1 %collective-permute-done.7.above_ref.rest_11_ = f32[20,8,256]{2,1,0:T(8,128)S(1)} collective-permute-done((f32[20,8,256]{2,1,0:T(8,128)S(1)}, f32[20,8,256]{2,1,0:T(8,128)S(1)}, u32[]{:S(2)}, u32[]{:S(2)}) %collective-permute-start.7) | collective-permute-done | bytes 163872 | tf_op jit(solution)/shard_map/ppermute | solution.py:882
  39.9 0.0 collective-permute-done.6.below_ref.rest_10_
  39.9 1.8 %shard_map.46 = (f32[16,24,256]{2,1,0:T(8,128)S(1)}, f32[8,512]{1,0:T(8,128)S(1)}, f32[512,128]{1,0:T(8,128)}) custom-call(f32[20,8,256]{2,1,0:T(8,128)S(1)} %pad_maximum_fusion.mid_ref.rest_9_, f32[20,8,256]{2,1,0:T(8,128)S(1)} %collective-permute-done.6.below_ref.rest_10_, f32[20,8,256]{2,1,0:T(8,128)S(1)} %collective-permute-done.7.above_ref.rest_11_, ...), custom_call_target="tpu_custom_call" | custom-call | flops 1000000 | bytes 1000000 | tf_op jit(solution)/shard_map/pallas_call | solution.py:547
  41.7 0.0 copy-done.18
  41.7 0.0 copy-done.19
  41.8 0.1 collective-permute-start.8
  41.8 4.8 %collective-permute-start.9 = (f32[7,8,512]{2,1,0:T(8,128)S(1)}, f32[7,8,512]{2,1,0:T(8,128)S(1)}, u32[]{:S(2)}, u32[]{:S(2)}) collective-permute-start(f32[7,8,512]{2,1,0:T(8,128)S(1)} %get-tuple-element.65), channel_id=1, source_target_pairs={{8,0},{16,8},{24,16},{32,24},{40,32},{48,40},{56,48},{64,56},{72,6... | collective-permute-start | bytes 344072 | tf_op jit(solution)/shard_map/ppermute | solution.py:882
  46.6 7.6 %all-to-all-start = ((f32[128,4,128]{2,1,0:T(4,128)}), f32[128,4,128]{2,1,0:T(4,128)S(1)}, u32[]{:S(2)}, u32[]{:S(2)}) async-start(f32[128,4,128]{2,1,0:T(4,128)} %bitcast), calls=%async_computation | async-start | bytes 524288 | tf_op jit(solution)/shard_map/all_to_all | solution.py:908
  54.2 0.0 collective-permute-done.8.low_ref.rest_5_
  54.2 0.0 collective-permute-done.9.high_ref.rest_6_
  54.3 1.9 %collective-permute-start.10 = (f32[14,8,512]{2,1,0:T(8,128)S(1)}, f32[14,8,512]{2,1,0:T(8,128)S(1)}, u32[]{:S(2)}, u32[]{:S(2)}) collective-permute-start(f32[14,8,512]{2,1,0:T(8,128)S(1)} %get-tuple-element.66), channel_id=1, source_target_pairs={{0,1},{1,2},{2,3},{3,4},{4,5},{5,6},{6,7},{7,0},{8,9},{9,10},{10,1... | collective-permute-start | bytes 688136 | tf_op jit(solution)/shard_map/ppermute | solution.py:877
  56.2 0.0 collective-permute-start.11
  56.2 5.6 %shard_map.49 = (f32[22,24,512]{2,1,0:T(8,128)}, f32[22,24,512]{2,1,0:T(8,128)}, f32[22,24,512]{2,1,0:T(8,128)}, f32[22,24,512]{2,1,0:T(8,128)}, f32[22,24,512]{2,1,0:T(8,128)}, /*index=5*/f32[22,24,512]{2,1,0:T(8,128)}) custom-call(f32[16,16,512]{2,1,0:T(8,128)} %copy-done.3, f32[16,16,512]{2,1,0:T(8,128)} %copy-done.4, f32[7,16,512]{2,1,0:T(8,128)} %copy-done.6, ...), custom_call_target="tpu_custom_call" | custom-call | flops 20000000 | bytes 20000000 | tf_op jit(solution)/shard_map/pallas_call | solution.py:620
  61.9 3.3 %all-to-all-done = f32[128,4,128]{2,1,0:T(4,128)S(1)} async-done(((f32[128,4,128]{2,1,0:T(4,128)}), f32[128,4,128]{2,1,0:T(4,128)S(1)}, u32[]{:S(2)}, u32[]{:S(2)}) %all-to-all-start) | async-done | bytes 262176 | tf_op jit(solution)/shard_map/all_to_all | solution.py:908
  65.2 0.0 collective-permute-done.10.rest_7_
  65.2 0.0 collective-permute-done.11.rest_8_
  65.2 0.7 copy-done.21
  65.9 0.1 copy-done.22
  66.0 0.1 copy-done.23
  66.1 9.6 %shard_map.50 = (f32[16,16,512]{2,1,0:T(8,128)}, f32[16,16,512]{2,1,0:T(8,128)}) custom-call(f32[512,128]{1,0:T(8,128)} %bitcast.2, f32[12,16,128]{2,1,0:T(8,128)} %copy-done.16, f32[12,16,128]{2,1,0:T(8,128)} %copy-done.17, f32[12,16,128]{2,1,0:T(8,128)} %copy-done.18, f32[12,16,128]{2,1,0:T(8,128)} %copy-done.19, f32[8,512]{1,0:T(8,128)} %copy-done.20, ...), custom_call_target="tpu_custom_call" | custom-call | flops 1000000 | bytes 1000000 | tf_op jit(solution)/shard_map/pallas_call | solution.py:860
  (40 shorter events, 0.2 us)
Async XLA Ops:
  0.6 1.0 %copy-start.2 = (f32[16,16,512]{2,1,0:T(8,128)S(1)}, f32[16,16,512]{2,1,0:T(8,128)}, u32[]{:S(2)}) copy-start(f32[16,16,512]{2,1,0:T(8,128)} %rest_25_.1) | copy-start | bytes 1572868
  1.7 1.0 %copy-start.8 = (f32[16,16,512]{2,1,0:T(8,128)S(1)}, f32[16,16,512]{2,1,0:T(8,128)}, u32[]{:S(2)}) copy-start(f32[16,16,512]{2,1,0:T(8,128)} %c_ref.3) | copy-start | bytes 1572868
  3.0 33.9 %copy-start.12 = (f32[8,8,256]{2,1,0:T(8,128)}, f32[8,8,256]{2,1,0:T(8,128)S(1)}, u32[]{:S(2)}) copy-start(f32[8,8,256]{2,1,0:T(8,128)S(1)} %get-tuple-element.42.c1_ref.rest_12_) | copy-start | bytes 196612
  3.0 11.1 %collective-permute-start = (f32[7,16,512]{2,1,0:T(8,128)S(1)}, f32[7,16,512]{2,1,0:T(8,128)S(1)}, u32[]{:S(2)}, u32[]{:S(2)}) collective-permute-start(f32[7,16,512]{2,1,0:T(8,128)S(1)} %get-tuple-element.43), channel_id=1, source_target_pairs={{0,8},{8,16},{16,24},{24,32},{32,40},{40,48},{48,56},{56,64},{64,7... | collective-permute-start | bytes 688136 | tf_op jit(solution)/shard_map/ppermute | solution.py:877
  5.1 9.0 %collective-permute-start.1 = (f32[7,16,512]{2,1,0:T(8,128)S(1)}, f32[7,16,512]{2,1,0:T(8,128)S(1)}, u32[]{:S(2)}, u32[]{:S(2)}) collective-permute-start(f32[7,16,512]{2,1,0:T(8,128)S(1)} %get-tuple-element.44), channel_id=1, source_target_pairs={{8,0},{16,8},{24,16},{32,24},{40,32},{48,40},{56,48},{64,56},{72,6... | collective-permute-start | bytes 688136 | tf_op jit(solution)/shard_map/ppermute | solution.py:882
  9.9 17.9 %copy-start.3 = (f32[16,16,512]{2,1,0:T(8,128)}, f32[16,16,512]{2,1,0:T(8,128)S(1)}, u32[]{:S(2)}) copy-start(f32[16,16,512]{2,1,0:T(8,128)S(1)} %get-tuple-element.69.c_ref) | copy-start | bytes 1572868
  9.9 17.9 %copy-start.4 = (f32[16,16,512]{2,1,0:T(8,128)}, f32[16,16,512]{2,1,0:T(8,128)S(1)}, u32[]{:S(2)}) copy-start(f32[16,16,512]{2,1,0:T(8,128)S(1)} %get-tuple-element.40.g_ref) | copy-start | bytes 1572868
  14.5 22.4 %copy-start.6 = (f32[7,16,512]{2,1,0:T(8,128)}, f32[7,16,512]{2,1,0:T(8,128)S(1)}, u32[]{:S(2)}) copy-start(f32[7,16,512]{2,1,0:T(8,128)S(1)} %get-tuple-element.45.low_ref.low0.rest_13_) | copy-start | bytes 688132
  14.5 22.4 %copy-start.7 = (f32[7,16,512]{2,1,0:T(8,128)}, f32[7,16,512]{2,1,0:T(8,128)S(1)}, u32[]{:S(2)}) copy-start(f32[7,16,512]{2,1,0:T(8,128)S(1)} %get-tuple-element.46.high_ref.high0.rest_14_) | copy-start | bytes 688132
  14.5 8.2 %collective-permute-start.2 = (f32[28,8,512]{2,1,0:T(8,128)S(1)}, f32[28,8,512]{2,1,0:T(8,128)S(1)}, u32[]{:S(2)}, u32[]{:S(2)}) collective-permute-start(f32[28,8,512]{2,1,0:T(8,128)S(1)} %get-tuple-element.47), channel_id=1, source_target_pairs={{0,1},{1,2},{2,3},{3,4},{4,5},{5,6},{6,7},{7,0},{8,9},{9,10},{10,1... | collective-permute-start | bytes 1376264 | tf_op jit(solution)/shard_map/ppermute | solution.py:877
  17.3 7.9 %collective-permute-start.3 = (f32[28,8,512]{2,1,0:T(8,128)S(1)}, f32[28,8,512]{2,1,0:T(8,128)S(1)}, u32[]{:S(2)}, u32[]{:S(2)}) collective-permute-start(f32[28,8,512]{2,1,0:T(8,128)S(1)} %get-tuple-element.48), channel_id=1, source_target_pairs={{1,0},{2,1},{3,2},{4,3},{5,4},{6,5},{7,6},{0,7},{9,8},{10,9},{11,1... | collective-permute-start | bytes 1376264 | tf_op jit(solution)/shard_map/ppermute | solution.py:882
  22.8 14.1 %copy-start = (f32[28,8,512]{2,1,0:T(8,128)}, f32[28,8,512]{2,1,0:T(8,128)S(1)}, u32[]{:S(2)}) copy-start(f32[28,8,512]{2,1,0:T(8,128)S(1)} %collective-permute-done.2.below_ref.below0.rest_15_) | copy-start | bytes 1376260
  25.3 11.7 %copy-start.1 = (f32[28,8,512]{2,1,0:T(8,128)}, f32[28,8,512]{2,1,0:T(8,128)S(1)}, u32[]{:S(2)}) copy-start(f32[28,8,512]{2,1,0:T(8,128)S(1)} %collective-permute-done.3.above_ref.above0.rest_16_) | copy-start | bytes 1376260
  27.9 26.4 %copy-start.5 = (f32[16,16,512]{2,1,0:T(8,128)}, f32[16,16,512]{2,1,0:T(8,128)S(1)}, u32[]{:S(2)}) copy-start(f32[16,16,512]{2,1,0:T(8,128)S(1)} %get-tuple-element.63.own_ref.rest_18_) | copy-start | bytes 1572868
  27.9 7.1 %collective-permute-start.4 = (f32[6,8,256]{2,1,0:T(8,128)S(1)}, f32[6,8,256]{2,1,0:T(8,128)S(1)}, u32[]{:S(2)}, u32[]{:S(2)}) collective-permute-start(f32[6,8,256]{2,1,0:T(8,128)S(1)} %get-tuple-element.76), channel_id=1, source_target_pairs={{0,8},{8,16},{16,24},{24,32},{32,40},{40,48},{48,56},{56,64},{64,7... | collective-permute-start | bytes 147464 | tf_op jit(solution)/shard_map/ppermute | solution.py:877
  28.0 7.1 %collective-permute-start.5 = (f32[6,8,256]{2,1,0:T(8,128)S(1)}, f32[6,8,256]{2,1,0:T(8,128)S(1)}, u32[]{:S(2)}, u32[]{:S(2)}) collective-permute-start(f32[6,8,256]{2,1,0:T(8,128)S(1)} %get-tuple-element.77), channel_id=1, source_target_pairs={{8,0},{16,8},{24,16},{32,24},{40,32},{48,40},{56,48},{64,56},{72,6... | collective-permute-start | bytes 147464 | tf_op jit(solution)/shard_map/ppermute | solution.py:882
  35.1 6.6 %copy-start.9 = (f32[20,8,256]{2,1,0:T(8,128)}, f32[20,8,256]{2,1,0:T(8,128)S(1)}, u32[]{:S(2)}) copy-start(f32[20,8,256]{2,1,0:T(8,128)S(1)} %pad_maximum_fusion.mid_ref.rest_9_) | copy-start | bytes 491524
  35.1 4.8 %collective-permute-start.7 = (f32[20,8,256]{2,1,0:T(8,128)S(1)}, f32[20,8,256]{2,1,0:T(8,128)S(1)}, u32[]{:S(2)}, u32[]{:S(2)}) collective-permute-start(f32[20,8,256]{2,1,0:T(8,128)S(1)} %pad_maximum_fusion.mid_ref.rest_9_), channel_id=1, source_target_pairs={{1,0},{2,1},{3,2},{4,3},{5,4},{6,5},{7,6},{0,7},{9,8},{10,9},{11,1... | collective-permute-start | bytes 491528 | tf_op jit(solution)/shard_map/ppermute | solution.py:882
  35.6 4.3 %collective-permute-start.6 = (f32[20,8,256]{2,1,0:T(8,128)S(1)}, f32[20,8,256]{2,1,0:T(8,128)S(1)}, u32[]{:S(2)}, u32[]{:S(2)}) collective-permute-start(f32[20,8,256]{2,1,0:T(8,128)S(1)} %pad_maximum_fusion.mid_ref.rest_9_), channel_id=1, source_target_pairs={{0,1},{1,2},{2,3},{3,4},{4,5},{5,6},{6,7},{7,0},{8,9},{9,10},{10,1... | collective-permute-start | bytes 491528 | tf_op jit(solution)/shard_map/ppermute | solution.py:877
  37.7 3.9 %copy-start.16 = (f32[12,16,128]{2,1,0:T(8,128)}, f32[12,16,128]{2,1,0:T(8,128)S(1)}, u32[]{:S(2)}) copy-start(f32[12,16,128]{2,1,0:T(8,128)S(1)} %get-tuple-element.55.wx2.rest_0_) | copy-start | bytes 294916
  37.7 3.9 %copy-start.17 = (f32[12,16,128]{2,1,0:T(8,128)}, f32[12,16,128]{2,1,0:T(8,128)S(1)}, u32[]{:S(2)}) copy-start(f32[12,16,128]{2,1,0:T(8,128)S(1)} %get-tuple-element.56.wy2.rest_1_) | copy-start | bytes 294916
  37.8 3.9 %copy-start.18 = (f32[12,16,128]{2,1,0:T(8,128)}, f32[12,16,128]{2,1,0:T(8,128)S(1)}, u32[]{:S(2)}) copy-start(f32[12,16,128]{2,1,0:T(8,128)S(1)} %get-tuple-element.57.wz2.rest_2_) | copy-start | bytes 294916
  37.8 3.9 %copy-start.19 = (f32[12,16,128]{2,1,0:T(8,128)}, f32[12,16,128]{2,1,0:T(8,128)S(1)}, u32[]{:S(2)}) copy-start(f32[12,16,128]{2,1,0:T(8,128)S(1)} %get-tuple-element.59.q2.rest_3_) | copy-start | bytes 294916
  39.9 1.8 %copy-start.10 = (f32[20,8,256]{2,1,0:T(8,128)}, f32[20,8,256]{2,1,0:T(8,128)S(1)}, u32[]{:S(2)}) copy-start(f32[20,8,256]{2,1,0:T(8,128)S(1)} %collective-permute-done.7.above_ref.rest_11_) | copy-start | bytes 491524
  39.9 1.8 %copy-start.11 = (f32[20,8,256]{2,1,0:T(8,128)}, f32[20,8,256]{2,1,0:T(8,128)S(1)}, u32[]{:S(2)}) copy-start(f32[20,8,256]{2,1,0:T(8,128)S(1)} %collective-permute-done.6.below_ref.rest_10_) | copy-start | bytes 491524
  41.7 20.1 %copy-start.15 = (f32[16,24,256]{2,1,0:T(8,128)}, f32[16,24,256]{2,1,0:T(8,128)S(1)}, u32[]{:S(2)}) copy-start(f32[16,24,256]{2,1,0:T(8,128)S(1)} %get-tuple-element.68.rest_17_) | copy-start | bytes 1179652
  41.7 20.1 %copy-start.20 = (f32[8,512]{1,0:T(8,128)}, f32[8,512]{1,0:T(8,128)S(1)}, u32[]{:S(2)}) copy-start(f32[8,512]{1,0:T(8,128)S(1)} %get-tuple-element.62.own2_ref.rest_4_) | copy-start | bytes 49156
  41.8 12.5 %collective-permute-start.8 = (f32[7,8,512]{2,1,0:T(8,128)S(1)}, f32[7,8,512]{2,1,0:T(8,128)S(1)}, u32[]{:S(2)}, u32[]{:S(2)}) collective-permute-start(f32[7,8,512]{2,1,0:T(8,128)S(1)} %get-tuple-element.64), channel_id=1, source_target_pairs={{0,8},{8,16},{16,24},{24,32},{32,40},{40,48},{48,56},{56,64},{64,7... | collective-permute-start | bytes 344072 | tf_op jit(solution)/shard_map/ppermute | solution.py:877
  41.8 12.4 %collective-permute-start.9 = (f32[7,8,512]{2,1,0:T(8,128)S(1)}, f32[7,8,512]{2,1,0:T(8,128)S(1)}, u32[]{:S(2)}, u32[]{:S(2)}) collective-permute-start(f32[7,8,512]{2,1,0:T(8,128)S(1)} %get-tuple-element.65), channel_id=1, source_target_pairs={{8,0},{16,8},{24,16},{32,24},{40,32},{48,40},{56,48},{64,56},{72,6... | collective-permute-start | bytes 344072 | tf_op jit(solution)/shard_map/ppermute | solution.py:882
  46.6 18.6 %all-to-all-start = ((f32[128,4,128]{2,1,0:T(4,128)}), f32[128,4,128]{2,1,0:T(4,128)S(1)}, u32[]{:S(2)}, u32[]{:S(2)}) async-start(f32[128,4,128]{2,1,0:T(4,128)} %bitcast), calls=%async_computation | async-start | bytes 524288 | tf_op jit(solution)/shard_map/all_to_all | solution.py:908
  54.2 7.6 %copy-start.13 = (f32[7,8,512]{2,1,0:T(8,128)}, f32[7,8,512]{2,1,0:T(8,128)S(1)}, u32[]{:S(2)}) copy-start(f32[7,8,512]{2,1,0:T(8,128)S(1)} %collective-permute-done.8.low_ref.rest_5_) | copy-start | bytes 344068
  54.3 7.6 %copy-start.14 = (f32[7,8,512]{2,1,0:T(8,128)}, f32[7,8,512]{2,1,0:T(8,128)S(1)}, u32[]{:S(2)}) copy-start(f32[7,8,512]{2,1,0:T(8,128)S(1)} %collective-permute-done.9.high_ref.rest_6_) | copy-start | bytes 344068
  54.3 10.9 %collective-permute-start.10 = (f32[14,8,512]{2,1,0:T(8,128)S(1)}, f32[14,8,512]{2,1,0:T(8,128)S(1)}, u32[]{:S(2)}, u32[]{:S(2)}) collective-permute-start(f32[14,8,512]{2,1,0:T(8,128)S(1)} %get-tuple-element.66), channel_id=1, source_target_pairs={{0,1},{1,2},{2,3},{3,4},{4,5},{5,6},{6,7},{7,0},{8,9},{9,10},{10,1... | collective-permute-start | bytes 688136 | tf_op jit(solution)/shard_map/ppermute | solution.py:877
  56.2 9.0 %collective-permute-start.11 = (f32[14,8,512]{2,1,0:T(8,128)S(1)}, f32[14,8,512]{2,1,0:T(8,128)S(1)}, u32[]{:S(2)}, u32[]{:S(2)}) collective-permute-start(f32[14,8,512]{2,1,0:T(8,128)S(1)} %get-tuple-element.67), channel_id=1, source_target_pairs={{1,0},{2,1},{3,2},{4,3},{5,4},{6,5},{7,6},{0,7},{9,8},{10,9},{11,1... | collective-permute-start | bytes 688136 | tf_op jit(solution)/shard_map/ppermute | solution.py:882
  65.2 0.7 copy-start.21
  65.2 0.8 %copy-start.22 = (f32[14,8,512]{2,1,0:T(8,128)}, f32[14,8,512]{2,1,0:T(8,128)S(1)}, u32[]{:S(2)}) copy-start(f32[14,8,512]{2,1,0:T(8,128)S(1)} %collective-permute-done.10.rest_7_) | copy-start | bytes 688132
  65.2 0.9 %copy-start.23 = (f32[14,8,512]{2,1,0:T(8,128)}, f32[14,8,512]{2,1,0:T(8,128)S(1)}, u32[]{:S(2)}) copy-start(f32[14,8,512]{2,1,0:T(8,128)S(1)} %collective-permute-done.11.rest_8_) | copy-start | bytes 688132

commit v6 on v5

--- a/solution.py
+++ b/solution.py
@@ -400,7 +400,7 @@
     def begin(i):
         return [(b, i, q[i] * g[i])]
 
-    loop(1, X0 - 1, begin, 2)
+    loop(1, X0 - 1, begin, 5)
     sweep(b, v, b, wx, wy, wz, q, 2, X0 - 2, 6)
 
     def own_of(i):
@@ -413,7 +413,7 @@
         both = defect(v, g, wx, wy, wz, d, i) + defect(v, g, wx, wy, wz, d, i + 1)
         return [(pairs, (j, k), lanes(both, k)) for k in range(Z0 // LANES)]
 
-    loop(0, 8, restrict, 2)
+    loop(0, 8, restrict, 4)
     rows = jnp.concatenate([halve_rows(pairs, i, 4, 8) for i in range(8)], axis=0)
     g1_ref[...] = (0.5 * pair_sums(rows)).reshape(8, 8, Z1)
 
@@ -502,7 +502,7 @@
         return [(b1_ref, i, q1[i] * g1[i])]
 
     loop(2, X1 - 2, begin1, 10)
-    sweep(b1_ref, v1_ref, b1_ref, wx1, wy1, wz1, q1, 3, X1 - 3, 6)
+    sweep(b1_ref, v1_ref, b1_ref, wx1, wy1, wz1, q1, 3, X1 - 3, 9)
 
     def restrict(j):
         i = 2 * j + 4
@@ -765,7 +765,7 @@
     def begin1(i):
         return [(b1, i, q1[i] * w1[i])]
 
-    loop(5, X1 - 5, begin1, 2)
+    loop(5, X1 - 5, begin1, 7)
 
     slabs = []
     for j in range(6):
@@ -833,8 +833,8 @@
             v0[i, 0:8] = jnp.where(half, below, head) + extra[0:8]
             v0[i, 8:16] = jnp.where(half, head, tail) + extra[8:16]
             v0[i, 16:24] = jnp.where(half, tail, above) + extra[16:24]
-    sweep(v0, w0, b0, wx0, wy0, wz0, q0, 1, X0 - 1, 4)
-    sweep(w0, v0, b0, wx0, wy0, wz0, q0, 2, X0 - 2, 3)
+    sweep(v0, w0, b0, wx0, wy0, wz0, q0, 1, X0 - 1, 5)
+    sweep(w0, v0, b0, wx0, wy0, wz0, q0, 2, X0 - 2, 6)
 
     pick = collect_matrix(Z0)
     rows = jnp.concatenate([pltpu.roll(v0[i + OX0], Y0 - OY0, 0)[0:16] for i in range(16)], axis=0)
@@ -845,7 +845,7 @@
         here, total = neighbours(v0, wx0, wy0, wz0, i + OX0)
         return [(residual_ref, i, pltpu.roll(total - d0[i + OX0] * here, Y0 - OY0, 0)[0:16])]
 
-    loop(0, 16, finish, 4)
+    loop(0, 16, finish, 8)
     for part in range(2):
         here = pl.ds(8 * part, 8)
         rows = residual_ref[here].reshape(128, Z0)

time: 76 us -> 75.9 us (level)
  no operation moved by 1% of the time
where the time goes in v6:
time: 75.9 us; the launch traced here: 75.6 us
  starting transfers between devices  29.8 us (39%)
  Pallas kernels  22.1 us (29%)
  waiting for transfers between devices  19.6 us (26%)
  local copies, waits for them, and re-layouts  3.02 us (4%)
  between operations  1.02 us (1%)
    ppermute x6, starting transfers between devices, to_previous(): lax.ppermute(cells, axis, [((i + 1) % count, i) for i in range(count)])  14 us
    ppermute x6, waiting for transfers between devices, to_next(): lax.ppermute(cells, axis, [(i, (i + 1) % count) for i in range(count)])  11.7 us
    pallas_call x1, Pallas kernels, up(): call(functools.partial(up_kernel, count_x, count_y), [struct(16, 16, Z0),...  9.57 us
    ppermute x6, starting transfers between devices, to_next(): lax.ppermute(cells, axis, [(i, (i + 1) % count) for i in range(count)])  8.25 us
    all_to_all x1, starting transfers between devices, shards(): lax.all_to_all(send3, ('gx', 'gy'), split_axis=0, concat_axis=0, tiled=True)  7.59 us
    pallas_call x1, Pallas kernels, weights0(): call(functools.partial(weights0_kernel, count_x, count_y), [struct(*frame...  5.6 us
    ppermute x6, waiting for transfers between devices, to_previous(): lax.ppermute(cells, axis, [((i + 1) % count, i) for i in range(count)])  4.6 us
    all_to_all x1, waiting for transfers between devices, shards(): lax.all_to_all(send3, ('gx', 'gy'), split_axis=0, concat_axis=0, tiled=True)  3.31 us
  transfers between devices with their start and end apart: 13, of which 6 were waited for; matrix products, arithmetic and copies ran while one was open for 0% of the time, Pallas kernels for 10%

profile of v6, /device:TPU:1, one launch (start us, length us, event | category | flops | bytes accessed | tf_op | source)
XLA Modules:
  0.0 75.6 jit_solution(4216225385064638712)
XLA Ops:
  0.6 0.0 copy-start.2
  0.6 1.0 %copy-done.2 = f32[16,16,512]{2,1,0:T(8,128)S(1)} copy-done((f32[16,16,512]{2,1,0:T(8,128)S(1)}, f32[16,16,512]{2,1,0:T(8,128)}, u32[]{:S(2)}) %copy-start.2) | copy-done | bytes 524312
  1.7 1.0 %copy-done.8 = f32[16,16,512]{2,1,0:T(8,128)S(1)} copy-done((f32[16,16,512]{2,1,0:T(8,128)S(1)}, f32[16,16,512]{2,1,0:T(8,128)}, u32[]{:S(2)}) %copy-start.8) | copy-done | bytes 524312
  2.7 0.2 shard_map.42
  3.0 0.0 copy-start.12
  3.0 2.1 %collective-permute-start = (f32[7,16,512]{2,1,0:T(8,128)S(1)}, f32[7,16,512]{2,1,0:T(8,128)S(1)}, u32[]{:S(2)}, u32[]{:S(2)}) collective-permute-start(f32[7,16,512]{2,1,0:T(8,128)S(1)} %get-tuple-element.43), channel_id=1, source_target_pairs={{0,8},{8,16},{16,24},{24,32},{32,40},{40,48},{48,56},{56,64},{64,7... | collective-permute-start | bytes 688136 | tf_op jit(solution)/shard_map/ppermute | solution.py:877
  5.1 3.8 %collective-permute-start.1 = (f32[7,16,512]{2,1,0:T(8,128)S(1)}, f32[7,16,512]{2,1,0:T(8,128)S(1)}, u32[]{:S(2)}, u32[]{:S(2)}) collective-permute-start(f32[7,16,512]{2,1,0:T(8,128)S(1)} %get-tuple-element.44), channel_id=1, source_target_pairs={{8,0},{16,8},{24,16},{32,24},{40,32},{48,40},{56,48},{64,56},{72,6... | collective-permute-start | bytes 688136 | tf_op jit(solution)/shard_map/ppermute | solution.py:882
  8.9 1.0 %shard_map.41 = (f32[16,16,512]{2,1,0:T(8,128)S(1)}, f32[16,16,512]{2,1,0:T(8,128)S(1)}, bf16[512,512]{1,0:T(8,128)(2,1)S(1)}) custom-call(f32[16,16,512]{2,1,0:T(8,128)S(1)} %copy-done.8, f32[16,16,512]{2,1,0:T(8,128)S(1)} %copy-done.2), custom_call_target="tpu_custom_call" | custom-call | flops 1000000 | bytes 1000000 | tf_op jit(solution)/shard_map/pallas_call | solution.py:293
  9.9 0.0 copy-start.3
  9.9 0.0 copy-start.4
  10.0 4.1 %collective-permute-done.low_raw = f32[7,16,512]{2,1,0:T(8,128)S(1)} collective-permute-done((f32[7,16,512]{2,1,0:T(8,128)S(1)}, f32[7,16,512]{2,1,0:T(8,128)S(1)}, u32[]{:S(2)}, u32[]{:S(2)}) %collective-permute-start) | collective-permute-done | bytes 229408 | tf_op jit(solution)/shard_map/ppermute | solution.py:877
  14.1 0.0 collective-permute-done.1.high_raw
  14.1 0.4 shard_map.43
  14.5 2.8 %collective-permute-start.2 = (f32[28,8,512]{2,1,0:T(8,128)S(1)}, f32[28,8,512]{2,1,0:T(8,128)S(1)}, u32[]{:S(2)}, u32[]{:S(2)}) collective-permute-start(f32[28,8,512]{2,1,0:T(8,128)S(1)} %get-tuple-element.47), channel_id=1, source_target_pairs={{0,1},{1,2},{2,3},{3,4},{4,5},{5,6},{6,7},{7,0},{8,9},{9,10},{10,1... | collective-permute-start | bytes 1376264 | tf_op jit(solution)/shard_map/ppermute | solution.py:877
  17.3 0.0 collective-permute-start.3
  17.4 5.4 %collective-permute-done.2.below_ref.below0.rest_15_ = f32[28,8,512]{2,1,0:T(8,128)S(1)} collective-permute-done((f32[28,8,512]{2,1,0:T(8,128)S(1)}, f32[28,8,512]{2,1,0:T(8,128)S(1)}, u32[]{:S(2)}, u32[]{:S(2)}) %collective-permute-start.2) | collective-permute-done | bytes 458784 | tf_op jit(solution)/shard_map/ppermute | solution.py:877
  22.8 2.5 %collective-permute-done.3.above_ref.above0.rest_16_ = f32[28,8,512]{2,1,0:T(8,128)S(1)} collective-permute-done((f32[28,8,512]{2,1,0:T(8,128)S(1)}, f32[28,8,512]{2,1,0:T(8,128)S(1)}, u32[]{:S(2)}, u32[]{:S(2)}) %collective-permute-start.3) | collective-permute-done | bytes 458784 | tf_op jit(solution)/shard_map/ppermute | solution.py:882
  25.3 2.6 %shard_map.44 = (f32[8,8,256]{2,1,0:T(8,128)S(1)}, f32[16,16,512]{2,1,0:T(8,128)S(1)}) custom-call(f32[16,16,512]{2,1,0:T(8,128)S(1)} %get-tuple-element.69.c_ref, f32[16,16,512]{2,1,0:T(8,128)S(1)} %get-tuple-element.40.g_ref, f32[7,16,512]{2,1,0:T(8,128)S(1)} %get-tuple-element.45.low_ref.low0.rest_13_, ...), custom_call_target="tpu_custom_call" | custom-call | flops 1000000 | bytes 1000000 | tf_op jit(solution)/shard_map/pallas_call | solution.py:423
  27.8 0.0 copy-done.3
  27.8 0.0 copy-done.4
  27.9 0.0 copy-start.5
  27.9 0.1 collective-permute-start.4
  28.0 4.9 %collective-permute-start.5 = (f32[6,8,256]{2,1,0:T(8,128)S(1)}, f32[6,8,256]{2,1,0:T(8,128)S(1)}, u32[]{:S(2)}, u32[]{:S(2)}) collective-permute-start(f32[6,8,256]{2,1,0:T(8,128)S(1)} %get-tuple-element.77), channel_id=1, source_target_pairs={{8,0},{16,8},{24,16},{32,24},{40,32},{48,40},{56,48},{64,56},{72,6... | collective-permute-start | bytes 147464 | tf_op jit(solution)/shard_map/ppermute | solution.py:882
  32.9 2.1 %collective-permute-done.4 = f32[6,8,256]{2,1,0:T(8,128)S(1)} collective-permute-done((f32[6,8,256]{2,1,0:T(8,128)S(1)}, f32[6,8,256]{2,1,0:T(8,128)S(1)}, u32[]{:S(2)}, u32[]{:S(2)}) %collective-permute-start.4) | collective-permute-done | bytes 49184 | tf_op jit(solution)/shard_map/ppermute | solution.py:877
  35.0 0.0 collective-permute-done.5
  35.1 0.0 copy-start.9
  35.1 0.5 collective-permute-start.7
  35.6 1.3 %collective-permute-start.6 = (f32[20,8,256]{2,1,0:T(8,128)S(1)}, f32[20,8,256]{2,1,0:T(8,128)S(1)}, u32[]{:S(2)}, u32[]{:S(2)}) collective-permute-start(f32[20,8,256]{2,1,0:T(8,128)S(1)} %pad_maximum_fusion.mid_ref.rest_9_), channel_id=1, source_target_pairs={{0,1},{1,2},{2,3},{3,4},{4,5},{5,6},{6,7},{7,0},{8,9},{9,10},{10,1... | collective-permute-start | bytes 491528 | tf_op jit(solution)/shard_map/ppermute | solution.py:877
  36.9 0.8 %shard_map.45 = (f32[24,24,256]{2,1,0:T(8,128)S(1)}, f32[24,24,256]{2,1,0:T(8,128)S(1)}, f32[24,24,256]{2,1,0:T(8,128)S(1)}, f32[24,24,256]{2,1,0:T(8,128)S(1)},...) custom-call(f32[8,8,256]{2,1,0:T(8,128)S(1)} %get-tuple-element.42.c, ...), custom_call_target="tpu_custom_call" | custom-call | flops 1000000 | bytes 1000000 | tf_op jit(solution)/shard_map/pallas_call | solution.py:477
  37.7 2.1 %collective-permute-done.7.above_ref.rest_11_ = f32[20,8,256]{2,1,0:T(8,128)S(1)} collective-permute-done((f32[20,8,256]{2,1,0:T(8,128)S(1)}, f32[20,8,256]{2,1,0:T(8,128)S(1)}, u32[]{:S(2)}, u32[]{:S(2)}) %collective-permute-start.7) | collective-permute-done | bytes 163872 | tf_op jit(solution)/shard_map/ppermute | solution.py:882
  39.9 0.0 collective-permute-done.6.below_ref.rest_10_
  39.9 1.8 %shard_map.46 = (f32[16,24,256]{2,1,0:T(8,128)S(1)}, f32[8,512]{1,0:T(8,128)S(1)}, f32[512,128]{1,0:T(8,128)}) custom-call(f32[20,8,256]{2,1,0:T(8,128)S(1)} %pad_maximum_fusion.mid_ref.rest_9_, f32[20,8,256]{2,1,0:T(8,128)S(1)} %collective-permute-done.6.below_ref.rest_10_, f32[20,8,256]{2,1,0:T(8,128)S(1)} %collective-permute-done.7.above_ref.rest_11_, ...), custom_call_target="tpu_custom_call" | custom-call | flops 1000000 | bytes 1000000 | tf_op jit(solution)/shard_map/pallas_call | solution.py:547
  41.6 0.0 copy-done.17
  41.7 0.1 collective-permute-start.8
  41.8 4.8 %collective-permute-start.9 = (f32[7,8,512]{2,1,0:T(8,128)S(1)}, f32[7,8,512]{2,1,0:T(8,128)S(1)}, u32[]{:S(2)}, u32[]{:S(2)}) collective-permute-start(f32[7,8,512]{2,1,0:T(8,128)S(1)} %get-tuple-element.65), channel_id=1, source_target_pairs={{8,0},{16,8},{24,16},{32,24},{40,32},{48,40},{56,48},{64,56},{72,6... | collective-permute-start | bytes 344072 | tf_op jit(solution)/shard_map/ppermute | solution.py:882
  46.6 7.6 %all-to-all-start = ((f32[128,4,128]{2,1,0:T(4,128)}), f32[128,4,128]{2,1,0:T(4,128)S(1)}, u32[]{:S(2)}, u32[]{:S(2)}) async-start(f32[128,4,128]{2,1,0:T(4,128)} %bitcast), calls=%async_computation | async-start | bytes 524288 | tf_op jit(solution)/shard_map/all_to_all | solution.py:908
  54.1 0.0 collective-permute-done.8.low_ref.rest_5_
  54.2 0.0 collective-permute-done.9.high_ref.rest_6_
  54.3 1.9 %collective-permute-start.10 = (f32[14,8,512]{2,1,0:T(8,128)S(1)}, f32[14,8,512]{2,1,0:T(8,128)S(1)}, u32[]{:S(2)}, u32[]{:S(2)}) collective-permute-start(f32[14,8,512]{2,1,0:T(8,128)S(1)} %get-tuple-element.66), channel_id=1, source_target_pairs={{0,1},{1,2},{2,3},{3,4},{4,5},{5,6},{6,7},{7,0},{8,9},{9,10},{10,1... | collective-permute-start | bytes 688136 | tf_op jit(solution)/shard_map/ppermute | solution.py:877
  56.2 0.0 collective-permute-start.11
  56.2 5.6 %shard_map.49 = (f32[22,24,512]{2,1,0:T(8,128)}, f32[22,24,512]{2,1,0:T(8,128)}, f32[22,24,512]{2,1,0:T(8,128)}, f32[22,24,512]{2,1,0:T(8,128)}, f32[22,24,512]{2,1,0:T(8,128)}, /*index=5*/f32[22,24,512]{2,1,0:T(8,128)}) custom-call(f32[16,16,512]{2,1,0:T(8,128)} %copy-done.3, f32[16,16,512]{2,1,0:T(8,128)} %copy-done.4, f32[7,16,512]{2,1,0:T(8,128)} %copy-done.6, ...), custom_call_target="tpu_custom_call" | custom-call | flops 20000000 | bytes 20000000 | tf_op jit(solution)/shard_map/pallas_call | solution.py:620
  61.8 3.3 %all-to-all-done = f32[128,4,128]{2,1,0:T(4,128)S(1)} async-done(((f32[128,4,128]{2,1,0:T(4,128)}), f32[128,4,128]{2,1,0:T(4,128)S(1)}, u32[]{:S(2)}, u32[]{:S(2)}) %all-to-all-start) | async-done | bytes 262176 | tf_op jit(solution)/shard_map/all_to_all | solution.py:908
  65.1 0.0 collective-permute-done.10.rest_7_
  65.1 0.0 collective-permute-done.11.rest_8_
  65.2 0.7 copy-done.21
  65.8 0.1 copy-done.22
  65.9 0.1 copy-done.23
  66.0 9.6 %shard_map.50 = (f32[16,16,512]{2,1,0:T(8,128)}, f32[16,16,512]{2,1,0:T(8,128)}) custom-call(f32[512,128]{1,0:T(8,128)} %bitcast.2, f32[12,16,128]{2,1,0:T(8,128)} %copy-done.16, f32[12,16,128]{2,1,0:T(8,128)} %copy-done.17, f32[12,16,128]{2,1,0:T(8,128)} %copy-done.18, f32[12,16,128]{2,1,0:T(8,128)} %copy-done.19, f32[8,512]{1,0:T(8,128)} %copy-done.20, ...), custom_call_target="tpu_custom_call" | custom-call | flops 1000000 | bytes 1000000 | tf_op jit(solution)/shard_map/pallas_call | solution.py:860
  (40 shorter events, 0.2 us)
Async XLA Ops:
  0.6 1.0 %copy-start.2 = (f32[16,16,512]{2,1,0:T(8,128)S(1)}, f32[16,16,512]{2,1,0:T(8,128)}, u32[]{:S(2)}) copy-start(f32[16,16,512]{2,1,0:T(8,128)} %rest_25_.1) | copy-start | bytes 1572868
  1.7 1.0 %copy-start.8 = (f32[16,16,512]{2,1,0:T(8,128)S(1)}, f32[16,16,512]{2,1,0:T(8,128)}, u32[]{:S(2)}) copy-start(f32[16,16,512]{2,1,0:T(8,128)} %c_ref.3) | copy-start | bytes 1572868
  3.0 33.9 %copy-start.12 = (f32[8,8,256]{2,1,0:T(8,128)}, f32[8,8,256]{2,1,0:T(8,128)S(1)}, u32[]{:S(2)}) copy-start(f32[8,8,256]{2,1,0:T(8,128)S(1)} %get-tuple-element.42.c1_ref.rest_12_) | copy-start | bytes 196612
  3.0 11.1 %collective-permute-start = (f32[7,16,512]{2,1,0:T(8,128)S(1)}, f32[7,16,512]{2,1,0:T(8,128)S(1)}, u32[]{:S(2)}, u32[]{:S(2)}) collective-permute-start(f32[7,16,512]{2,1,0:T(8,128)S(1)} %get-tuple-element.43), channel_id=1, source_target_pairs={{0,8},{8,16},{16,24},{24,32},{32,40},{40,48},{48,56},{56,64},{64,7... | collective-permute-start | bytes 688136 | tf_op jit(solution)/shard_map/ppermute | solution.py:877
  5.1 9.0 %collective-permute-start.1 = (f32[7,16,512]{2,1,0:T(8,128)S(1)}, f32[7,16,512]{2,1,0:T(8,128)S(1)}, u32[]{:S(2)}, u32[]{:S(2)}) collective-permute-start(f32[7,16,512]{2,1,0:T(8,128)S(1)} %get-tuple-element.44), channel_id=1, source_target_pairs={{8,0},{16,8},{24,16},{32,24},{40,32},{48,40},{56,48},{64,56},{72,6... | collective-permute-start | bytes 688136 | tf_op jit(solution)/shard_map/ppermute | solution.py:882
  9.9 17.9 %copy-start.3 = (f32[16,16,512]{2,1,0:T(8,128)}, f32[16,16,512]{2,1,0:T(8,128)S(1)}, u32[]{:S(2)}) copy-start(f32[16,16,512]{2,1,0:T(8,128)S(1)} %get-tuple-element.69.c_ref) | copy-start | bytes 1572868
  9.9 17.9 %copy-start.4 = (f32[16,16,512]{2,1,0:T(8,128)}, f32[16,16,512]{2,1,0:T(8,128)S(1)}, u32[]{:S(2)}) copy-start(f32[16,16,512]{2,1,0:T(8,128)S(1)} %get-tuple-element.40.g_ref) | copy-start | bytes 1572868
  14.5 22.3 %copy-start.6 = (f32[7,16,512]{2,1,0:T(8,128)}, f32[7,16,512]{2,1,0:T(8,128)S(1)}, u32[]{:S(2)}) copy-start(f32[7,16,512]{2,1,0:T(8,128)S(1)} %get-tuple-element.45.low_ref.low0.rest_13_) | copy-start | bytes 688132
  14.5 22.3 %copy-start.7 = (f32[7,16,512]{2,1,0:T(8,128)}, f32[7,16,512]{2,1,0:T(8,128)S(1)}, u32[]{:S(2)}) copy-start(f32[7,16,512]{2,1,0:T(8,128)S(1)} %get-tuple-element.46.high_ref.high0.rest_14_) | copy-start | bytes 688132
  14.5 8.2 %collective-permute-start.2 = (f32[28,8,512]{2,1,0:T(8,128)S(1)}, f32[28,8,512]{2,1,0:T(8,128)S(1)}, u32[]{:S(2)}, u32[]{:S(2)}) collective-permute-start(f32[28,8,512]{2,1,0:T(8,128)S(1)} %get-tuple-element.47), channel_id=1, source_target_pairs={{0,1},{1,2},{2,3},{3,4},{4,5},{5,6},{6,7},{7,0},{8,9},{9,10},{10,1... | collective-permute-start | bytes 1376264 | tf_op jit(solution)/shard_map/ppermute | solution.py:877
  17.3 7.9 %collective-permute-start.3 = (f32[28,8,512]{2,1,0:T(8,128)S(1)}, f32[28,8,512]{2,1,0:T(8,128)S(1)}, u32[]{:S(2)}, u32[]{:S(2)}) collective-permute-start(f32[28,8,512]{2,1,0:T(8,128)S(1)} %get-tuple-element.48), channel_id=1, source_target_pairs={{1,0},{2,1},{3,2},{4,3},{5,4},{6,5},{7,6},{0,7},{9,8},{10,9},{11,1... | collective-permute-start | bytes 1376264 | tf_op jit(solution)/shard_map/ppermute | solution.py:882
  22.8 14.1 %copy-start = (f32[28,8,512]{2,1,0:T(8,128)}, f32[28,8,512]{2,1,0:T(8,128)S(1)}, u32[]{:S(2)}) copy-start(f32[28,8,512]{2,1,0:T(8,128)S(1)} %collective-permute-done.2.below_ref.below0.rest_15_) | copy-start | bytes 1376260
  25.3 11.6 %copy-start.1 = (f32[28,8,512]{2,1,0:T(8,128)}, f32[28,8,512]{2,1,0:T(8,128)S(1)}, u32[]{:S(2)}) copy-start(f32[28,8,512]{2,1,0:T(8,128)S(1)} %collective-permute-done.3.above_ref.above0.rest_16_) | copy-start | bytes 1376260
  27.9 26.3 %copy-start.5 = (f32[16,16,512]{2,1,0:T(8,128)}, f32[16,16,512]{2,1,0:T(8,128)S(1)}, u32[]{:S(2)}) copy-start(f32[16,16,512]{2,1,0:T(8,128)S(1)} %get-tuple-element.63.own_ref.rest_18_) | copy-start | bytes 1572868
  27.9 7.1 %collective-permute-start.4 = (f32[6,8,256]{2,1,0:T(8,128)S(1)}, f32[6,8,256]{2,1,0:T(8,128)S(1)}, u32[]{:S(2)}, u32[]{:S(2)}) collective-permute-start(f32[6,8,256]{2,1,0:T(8,128)S(1)} %get-tuple-element.76), channel_id=1, source_target_pairs={{0,8},{8,16},{16,24},{24,32},{32,40},{40,48},{48,56},{56,64},{64,7... | collective-permute-start | bytes 147464 | tf_op jit(solution)/shard_map/ppermute | solution.py:877
  28.0 7.1 %collective-permute-start.5 = (f32[6,8,256]{2,1,0:T(8,128)S(1)}, f32[6,8,256]{2,1,0:T(8,128)S(1)}, u32[]{:S(2)}, u32[]{:S(2)}) collective-permute-start(f32[6,8,256]{2,1,0:T(8,128)S(1)} %get-tuple-element.77), channel_id=1, source_target_pairs={{8,0},{16,8},{24,16},{32,24},{40,32},{48,40},{56,48},{64,56},{72,6... | collective-permute-start | bytes 147464 | tf_op jit(solution)/shard_map/ppermute | solution.py:882
  35.1 6.5 %copy-start.9 = (f32[20,8,256]{2,1,0:T(8,128)}, f32[20,8,256]{2,1,0:T(8,128)S(1)}, u32[]{:S(2)}) copy-start(f32[20,8,256]{2,1,0:T(8,128)S(1)} %pad_maximum_fusion.mid_ref.rest_9_) | copy-start | bytes 491524
  35.1 4.8 %collective-permute-start.7 = (f32[20,8,256]{2,1,0:T(8,128)S(1)}, f32[20,8,256]{2,1,0:T(8,128)S(1)}, u32[]{:S(2)}, u32[]{:S(2)}) collective-permute-start(f32[20,8,256]{2,1,0:T(8,128)S(1)} %pad_maximum_fusion.mid_ref.rest_9_), channel_id=1, source_target_pairs={{1,0},{2,1},{3,2},{4,3},{5,4},{6,5},{7,6},{0,7},{9,8},{10,9},{11,1... | collective-permute-start | bytes 491528 | tf_op jit(solution)/shard_map/ppermute | solution.py:882
  35.6 4.3 %collective-permute-start.6 = (f32[20,8,256]{2,1,0:T(8,128)S(1)}, f32[20,8,256]{2,1,0:T(8,128)S(1)}, u32[]{:S(2)}, u32[]{:S(2)}) collective-permute-start(f32[20,8,256]{2,1,0:T(8,128)S(1)} %pad_maximum_fusion.mid_ref.rest_9_), channel_id=1, source_target_pairs={{0,1},{1,2},{2,3},{3,4},{4,5},{5,6},{6,7},{7,0},{8,9},{9,10},{10,1... | collective-permute-start | bytes 491528 | tf_op jit(solution)/shard_map/ppermute | solution.py:877
  37.7 3.9 %copy-start.16 = (f32[12,16,128]{2,1,0:T(8,128)}, f32[12,16,128]{2,1,0:T(8,128)S(1)}, u32[]{:S(2)}) copy-start(f32[12,16,128]{2,1,0:T(8,128)S(1)} %get-tuple-element.55.wx2.rest_0_) | copy-start | bytes 294916
  37.7 3.9 %copy-start.17 = (f32[12,16,128]{2,1,0:T(8,128)}, f32[12,16,128]{2,1,0:T(8,128)S(1)}, u32[]{:S(2)}) copy-start(f32[12,16,128]{2,1,0:T(8,128)S(1)} %get-tuple-element.56.wy2.rest_1_) | copy-start | bytes 294916
  37.7 3.9 %copy-start.18 = (f32[12,16,128]{2,1,0:T(8,128)}, f32[12,16,128]{2,1,0:T(8,128)S(1)}, u32[]{:S(2)}) copy-start(f32[12,16,128]{2,1,0:T(8,128)S(1)} %get-tuple-element.57.wz2.rest_2_) | copy-start | bytes 294916
  37.7 3.9 %copy-start.19 = (f32[12,16,128]{2,1,0:T(8,128)}, f32[12,16,128]{2,1,0:T(8,128)S(1)}, u32[]{:S(2)}) copy-start(f32[12,16,128]{2,1,0:T(8,128)S(1)} %get-tuple-element.59.q2.rest_3_) | copy-start | bytes 294916
  39.9 1.8 %copy-start.10 = (f32[20,8,256]{2,1,0:T(8,128)}, f32[20,8,256]{2,1,0:T(8,128)S(1)}, u32[]{:S(2)}) copy-start(f32[20,8,256]{2,1,0:T(8,128)S(1)} %collective-permute-done.7.above_ref.rest_11_) | copy-start | bytes 491524
  39.9 1.8 %copy-start.11 = (f32[20,8,256]{2,1,0:T(8,128)}, f32[20,8,256]{2,1,0:T(8,128)S(1)}, u32[]{:S(2)}) copy-start(f32[20,8,256]{2,1,0:T(8,128)S(1)} %collective-permute-done.6.below_ref.rest_10_) | copy-start | bytes 491524
  41.7 20.1 %copy-start.15 = (f32[16,24,256]{2,1,0:T(8,128)}, f32[16,24,256]{2,1,0:T(8,128)S(1)}, u32[]{:S(2)}) copy-start(f32[16,24,256]{2,1,0:T(8,128)S(1)} %get-tuple-element.68.rest_17_) | copy-start | bytes 1179652
  41.7 20.1 %copy-start.20 = (f32[8,512]{1,0:T(8,128)}, f32[8,512]{1,0:T(8,128)S(1)}, u32[]{:S(2)}) copy-start(f32[8,512]{1,0:T(8,128)S(1)} %get-tuple-element.62.own2_ref.rest_4_) | copy-start | bytes 49156
  41.7 12.5 %collective-permute-start.8 = (f32[7,8,512]{2,1,0:T(8,128)S(1)}, f32[7,8,512]{2,1,0:T(8,128)S(1)}, u32[]{:S(2)}, u32[]{:S(2)}) collective-permute-start(f32[7,8,512]{2,1,0:T(8,128)S(1)} %get-tuple-element.64), channel_id=1, source_target_pairs={{0,8},{8,16},{16,24},{24,32},{32,40},{40,48},{48,56},{56,64},{64,7... | collective-permute-start | bytes 344072 | tf_op jit(solution)/shard_map/ppermute | solution.py:877
  41.8 12.4 %collective-permute-start.9 = (f32[7,8,512]{2,1,0:T(8,128)S(1)}, f32[7,8,512]{2,1,0:T(8,128)S(1)}, u32[]{:S(2)}, u32[]{:S(2)}) collective-permute-start(f32[7,8,512]{2,1,0:T(8,128)S(1)} %get-tuple-element.65), channel_id=1, source_target_pairs={{8,0},{16,8},{24,16},{32,24},{40,32},{48,40},{56,48},{64,56},{72,6... | collective-permute-start | bytes 344072 | tf_op jit(solution)/shard_map/ppermute | solution.py:882
  46.6 18.6 %all-to-all-start = ((f32[128,4,128]{2,1,0:T(4,128)}), f32[128,4,128]{2,1,0:T(4,128)S(1)}, u32[]{:S(2)}, u32[]{:S(2)}) async-start(f32[128,4,128]{2,1,0:T(4,128)} %bitcast), calls=%async_computation | async-start | bytes 524288 | tf_op jit(solution)/shard_map/all_to_all | solution.py:908
  54.2 7.6 %copy-start.13 = (f32[7,8,512]{2,1,0:T(8,128)}, f32[7,8,512]{2,1,0:T(8,128)S(1)}, u32[]{:S(2)}) copy-start(f32[7,8,512]{2,1,0:T(8,128)S(1)} %collective-permute-done.8.low_ref.rest_5_) | copy-start | bytes 344068
  54.2 7.6 %copy-start.14 = (f32[7,8,512]{2,1,0:T(8,128)}, f32[7,8,512]{2,1,0:T(8,128)S(1)}, u32[]{:S(2)}) copy-start(f32[7,8,512]{2,1,0:T(8,128)S(1)} %collective-permute-done.9.high_ref.rest_6_) | copy-start | bytes 344068
  54.3 10.9 %collective-permute-start.10 = (f32[14,8,512]{2,1,0:T(8,128)S(1)}, f32[14,8,512]{2,1,0:T(8,128)S(1)}, u32[]{:S(2)}, u32[]{:S(2)}) collective-permute-start(f32[14,8,512]{2,1,0:T(8,128)S(1)} %get-tuple-element.66), channel_id=1, source_target_pairs={{0,1},{1,2},{2,3},{3,4},{4,5},{5,6},{6,7},{7,0},{8,9},{9,10},{10,1... | collective-permute-start | bytes 688136 | tf_op jit(solution)/shard_map/ppermute | solution.py:877
  56.2 9.0 %collective-permute-start.11 = (f32[14,8,512]{2,1,0:T(8,128)S(1)}, f32[14,8,512]{2,1,0:T(8,128)S(1)}, u32[]{:S(2)}, u32[]{:S(2)}) collective-permute-start(f32[14,8,512]{2,1,0:T(8,128)S(1)} %get-tuple-element.67), channel_id=1, source_target_pairs={{1,0},{2,1},{3,2},{4,3},{5,4},{6,5},{7,6},{0,7},{9,8},{10,9},{11,1... | collective-permute-start | bytes 688136 | tf_op jit(solution)/shard_map/ppermute | solution.py:882
  65.1 0.7 copy-start.21
  65.1 0.8 %copy-start.22 = (f32[14,8,512]{2,1,0:T(8,128)}, f32[14,8,512]{2,1,0:T(8,128)S(1)}, u32[]{:S(2)}) copy-start(f32[14,8,512]{2,1,0:T(8,128)S(1)} %collective-permute-done.10.rest_7_) | copy-start | bytes 688132
  65.1 0.9 %copy-start.23 = (f32[14,8,512]{2,1,0:T(8,128)}, f32[14,8,512]{2,1,0:T(8,128)S(1)}, u32[]{:S(2)}) copy-start(f32[14,8,512]{2,1,0:T(8,128)S(1)} %collective-permute-done.11.rest_8_) | copy-start | bytes 688132
